TPU v7x, 32 devices: a whole 2x2x4 slice. The times are simulated.
32 devices in a mesh: head: 4 (over x, core), wide: 8 (over z, y).
Axes of the slice: x: 2, y: 2, z: 4, core: 2. Of those that a mesh axis runs over, the one named last changes fastest.
Arguments:
- tokens: bfloat16 [8192, 2048], P(('wide', 'head')), may hold values from -6 to 6
- cotangent: bfloat16 [8192, 2048], P(('wide', 'head')), may hold values from -6 to 6
- segment_ids: int32 [8192], P('wide'), may hold values from 0 to 31, as said below
- domain_ids: int32 [8192], P(('wide', 'head')), may hold values from 0 to 7, as said below
- domain_weights: float32 [8], replicated, may hold values from 0.5 to 2
- gains: float32 [4352], replicated, may hold values from 0.5 to 1.7
- gain_first: float32 [4352], replicated, may hold values from -0.00036621094 to 0.00036621094
- gain_second: float32 [4352], replicated, may hold values from 8.339221e-09 to 1.3303043e-07
- query_weight: float32 [2048, 2048], P('wide', 'head'), may hold values from -0.125 to 0.125
- query_first: float32 [2048, 2048], P('wide', 'head'), may hold values from -9.1552734e-05 to 9.1552734e-05
- query_second: float32 [2048, 2048], P('wide', 'head'), may hold values from 5.2219407e-10 to 8.339221e-09
- keyvalue_weight: float32 [2, 2048, 1024], P(None, 'wide', 'head'), may hold values from -0.125 to 0.125
- keyvalue_first: float32 [2, 2048, 1024], P(None, 'wide', 'head'), may hold values from -9.1552734e-05 to 9.1552734e-05
- keyvalue_second: float32 [2, 2048, 1024], P(None, 'wide', 'head'), may hold values from 5.2219407e-10 to 8.339221e-09
- headgate_weight: float32 [2048, 16], P('wide', 'head'), may hold values from -0.125 to 0.125
- headgate_first: float32 [2048, 16], P('wide', 'head'), may hold values from -9.1552734e-05 to 9.1552734e-05
- headgate_second: float32 [2048, 16], P('wide', 'head'), may hold values from 5.2219407e-10 to 8.339221e-09
- output_weight: float32 [2048, 2048], P('head', 'wide'), may hold values from -1 to 1
- output_first: float32 [2048, 2048], P('head', 'wide'), may hold values from -7.6293945e-06 to 7.6293945e-06
- output_second: float32 [2048, 2048], P('head', 'wide'), may hold values from 8.1490726e-12 to 3.259629e-11
- expand_weight: float32 [2, 2048, 6144], P(None, 'head', 'wide'), may hold values from -0.125 to 0.125
- expand_first: float32 [2, 2048, 6144], P(None, 'head', 'wide'), may hold values from -9.1552734e-05 to 9.1552734e-05
- expand_second: float32 [2, 2048, 6144], P(None, 'head', 'wide'), may hold values from 5.2219407e-10 to 8.339221e-09
- reduce_weight: float32 [6144, 2048], P('wide', 'head'), may hold values from -0.078125 to 0.078125
- reduce_first: float32 [6144, 2048], P('wide', 'head'), may hold values from -9.1552734e-05 to 9.1552734e-05
- reduce_second: float32 [6144, 2048], P('wide', 'head'), may hold values from 5.2219407e-10 to 8.339221e-09
Outputs:
- grad_norm: float32 [], replicated
- block_output: bfloat16 [8192, 2048], P(('wide', 'head'))
- input_grad: float32 [8192, 2048], P(('wide', 'head'))
- updated_gains: float32 [4352], replicated
- first_gains: float32 [4352], replicated
- second_gains: float32 [4352], replicated
- updated_query: float32 [2048, 2048], P('wide', 'head')
- first_query: float32 [2048, 2048], P('wide', 'head')
- second_query: float32 [2048, 2048], P('wide', 'head')
- copied_query: bfloat16 [2048, 2048], P('wide', 'head')
- updated_keyvalue: float32 [2, 2048, 1024], P(None, 'wide', 'head')
- first_keyvalue: float32 [2, 2048, 1024], P(None, 'wide', 'head')
- second_keyvalue: float32 [2, 2048, 1024], P(None, 'wide', 'head')
- copied_keyvalue: bfloat16 [2, 2048, 1024], P(None, 'wide', 'head')
- updated_headgate: float32 [2048, 16], P('wide', 'head')
- first_headgate: float32 [2048, 16], P('wide', 'head')
- second_headgate: float32 [2048, 16], P('wide', 'head')
- copied_headgate: bfloat16 [2048, 16], P('wide', 'head')
- updated_output: float32 [2048, 2048], P('head', 'wide')
- first_output: float32 [2048, 2048], P('head', 'wide')
- second_output: float32 [2048, 2048], P('head', 'wide')
- copied_output: bfloat16 [2048, 2048], P('head', 'wide')
- updated_expand: float32 [2, 2048, 6144], P(None, 'head', 'wide')
- first_expand: float32 [2, 2048, 6144], P(None, 'head', 'wide')
- second_expand: float32 [2, 2048, 6144], P(None, 'head', 'wide')
- copied_expand: bfloat16 [2, 2048, 6144], P(None, 'head', 'wide')
- updated_reduce: float32 [6144, 2048], P('wide', 'head')
- first_reduce: float32 [6144, 2048], P('wide', 'head')
- second_reduce: float32 [6144, 2048], P('wide', 'head')
- copied_reduce: bfloat16 [6144, 2048], P('wide', 'head')
Inputs may be any that keep to these rules, and one draw needn't show every extreme that they name: `segment_ids`: segment ids never fall along the tokens, and no segment crosses the border between two packed rows of 1024 tokens. `domain_ids`: all tokens of one segment have the same domain.
All inputs are finite; a program needn't handle non-finite values.
Results may differ from a plain program's by a relative error of at most 0.022.
Values may be sent and summed in bfloat16 or wider, within the bound.
No kernel may reach another device: no remote copies, remote signals or barrier semaphores. Data moves between devices by JAX's collectives and lax.ppermute only.
A program may use at most 320 MiB of HBM per device.

v0:
```python
import jax
import jax.numpy as jnp
from jax import lax
from jax.sharding import PartitionSpec as P

D = 2048
H = 16
HD = 128
KVH = 8
NDOM = 8
STEP = 10


NORM_EPS = 1e-06
ROPE_BASE = 1000000.0
MASK_FILL = -1e30
CLIP_NORM = 1.0
WEIGHT_RATE = 0.02
OUTPUT_RATE = 0.12
GAIN_RATE = 0.7
BETA_FIRST = 0.9
BETA_SECOND = 0.95
ADAM_EPS = 1e-08
WEIGHT_DECAY = 0.1


def rms_scale(values):
    return values * lax.rsqrt(jnp.mean(values * values, -1, keepdims=True) + NORM_EPS)


def norm_rows(values, gain):
    return rms_scale(values) * gain


def positions(segments):
    length = segments.shape[0]
    places = jnp.arange(length, dtype=jnp.int32)
    starts = jnp.concatenate([jnp.ones((1,), dtype=bool), segments[1:] != segments[:-1]])
    return places - lax.cummax(jnp.where(starts, places, 0), axis=0)


def rotate(values, places):
    half = values.shape[-1] // 2
    freqs = ROPE_BASE ** (-2.0 * jnp.arange(half, dtype=jnp.float32) / values.shape[-1])
    angles = places.astype(jnp.float32)[:, None] * freqs[None, :]
    cosine = jnp.cos(angles)[:, None, :]
    sine = jnp.sin(angles)[:, None, :]
    first_half = values[..., :half]
    second_half = values[..., half:]
    return jnp.concatenate(
        [first_half * cosine - second_half * sine, second_half * cosine + first_half * sine], -1
    )


def head_prep(raw, gain, places):
    shaped = raw.reshape(raw.shape[0], -1, gain.shape[0])
    return rotate(rms_scale(shaped) * gain, places)


def contract_rows(left, right):
    return lax.dot_general(
        left, right, (((0,), (0,)), ((), ())), preferred_element_type=jnp.float32
    )


def contract_cols(left, right):
    return lax.dot_general(
        left, right, (((1,), (1,)), ((), ())), preferred_element_type=jnp.float32
    )


def swiglu_back(activation_grad, gate_pre, up_pre):
    gate_sigmoid = jax.nn.sigmoid(gate_pre)
    gate_grad = (
        activation_grad * up_pre * gate_sigmoid * (1.0 + gate_pre * (1.0 - gate_sigmoid))
    ).astype(jnp.bfloat16)
    up_grad = (activation_grad * gate_pre * gate_sigmoid).astype(jnp.bfloat16)
    return (gate_grad, up_grad)


def adam_step(weight, grad, first, second, rate, decay):
    first_new = BETA_FIRST * first + (1.0 - BETA_FIRST) * grad
    second_new = BETA_SECOND * second + (1.0 - BETA_SECOND) * grad * grad
    first_hat = first_new / (1.0 - BETA_FIRST**STEP)
    second_hat = second_new / (1.0 - BETA_SECOND**STEP)
    updated = weight - rate * (first_hat / (jnp.sqrt(second_hat) + ADAM_EPS) + decay * weight)
    return (updated, first_new, second_new)


def body(
    tokens,
    cotangent,
    segment_ids,
    domain_ids,
    domain_weights,
    gains,
    gain_first,
    gain_second,
    query_weight,
    query_first,
    query_second,
    keyvalue_weight,
    keyvalue_first,
    keyvalue_second,
    headgate_weight,
    headgate_first,
    headgate_second,
    output_weight,
    output_first,
    output_second,
    expand_weight,
    expand_first,
    expand_second,
    reduce_weight,
    reduce_first,
    reduce_second,
):
    head_devices = lax.axis_size("head")
    heads_local = H // head_devices
    groups_local = KVH // head_devices
    repeat = H // KVH
    labels = jnp.arange(NDOM, dtype=jnp.int32)
    onehot = domain_ids[:, None] == labels[None, :]
    token_weight = jnp.sum(jnp.where(onehot, domain_weights[None, :], 0.0), -1)
    upstream = cotangent.astype(jnp.float32) * token_weight[:, None]
    norm_one = gains[:D]
    norm_two = gains[D : 2 * D]
    query_gain = gains[2 * D : 2 * D + HD]
    key_gain = gains[2 * D + HD :]
    inputs = tokens.astype(jnp.float32)
    normed = norm_rows(inputs, norm_one).astype(jnp.bfloat16)
    group_in, expand_all, reduce_all = (
        lax.all_gather(normed, "head", axis=0, tiled=True),
        lax.all_gather(expand_weight.astype(jnp.bfloat16), "head", axis=1, tiled=True),
        lax.all_gather(reduce_weight.astype(jnp.bfloat16), "head", axis=1, tiled=True),
    )
    query_all, keyvalue_all, headgate_all, output_all = (
        lax.all_gather(query_weight.astype(jnp.bfloat16), "wide", axis=0, tiled=True),
        lax.all_gather(keyvalue_weight.astype(jnp.bfloat16), "wide", axis=1, tiled=True),
        lax.all_gather(headgate_weight.astype(jnp.bfloat16), "wide", axis=0, tiled=True),
        lax.all_gather(output_weight.astype(jnp.bfloat16), "wide", axis=1, tiled=True),
    )
    group_size = group_in.shape[0]
    places = positions(segment_ids)
    query_raw = jnp.dot(group_in, query_all, preferred_element_type=jnp.float32)
    key_raw = jnp.dot(group_in, keyvalue_all[0], preferred_element_type=jnp.float32)
    value_raw = jnp.dot(group_in, keyvalue_all[1], preferred_element_type=jnp.float32)
    gate_logit = jnp.dot(group_in, headgate_all, preferred_element_type=jnp.float32)
    query_rot = head_prep(query_raw, query_gain, places).astype(jnp.bfloat16)
    key_low = head_prep(key_raw, key_gain, places).astype(jnp.bfloat16)
    value_low = value_raw.astype(jnp.bfloat16).reshape(group_size, groups_local, HD)
    block_size = min(512, group_size)
    block_count = group_size // block_size
    key_places = jnp.arange(group_size, dtype=jnp.int32)
    score_scale = HD ** (-0.5)
    block_starts = jnp.arange(block_count, dtype=jnp.int32) * block_size
    query_blocks = query_rot.reshape(block_count, block_size, groups_local, repeat, HD)

    def masked_scores(query_block, start):
        raw_scores = (
            jnp.einsum("qgrd,kgd->grqk", query_block, key_low, preferred_element_type=jnp.float32)
            * score_scale
        )
        query_places = start + jnp.arange(block_size, dtype=jnp.int32)
        query_segments = lax.dynamic_slice_in_dim(segment_ids, start, block_size)
        allowed = (key_places[None, :] <= query_places[:, None]) & (
            segment_ids[None, :] == query_segments[:, None]
        )
        return jnp.where(allowed, raw_scores, MASK_FILL)

    def attend_block(args):
        query_block, start = args
        scores = masked_scores(query_block, start)
        largest = jnp.max(scores, -1, keepdims=True)
        exponent = jnp.exp(scores - largest)
        totals = jnp.sum(exponent, -1, keepdims=True)
        probs = (exponent / totals).astype(jnp.bfloat16)
        attended = jnp.einsum(
            "grqk,kgd->qgrd", probs, value_low, preferred_element_type=jnp.float32
        )
        return (attended, largest[..., 0] + jnp.log(totals[..., 0]))

    attended, log_totals = lax.map(attend_block, (query_blocks, block_starts))
    attended = attended.reshape(group_size, heads_local, HD)
    gate_sig = jax.nn.sigmoid(gate_logit)
    gated = (
        (attended * gate_sig[:, :, None]).reshape(group_size, heads_local * HD).astype(jnp.bfloat16)
    )
    piece = gated
    residual = inputs + lax.psum_scatter(
        jnp.dot(piece, output_all, preferred_element_type=jnp.float32),
        "head",
        scatter_dimension=0,
        tiled=True,
    )
    mixed = norm_rows(residual, norm_two).astype(jnp.bfloat16)
    mixed_all = lax.all_gather(mixed, "wide", axis=0, tiled=True)
    gate_pre = jnp.dot(mixed_all, expand_all[0], preferred_element_type=jnp.float32)
    up_pre = jnp.dot(mixed_all, expand_all[1], preferred_element_type=jnp.float32)
    activation = (jax.nn.silu(gate_pre) * up_pre).astype(jnp.bfloat16)
    piece = activation
    block_output = (
        residual
        + lax.psum_scatter(
            jnp.dot(piece, reduce_all, preferred_element_type=jnp.float32).astype(jnp.bfloat16),
            "wide",
            scatter_dimension=0,
            tiled=True,
        ).astype(jnp.float32)
    ).astype(jnp.bfloat16)
    upstream_all = lax.all_gather(upstream.astype(jnp.bfloat16), "wide", axis=0, tiled=True)
    activation_grad = contract_cols(upstream_all, reduce_all)
    reduce_grad = contract_rows(activation, upstream_all)
    gate_grad, up_grad = swiglu_back(activation_grad, gate_pre, up_pre)
    expand_grad = jnp.stack(
        [contract_rows(mixed_all, gate_grad), contract_rows(mixed_all, up_grad)]
    )
    mixed_grad = lax.psum_scatter(
        contract_cols(gate_grad, expand_all[0]) + contract_cols(up_grad, expand_all[1]),
        "wide",
        scatter_dimension=0,
        tiled=True,
    )
    _, second_back = jax.vjp(norm_rows, residual, norm_two)
    residual_from, two_grad = second_back(mixed_grad)
    residual_grad = upstream + residual_from
    expand_part, reduce_part = (
        lax.psum_scatter(
            expand_grad.astype(jnp.bfloat16), "head", scatter_dimension=1, tiled=True
        ).astype(jnp.float32),
        lax.psum_scatter(
            reduce_grad.astype(jnp.bfloat16), "head", scatter_dimension=1, tiled=True
        ).astype(jnp.float32),
    )
    residual_all = lax.all_gather(residual_grad.astype(jnp.bfloat16), "head", axis=0, tiled=True)
    output_grad = contract_rows(gated, residual_all)
    gated_grad = contract_cols(residual_all, output_all).reshape(group_size, heads_local, HD)
    attended_grad = (gated_grad * gate_sig[:, :, None]).astype(jnp.bfloat16)
    logit_grad = (jnp.sum(gated_grad * attended, -1) * gate_sig * (1.0 - gate_sig)).astype(
        jnp.bfloat16
    )
    grad_blocks = attended_grad.reshape(block_count, block_size, groups_local, repeat, HD)

    def back_block(carry, args):
        key_sum, value_sum = carry
        query_block, grad_block, log_block, start = args
        scores = masked_scores(query_block, start)
        probs = jnp.exp(scores - log_block[..., None])
        prob_grad = jnp.einsum(
            "qgrd,kgd->grqk", grad_block, value_low, preferred_element_type=jnp.float32
        )
        inner = jnp.sum(probs * prob_grad, -1, keepdims=True)
        score_grad = (probs * (prob_grad - inner)).astype(jnp.bfloat16)
        query_grad = (
            jnp.einsum("grqk,kgd->qgrd", score_grad, key_low, preferred_element_type=jnp.float32)
            * score_scale
        )
        key_sum = (
            key_sum
            + jnp.einsum(
                "grqk,qgrd->kgd", score_grad, query_block, preferred_element_type=jnp.float32
            )
            * score_scale
        )
        value_sum = value_sum + jnp.einsum(
            "grqk,qgrd->kgd",
            probs.astype(jnp.bfloat16),
            grad_block,
            preferred_element_type=jnp.float32,
        )
        return ((key_sum, value_sum), query_grad)

    zeros = jnp.zeros((group_size, groups_local, HD), jnp.float32)
    (key_rot_grad, value_grad), query_grads = lax.scan(
        back_block, (zeros, zeros), (query_blocks, grad_blocks, log_totals, block_starts)
    )
    _, query_back = jax.vjp(lambda raw, gain: head_prep(raw, gain, places), query_raw, query_gain)
    query_raw_grad, query_gain_grad = query_back(query_grads.reshape(group_size, heads_local, HD))
    _, key_back = jax.vjp(lambda raw, gain: head_prep(raw, gain, places), key_raw, key_gain)
    key_raw_grad, key_gain_grad = key_back(key_rot_grad)
    query_low_grad = query_raw_grad.astype(jnp.bfloat16)
    key_low_grad = key_raw_grad.astype(jnp.bfloat16)
    value_low_grad = value_grad.reshape(group_size, groups_local * HD).astype(jnp.bfloat16)
    query_wgrad = contract_rows(group_in, query_low_grad)
    keyvalue_wgrad = jnp.stack(
        [contract_rows(group_in, key_low_grad), contract_rows(group_in, value_low_grad)]
    )
    headgate_wgrad = contract_rows(group_in, logit_grad)
    total = contract_cols(query_low_grad, query_all)
    total = total + contract_cols(key_low_grad, keyvalue_all[0])
    total = total + contract_cols(value_low_grad, keyvalue_all[1])
    normed_grad = lax.psum_scatter(
        (total + contract_cols(logit_grad, headgate_all)).astype(jnp.bfloat16),
        "head",
        scatter_dimension=0,
        tiled=True,
    ).astype(jnp.float32)
    _, first_back = jax.vjp(norm_rows, inputs, norm_one)
    input_from, one_grad = first_back(normed_grad)
    input_grad = residual_grad + input_from
    query_part, keyvalue_part, headgate_part, output_part = (
        lax.psum_scatter(
            query_wgrad.astype(jnp.bfloat16), "wide", scatter_dimension=0, tiled=True
        ).astype(jnp.float32),
        lax.psum_scatter(
            keyvalue_wgrad.astype(jnp.bfloat16), "wide", scatter_dimension=1, tiled=True
        ).astype(jnp.float32),
        lax.psum_scatter(
            headgate_wgrad.astype(jnp.bfloat16), "wide", scatter_dimension=0, tiled=True
        ).astype(jnp.float32),
        lax.psum_scatter(
            output_grad.astype(jnp.bfloat16), "wide", scatter_dimension=1, tiled=True
        ).astype(jnp.float32),
    )
    gain_partial = jnp.concatenate([one_grad, two_grad, query_gain_grad, key_gain_grad])
    parts = (query_part, keyvalue_part, headgate_part, output_part, expand_part, reduce_part)
    squares = jnp.zeros((), jnp.float32)
    for part_grad in parts:
        squares = squares + jnp.sum(part_grad * part_grad)
    gains_grad, square_total = lax.psum((gain_partial, squares), ("head", "wide"))
    grad_norm = jnp.sqrt(square_total + jnp.sum(gains_grad * gains_grad))
    clip = CLIP_NORM / jnp.maximum(grad_norm, CLIP_NORM)
    gains_new = adam_step(gains, gains_grad * clip, gain_first, gain_second, GAIN_RATE, 0.0)
    masters = (
        query_weight,
        keyvalue_weight,
        headgate_weight,
        output_weight,
        expand_weight,
        reduce_weight,
    )
    states = (
        (query_first, query_second),
        (keyvalue_first, keyvalue_second),
        (headgate_first, headgate_second),
        (output_first, output_second),
        (expand_first, expand_second),
        (reduce_first, reduce_second),
    )
    results = [grad_norm, block_output, input_grad, gains_new[0], gains_new[1], gains_new[2]]
    for index in range(6):
        rate = OUTPUT_RATE if index == 3 else WEIGHT_RATE
        updated, first_new, second_new = adam_step(
            masters[index],
            parts[index] * clip,
            states[index][0],
            states[index][1],
            rate,
            WEIGHT_DECAY,
        )
        results = results + [updated, first_new, second_new, updated.astype(jnp.bfloat16)]
    return tuple(results)


def solution(mesh):
    return jax.shard_map(
        body,
        mesh=mesh,
        in_specs=(
            P(("wide", "head"), None),
            P(("wide", "head"), None),
            P("wide"),
            P(("wide", "head")),
            P(),
            P(),
            P(),
            P(),
            P("wide", "head"),
            P("wide", "head"),
            P("wide", "head"),
            P(None, "wide", "head"),
            P(None, "wide", "head"),
            P(None, "wide", "head"),
            P("wide", "head"),
            P("wide", "head"),
            P("wide", "head"),
            P("head", "wide"),
            P("head", "wide"),
            P("head", "wide"),
            P(None, "head", "wide"),
            P(None, "head", "wide"),
            P(None, "head", "wide"),
            P("wide", "head"),
            P("wide", "head"),
            P("wide", "head"),
        ),
        out_specs=(
            P(),
            P(("wide", "head"), None),
            P(("wide", "head"), None),
            P(),
            P(),
            P(),
            P("wide", "head"),
            P("wide", "head"),
            P("wide", "head"),
            P("wide", "head"),
            P(None, "wide", "head"),
            P(None, "wide", "head"),
            P(None, "wide", "head"),
            P(None, "wide", "head"),
            P("wide", "head"),
            P("wide", "head"),
            P("wide", "head"),
            P("wide", "head"),
            P("head", "wide"),
            P("head", "wide"),
            P("head", "wide"),
            P("head", "wide"),
            P(None, "head", "wide"),
            P(None, "head", "wide"),
            P(None, "head", "wide"),
            P(None, "head", "wide"),
            P("wide", "head"),
            P("wide", "head"),
            P("wide", "head"),
            P("wide", "head"),
        ),
        check_vma=False,
    )
```

profile of v0, /device:TPU:0, one launch (start us, length us, event | category | flops | bytes accessed | tf_op | source)
XLA Modules:
  0.0 1642.1 jit_solution(12389435591505945076)
XLA Ops:
  12.0 2.5 fusion.72
  17.8 28.0 %all_gather.35 = bf16[2048,4]{0,1:T(4,128)(2,1)S(1)} all-gather(bf16[256,4]{0,1:T(4,128)(2,1)S(1)} %convert_element_type.174), channel_id=1, replica_groups=mesh['head'=4,'wide'=8] {'wide'}, dimensions={0}, use_global_device_ids=true | all-gather | bytes 18432 | tf_op jit(solution)/shard_map/all_gather | solution.py:140
  48.8 14.0 all-gather.14.cloned.1.call-done
  64.8 33.2 %all-gather.10.cloned.1.call-done = bf16[1024,2048]{1,0:T(8,128)(2,1)} async-done(((bf16[256,2048]{1,0:T(8,128)(2,1)}), bf16[1024,2048]{1,0:T(8,128)(2,1)}) %all-gather.10.cloned.1.call-update) | async-done | bytes 4194320 | tf_op jit(solution)/shard_map/all_gather | solution.py:133
  98.0 3.6 multiply_reduce_fusion.9
  104.5 3.8 convolution_convert_fusion.9
  109.3 40.7 %all-gather.12.cloned.1.call-done = bf16[2048,512]{1,0:T(8,128)(2,1)} async-done(((bf16[256,512]{1,0:T(8,128)(2,1)}), bf16[2048,512]{1,0:T(8,128)(2,1)}) %all-gather.12.cloned.1.call-update) | async-done | bytes 2097168 | tf_op jit(solution)/shard_map/all_gather | solution.py:138
  150.0 6.6 multiply_reduce_fusion.6
  168.0 26.0 %while.28 = (s32[]{:T(128)}, f32[2,512,2,2,128]{4,1,3,2,0:T(8,128)}, f32[2,2,2,512]{3,2,1,0:T(2,128)S(1)}, s32[2]{0:T(128)S(1)}, s32[1024]{0:T(1024)S(1)}, /*ind...) while((s32[]{:T(128)}, ...), condition=%wide.region_9.10_spmd.clone, body=%wide.region_6.9_spmd.clone.sunk | while | flops 1100478976 | bytes 46741744 | solution.py:183
  174.0 2.5 fusion.205
  176.5 3.3 fusion.206
  186.8 2.5 fusion.205
  189.3 3.3 fusion.206
  194.0 5.3 copy.148
  199.3 3.9 reshape.305
  205.5 7.6 fusion.139
  217.0 3.4 convert_element_type.178
  220.4 63.1 %reduce-scatter.13.cloned.1.call-done = f32[256,2048]{1,0:T(8,128)} async-done(((f32[1024,2048]{1,0:T(8,128)}), f32[256,2048]{1,0:T(8,128)}) %reduce-scatter.13.cloned.1.call-update) | async-done | bytes 2097168 | tf_op jit(solution)/shard_map/reduce_scatter | solution.py:190
  286.8 27.4 %all-gather.18.cloned.1.call-done = bf16[768,2048]{1,0:T(8,128)(2,1)} async-done(((bf16[768,512]{1,0:T(8,128)(2,1)}), bf16[768,2048]{1,0:T(8,128)(2,1)}) %all-gather.18.cloned.1.call-update) | async-done | bytes 3145744 | tf_op jit(solution)/shard_map/all_gather | solution.py:135
  314.2 127.9 %all-gather.16.cloned.1.call-done = bf16[2048,2048]{1,0:T(8,128)(2,1)} async-done(((bf16[256,2048]{1,0:T(8,128)(2,1)}), bf16[2048,2048]{1,0:T(8,128)(2,1)}) %all-gather.16.cloned.1.call-update) | async-done | bytes 8388624 | tf_op jit(solution)/shard_map/all_gather | solution.py:211
  442.1 12.0 fusion.138
  454.1 34.8 %all-gather.24.cloned.1.call-done = bf16[2,2048,768]{2,1,0:T(8,128)(2,1)} async-done(((bf16[2,512,768]{2,1,0:T(8,128)(2,1)}), bf16[2,2048,768]{2,1,0:T(8,128)(2,1)}) %all-gather.24.cloned.1.call-update) | async-done | bytes 6291472 | tf_op jit(solution)/shard_map/all_gather | solution.py:134
  488.9 127.9 %all-gather.22.cloned.1.call-done = bf16[2048,2048]{1,0:T(8,128)(2,1)} async-done(((bf16[256,2048]{1,0:T(8,128)(2,1)}), bf16[2048,2048]{1,0:T(8,128)(2,1)}) %all-gather.22.cloned.1.call-update) | async-done | bytes 8388624 | tf_op jit(solution)/shard_map/all_gather | solution.py:197
  616.8 11.8 fusion.67
  628.6 14.2 multiply_convert_fusion
  642.8 13.7 fusion.66
  656.5 13.8 convolution_add_fusion
  670.4 11.3 convolution_convert_fusion
  681.8 269.5 %reduce-scatter.15.cloned.1.call-done = f32[256,2048]{1,0:T(8,128)} async-done(((f32[2048,2048]{1,0:T(8,128)}), f32[256,2048]{1,0:T(8,128)}) %reduce-scatter.15.cloned.1.call-update) | async-done | bytes 2097168 | tf_op jit(solution)/shard_map/reduce_scatter | solution.py:218
  951.4 2.7 multiply_reduce_fusion.1
  954.1 149.0 %reduce-scatter.29.cloned.1.call-done = bf16[256,2048]{1,0:T(8,128)(2,1)} async-done(((bf16[2048,2048]{1,0:T(8,128)(2,1)}), bf16[256,2048]{1,0:T(8,128)(2,1)}) %reduce-scatter.29.cloned.1.call-update) | async-done | bytes 1048592 | tf_op jit(solution)/shard_map/reduce_scatter | solution.py:204
  1103.1 4.7 fusion.134
  1107.8 12.1 convolution_convert_fusion.1
  1120.0 10.9 fusion.63
  1130.9 9.3 fusion.64
  1140.2 3.2 pad_maximum_fusion
  1146.6 5.2 fusion.140
  1153.2 2.9 reshape.306
  1156.1 3.1 copy.160
  1159.2 2.4 multiply_reduce_fusion.2
  1163.8 4.3 copy.151
  1168.1 2.7 multiply_convert_fusion.3
  1170.9 36.4 %while.29 = (s32[]{:T(128)}, f32[1024,2,128]{0,2,1:T(8,128)S(1)}, f32[1024,2,128]{0,2,1:T(8,128)}, f32[2,512,2,2,128]{4,1,0,3,2:T(8,128)}, bf16[2,512,2,2,128]{4...) while((s32[]{:T(128)}, f32[1024,2,128]{0,2,1:T(8,128)S(1)}, ...), condition=%wide.region_16.17_spmd.clone, body=%wide.region_14.16_spmd.clone.sunk | while | flops 2718956032 | bytes 103356784 | solution.py:274
  1176.2 2.6 fusion.220
  1178.8 3.3 fusion.217
  1182.2 2.4 fusion.218
  1194.6 2.6 fusion.220
  1197.2 3.3 fusion.217
  1200.5 2.4 fusion.218
  1210.7 3.7 fusion.70
  1224.5 6.4 convolution_convert_fusion.5
  1231.0 6.3 convolution_convert_fusion.4
  1241.1 5.7 fusion.141
  1246.9 7.2 add_convert_fusion
  1256.5 2.8 fusion.61
  1259.3 49.7 %reduce-scatter.31.cloned.1.call-done = bf16[256,4]{1,0:T(8,128)(2,1)} async-done(((bf16[2048,4]{1,0:T(8,128)(2,1)}), bf16[256,4]{1,0:T(8,128)(2,1)}) %reduce-scatter.31.cloned.1.call-update) | async-done | bytes 2064
  1310.5 69.4 %reduce-scatter.19.cloned.1.call-done = bf16[2,256,256]{2,1,0:T(8,128)(2,1)} async-done(((bf16[2,2048,256]{2,1,0:T(8,128)(2,1)}), bf16[2,256,256]{2,1,0:T(8,128)(2,1)}) %reduce-scatter.19.cloned.1.call-update) | async-done | bytes 262160 | tf_op jit(solution)/shard_map/reduce_scatter | solution.py:305
  1381.6 69.1 %reduce-scatter.17.cloned.1.call-done = bf16[256,512]{1,0:T(8,128)(2,1)} async-done(((bf16[2048,512]{1,0:T(8,128)(2,1)}), bf16[256,512]{1,0:T(8,128)(2,1)}) %reduce-scatter.17.cloned.1.call-update) | async-done | bytes 262160 | tf_op jit(solution)/shard_map/reduce_scatter | solution.py:302
  1454.4 67.7 %reduce-scatter.21.cloned.1.call-done = bf16[512,256]{1,0:T(8,128)(2,1)} async-done(((bf16[512,2048]{1,0:T(8,128)(2,1)}), bf16[512,256]{1,0:T(8,128)(2,1)}) %reduce-scatter.21.cloned.1.call-update) | async-done | bytes 262160 | tf_op jit(solution)/shard_map/reduce_scatter | solution.py:311
  1525.7 42.4 %reduce-scatter.27.cloned.1.call-done = bf16[256,2048]{1,0:T(8,128)(2,1)} async-done(((bf16[1024,2048]{1,0:T(8,128)(2,1)}), bf16[256,2048]{1,0:T(8,128)(2,1)}) %reduce-scatter.27.cloned.1.call-update) | async-done | bytes 1048592 | tf_op jit(solution)/shard_map/reduce_scatter | solution.py:292
  1570.5 40.0 %all-reduce.4 = (f32[]{:T(128)}, f32[4352]{0:T(1024)S(1)}) all-reduce(f32[]{:T(128)S(6)} %add.308, f32[4352]{0:T(1024)S(1)} %pad_maximum_fusion.4), channel_id=1, replica_groups=mesh['head'=4,'wide'=8] {'head','wide'}, use_global_device_ids=true, to_apply=%region_32.33 | all-reduce | flops 4353 | bytes 34824 | tf_op jit(solution)/shard_map/psum | solution.py:320
  1613.8 3.3 fusion.76
  1623.2 3.4 fusion.115
  1629.3 5.0 fusion.118
  (395 shorter events, 108.5 us)
Async XLA Ops:
  7.2 7.4 copy-start.51
  7.2 8.2 copy-start.48
  7.2 55.6 %all-gather.14.cloned.1.call-start = ((), (), s32[]{:S(2)}) async-start(), calls=%async_computation.12 | async-start | bytes 2359296 | tf_op jit(solution)/shard_map/all_gather | solution.py:139
  9.1 7.9 copy-start.55
  9.2 8.0 copy-start.93
  9.2 88.8 %all-gather.10.cloned.1.call-start = ((), (), s32[]{:S(2)}) async-start(), calls=%async_computation.10 | async-start | bytes 5242880 | tf_op jit(solution)/shard_map/all_gather | solution.py:133
  12.0 35.8 %copy-start.77 = (f32[2048]{0:T(1024)}, f32[2048]{0:T(1024)S(1)}, u32[]{:S(2)}) copy-start(f32[2048]{0:T(1024)S(1)} %get-tuple-element.394) | copy-start | bytes 24580
  14.6 135.5 %all-gather.12.cloned.1.call-start = ((), (), s32[]{:S(2)}) async-start(), calls=%async_computation.11 | async-start | bytes 2359296 | tf_op jit(solution)/shard_map/all_gather | solution.py:138
  15.4 190.1 %all-gather.20.cloned.1.call-start = ((), (), s32[]{:S(2)}) async-start(), calls=%async_computation.15 | async-start | bytes 2359296 | tf_op jit(solution)/shard_map/all_gather | solution.py:141
  16.2 267.3 %reduce-scatter.13.cloned.1.call-start = ((), (), s32[]{:S(2)}) async-start(), calls=%async_computation.16 | async-start | bytes 10485760 | tf_op jit(solution)/shard_map/reduce_scatter | solution.py:190
  17.0 91.6 %copy-start.97 = (f32[128]{0:T(128)}, f32[128]{0:T(128)S(1)}, u32[]{:S(2)}) copy-start(f32[128]{0:T(128)S(1)} %get-tuple-element.395) | copy-start | bytes 1540
  17.0 141.6 %copy-start.99 = (f32[128]{0:T(128)}, f32[128]{0:T(128)S(1)}, u32[]{:S(2)}) copy-start(f32[128]{0:T(128)S(1)} %get-tuple-element.396) | copy-start | bytes 1540
  45.8 56.4 %copy-start.75 = (bf16[2048,4]{0,1:T(4,128)(2,1)}, bf16[2048,4]{0,1:T(4,128)(2,1)S(1)}, u32[]{:S(2)}) copy-start(bf16[2048,4]{0,1:T(4,128)(2,1)S(1)} %all_gather.35) | copy-start | bytes 49156
  46.8 62.0 %copy-start.35 = (f32[1024,64]{0,1:T(8,128)}, f32[1024,64]{0,1:T(8,128)S(1)}, u32[]{:S(2)}) copy-start(f32[1024,64]{0,1:T(8,128)S(1)} %get-tuple-element.397) | copy-start | bytes 786436
  46.8 62.0 %copy-start.37 = (f32[1024,64]{0,1:T(8,128)}, f32[1024,64]{0,1:T(8,128)S(1)}, u32[]{:S(2)}) copy-start(f32[1024,64]{0,1:T(8,128)S(1)} %get-tuple-element.398) | copy-start | bytes 786436
  101.6 7.0 copy-start.15
  194.0 9.3 copy-start
  194.0 9.3 copy-start.2
  194.0 9.3 copy-start.11
  194.0 9.3 copy-start.81
  194.0 9.3 copy-start.108
  205.5 7.7 copy-start.57
  213.2 101.0 %all-gather.18.cloned.1.call-start = ((), (), s32[]{:S(2)}) async-start(), calls=%async_computation.14 | async-start | bytes 3932160 | tf_op jit(solution)/shard_map/all_gather | solution.py:135
  215.5 226.5 %all-gather.16.cloned.1.call-start = ((), (), s32[]{:S(2)}) async-start(), calls=%async_computation.13 | async-start | bytes 9437184 | tf_op jit(solution)/shard_map/all_gather | solution.py:211
  216.9 66.6 %copy-start.9 = (bf16[256,2048]{1,0:T(8,128)(2,1)S(1)}, bf16[256,2048]{1,0:T(8,128)(2,1)}, u32[]{:S(2)}) copy-start(bf16[256,2048]{1,0:T(8,128)(2,1)} %param.30) | copy-start | bytes 3145732
  216.9 271.9 %all-gather.24.cloned.1.call-start = ((), (), s32[]{:S(2)}) async-start(), calls=%async_computation.18 | async-start | bytes 7864320 | tf_op jit(solution)/shard_map/all_gather | solution.py:134
  220.4 396.4 %all-gather.22.cloned.1.call-start = ((), (), s32[]{:S(2)}) async-start(), calls=%async_computation.17 | async-start | bytes 9437184 | tf_op jit(solution)/shard_map/all_gather | solution.py:197
  286.7 664.6 %reduce-scatter.15.cloned.1.call-start = ((), (), s32[]{:S(2)}) async-start(), calls=%async_computation.19 | async-start | bytes 18874368 | tf_op jit(solution)/shard_map/reduce_scatter | solution.py:218
  616.8 11.8 copy-start.105
  642.8 13.8 copy-start.110
  642.8 13.8 copy-start.106
  670.4 432.7 %reduce-scatter.29.cloned.1.call-start = ((), (), s32[]{:S(2)}) async-start(), calls=%async_computation.27 | async-start | bytes 9437184 | tf_op jit(solution)/shard_map/reduce_scatter | solution.py:204
  681.7 421.3 %copy-start.39 = (bf16[256,2048]{1,0:T(8,128)(2,1)S(1)}, bf16[256,2048]{1,0:T(8,128)(2,1)}, u32[]{:S(2)}) copy-start(bf16[256,2048]{1,0:T(8,128)(2,1)} %param.31) | copy-start | bytes 3145732
  681.8 464.8 %all-gather.26.cloned.1.call-start = ((), (), s32[]{:S(2)}) async-start(), calls=%async_computation.20 | async-start | bytes 5242880 | tf_op jit(solution)/shard_map/all_gather | solution.py:235
  1107.8 146.4 %reduce-scatter.25.cloned.1.call-start = ((), (), s32[]{:S(2)}) async-start(), calls=%async_computation.25 | async-start | bytes 3932160 | tf_op jit(solution)/shard_map/reduce_scatter | solution.py:231
  1119.9 11.0 copy-start.111
  1119.9 136.6 %reduce-scatter.23.cloned.1.call-start = ((), (), s32[]{:S(2)}) async-start(), calls=%async_computation.24 | async-start | bytes 7864320 | tf_op jit(solution)/shard_map/reduce_scatter | solution.py:228
  1143.5 165.5 %reduce-scatter.31.cloned.1.call-start = ((), (), s32[]{:S(2)}) async-start(), calls=%async_computation.28 | async-start | bytes 589824
  1163.8 7.0 copy-start.1
  1163.8 7.0 copy-start.3
  1163.8 7.0 copy-start.12
  1163.8 7.0 copy-start.56
  1163.8 7.0 copy-start.82
  1163.8 7.0 copy-start.109
  1170.8 37.9 %copy-start.36 = (f32[1024,64]{0,1:T(8,128)S(1)}, f32[1024,64]{0,1:T(8,128)}, u32[]{:S(2)}) copy-start(f32[1024,64]{0,1:T(8,128)} %copy-done.35) | copy-start | bytes 786436
  1210.7 169.2 %reduce-scatter.19.cloned.1.call-start = ((), (), s32[]{:S(2)}) async-start(), calls=%async_computation.22 | async-start | bytes 2359296 | tf_op jit(solution)/shard_map/reduce_scatter | solution.py:305
  1217.4 233.3 %reduce-scatter.17.cloned.1.call-start = ((), (), s32[]{:S(2)}) async-start(), calls=%async_computation.21 | async-start | bytes 2359296 | tf_op jit(solution)/shard_map/reduce_scatter | solution.py:302
  1224.5 6.4 copy-start.60
  1230.9 6.9 copy-start.34
  1230.9 6.9 copy-start.44
  1231.0 291.2 %reduce-scatter.21.cloned.1.call-start = ((), (), s32[]{:S(2)}) async-start(), calls=%async_computation.23 | async-start | bytes 2359296 | tf_op jit(solution)/shard_map/reduce_scatter | solution.py:311
  1237.4 330.8 %reduce-scatter.27.cloned.1.call-start = ((), (), s32[]{:S(2)}) async-start(), calls=%async_computation.26 | async-start | bytes 5242880 | tf_op jit(solution)/shard_map/reduce_scatter | solution.py:292
  1254.0 314.2 %copy-start.10 = (bf16[256,2048]{1,0:T(8,128)(2,1)S(1)}, bf16[256,2048]{1,0:T(8,128)(2,1)}, u32[]{:S(2)}) copy-start(bf16[256,2048]{1,0:T(8,128)(2,1)} %param.30) | copy-start | bytes 3145732
  1254.0 314.2 %copy-start.78 = (f32[2048]{0:T(1024)S(1)}, f32[2048]{0:T(1024)}, u32[]{:S(2)}) copy-start(f32[2048]{0:T(1024)} %copy-done.77) | copy-start | bytes 24580
  1254.0 314.2 %copy-start.92 = (f32[256]{0:T(256)S(1)}, f32[256]{0:T(256)}, u32[]{:S(2)}) copy-start(f32[256]{0:T(256)} %copy-done.91) | copy-start | bytes 3076
  1254.0 316.4 %copy-start.86 = (f32[2048]{0:T(1024)S(1)}, f32[2048]{0:T(1024)}, u32[]{:S(2)}) copy-start(f32[2048]{0:T(1024)} %get-tuple-element.300) | copy-start | bytes 24580
  1254.1 316.4 %copy-start.96 = (f32[256]{0:T(256)S(1)}, f32[256]{0:T(256)}, u32[]{:S(2)}) copy-start(f32[256]{0:T(256)} %copy-done.95) | copy-start | bytes 3076
  1254.1 358.4 %copy-start.94 = (f32[256,4]{0,1:T(4,128)S(1)}, f32[256,4]{0,1:T(4,128)}, u32[]{:S(2)}) copy-start(f32[256,4]{0,1:T(4,128)} %param.44) | copy-start | bytes 12292
  1254.1 358.4 %copy-start.101 = (f32[256,4]{0,1:T(4,128)S(1)}, f32[256,4]{0,1:T(4,128)}, u32[]{:S(2)}) copy-start(f32[256,4]{0,1:T(4,128)} %param.45) | copy-start | bytes 12292
  1254.1 358.4 %copy-start.102 = (f32[256,4]{0,1:T(4,128)S(1)}, f32[256,4]{0,1:T(4,128)}, u32[]{:S(2)}) copy-start(f32[256,4]{0,1:T(4,128)} %param.46) | copy-start | bytes 12292
  1254.1 359.0 %copy-start.83 = (f32[4352]{0:T(1024)S(1)}, f32[4352]{0:T(1024)}, u32[]{:S(2)}) copy-start(f32[4352]{0:T(1024)} %param.35) | copy-start | bytes 52228
  1254.1 359.0 %copy-start.89 = (f32[4352]{0:T(1024)S(1)}, f32[4352]{0:T(1024)}, u32[]{:S(2)}) copy-start(f32[4352]{0:T(1024)} %param.36) | copy-start | bytes 52228
  1254.1 359.0 %copy-start.90 = (f32[4352]{0:T(1024)S(1)}, f32[4352]{0:T(1024)}, u32[]{:S(2)}) copy-start(f32[4352]{0:T(1024)} %param.37) | copy-start | bytes 52228
  1254.1 359.6 %copy-start.17 = (f32[256,2048]{1,0:T(8,128)S(1)}, f32[256,2048]{1,0:T(8,128)}, u32[]{:S(2)}) copy-start(f32[256,2048]{1,0:T(8,128)} %get-tuple-element.374) | copy-start | bytes 6291460
  (74 other events, 200.2 us)
Sparse Core Ops, SparseCore 0:
  10.8 51.9 all-gather.13
  65.0 32.9 all-gather.9
  100.7 49.2 all-gather.11
  152.5 49.5 all-gather.19
  213.3 70.1 reduce-scatter.12
  285.6 28.5 all-gather.17
  317.1 124.9 all-gather.15
  444.3 44.5 all-gather.23
  491.8 124.9 all-gather.21
  670.5 280.8 reduce-scatter.14
  955.0 148.0 reduce-scatter.28
  1107.9 33.4 all-gather.25
  1144.1 37.9 reduce-scatter.24
  1184.5 58.3 reduce-scatter.22
  1247.0 61.9 reduce-scatter.30
  1313.0 66.8 reduce-scatter.18
  1383.8 66.8 reduce-scatter.16
  1454.7 67.3 reduce-scatter.20
  1524.6 43.5 reduce-scatter.26
where the time goes:
time: 1650 us; the launch traced here: 1640 us
  waiting for transfers between devices  1190 us (72%)
  matrix products  200 us (12%)
  other arithmetic  93.3 us (6%)
  blocking collectives  68 us (4%)
  local copies, waits for them, and re-layouts  62.3 us (4%)
  between operations  21.9 us (1%)
    reduce_scatter x1, waiting for transfers between devices, body(): lax.psum_scatter(contract_cols(gate_grad, expand_all[0]) + contract_cols(...  270 us
    reduce_scatter x1, waiting for transfers between devices, body(): lax.psum_scatter(jnp.dot(piece, reduce_all, preferred_element_type=jnp.fl...  149 us
    all_gather x1, waiting for transfers between devices, body(): mixed_all = lax.all_gather(mixed, 'wide', axis=0, tiled=True)  128 us
    all_gather x1, waiting for transfers between devices, body(): lax.all_gather(upstream.astype(jnp.bfloat16), 'wide', axis=0, tiled=True)  128 us
    reduce_scatter x1, waiting for transfers between devices, body(): lax.psum_scatter(keyvalue_wgrad.astype(jnp.bfloat16), 'wide', scatter_dim...  69.4 us
    reduce_scatter x1, waiting for transfers between devices, body(): lax.psum_scatter(query_wgrad.astype(jnp.bfloat16), 'wide', scatter_dimens...  69.1 us
    reduce_scatter x1, waiting for transfers between devices, body(): lax.psum_scatter(output_grad.astype(jnp.bfloat16), 'wide', scatter_dimens...  67.7 us
    reduce_scatter x1, waiting for transfers between devices, body(): lax.psum_scatter(jnp.dot(piece, output_all, preferred_element_type=jnp.fl...  63.1 us
  transfers between devices with their start and end apart: 19, of which 15 were waited for; matrix products, arithmetic and copies ran while one was open for 15% of the time, Pallas kernels for 0%

commit v1 on v0

--- a/solution.py
+++ b/solution.py
@@ -1,6 +1,7 @@
 import jax
 import jax.numpy as jnp
 from jax import lax
+from jax.sharding import Mesh
 from jax.sharding import PartitionSpec as P
 
 D = 2048
@@ -85,6 +86,99 @@
     second_hat = second_new / (1.0 - BETA_SECOND**STEP)
     updated = weight - rate * (first_hat / (jnp.sqrt(second_hat) + ADAM_EPS) + decay * weight)
     return (updated, first_new, second_new)
+
+
+def hop(value, axis):
+    size = lax.axis_size(axis)
+    return lax.ppermute(value, axis, [(i, (i - 1) % size) for i in range(size)])
+
+
+def ring_gather(value, axis):
+    pieces = [value]
+    for _ in range(lax.axis_size(axis) - 1):
+        pieces.append(hop(pieces[-1], axis))
+    return pieces
+
+
+def ring_scatter(parts, axis):
+    size = lax.axis_size(axis)
+    total = parts[1 % size]
+    for step in range(1, size):
+        total = parts[(step + 1) % size] + hop(total.astype(jnp.bfloat16), axis).astype(jnp.float32)
+    return total
+
+
+def all_sum(value, axis):
+    pieces = ring_gather(value, axis)
+    while len(pieces) > 1:
+        half = len(pieces) // 2
+        pieces = [pieces[i] + pieces[i + half] for i in range(half)]
+    return pieces[0]
+
+
+def rolled(values, shift, axis):
+    size = values.shape[axis]
+    return lax.dynamic_slice_in_dim(
+        jnp.concatenate([values, values], axis), lax.rem(shift + size, size), size, axis
+    )
+
+
+def to_relative(values):
+    rows, width = values.shape
+    shaped = values.reshape(rows, lax.axis_size("a"), lax.axis_size("b"), -1)
+    shaped = rolled(rolled(shaped, lax.axis_index("a"), 1), lax.axis_index("b"), 2)
+    return shaped.reshape(rows, width)
+
+
+def from_relative(values):
+    rows, width = values.shape
+    shaped = values.reshape(rows, lax.axis_size("a"), lax.axis_size("b"), -1)
+    shaped = rolled(rolled(shaped, -lax.axis_index("a"), 1), -lax.axis_index("b"), 2)
+    return shaped.reshape(rows, width)
+
+
+def wide_gather(value):
+    pieces = []
+    for piece in ring_gather(value, "a"):
+        pieces = pieces + ring_gather(piece, "b")
+    return pieces
+
+
+def wide_scatter(parts):
+    inner = lax.axis_size("b")
+    sums = []
+    for i in range(lax.axis_size("a")):
+        sums.append(ring_scatter(parts[i * inner : (i + 1) * inner], "b"))
+    return ring_scatter(sums, "a")
+
+
+def head_gather(value):
+    rows, width = value.shape
+    x_size = lax.axis_size("x")
+    x_me, c_me = lax.axis_index("x"), lax.axis_index("c")
+    result = jnp.zeros((x_size * 2 * rows, width), value.dtype)
+    for i, piece in enumerate(ring_gather(value, "x")):
+        for j, item in enumerate(ring_gather(piece, "c")):
+            slot = lax.rem(x_me + i, x_size) * 2 + lax.rem(c_me + j, 2)
+            result = lax.dynamic_update_slice(result, item, (slot * rows, 0))
+    return result
+
+
+def head_scatter(values, contract):
+    x_size = lax.axis_size("x")
+    x_me, c_me = lax.axis_index("x"), lax.axis_index("c")
+    width = values.shape[-1]
+    shaped = values.reshape(x_size, 2, -1, width)
+    rows = shaped.shape[2]
+    other = lax.dynamic_slice_in_dim(shaped, 1 - c_me, 1, 1).reshape(-1, width)
+    mine = lax.dynamic_slice_in_dim(shaped, c_me, 1, 1).reshape(-1, width)
+    received = lax.ppermute(contract(other).astype(jnp.bfloat16), "c", [(0, 1), (1, 0)])
+    total = contract(mine) + received.astype(jnp.float32)
+    parts = [
+        lax.dynamic_slice_in_dim(total, lax.rem(x_me + i, x_size) * rows, rows, 0)
+        for i in range(x_size)
+    ]
+    return ring_scatter(parts, "x")
 
 
 def body(
@@ -115,7 +209,8 @@
     reduce_first,
     reduce_second,
 ):
-    head_devices = lax.axis_size("head")
+    head_devices = lax.axis_size("x") * lax.axis_size("c")
+    outer, inner = lax.axis_size("a"), lax.axis_size("b")
     heads_local = H // head_devices
     groups_local = KVH // head_devices
     repeat = H // KVH
@@ -129,23 +224,40 @@
     key_gain = gains[2 * D + HD :]
     inputs = tokens.astype(jnp.float32)
     normed = norm_rows(inputs, norm_one).astype(jnp.bfloat16)
-    group_in, expand_all, reduce_all = (
-        lax.all_gather(normed, "head", axis=0, tiled=True),
-        lax.all_gather(expand_weight.astype(jnp.bfloat16), "head", axis=1, tiled=True),
-        lax.all_gather(reduce_weight.astype(jnp.bfloat16), "head", axis=1, tiled=True),
-    )
-    query_all, keyvalue_all, headgate_all, output_all = (
-        lax.all_gather(query_weight.astype(jnp.bfloat16), "wide", axis=0, tiled=True),
-        lax.all_gather(keyvalue_weight.astype(jnp.bfloat16), "wide", axis=1, tiled=True),
-        lax.all_gather(headgate_weight.astype(jnp.bfloat16), "wide", axis=0, tiled=True),
-        lax.all_gather(output_weight.astype(jnp.bfloat16), "wide", axis=1, tiled=True),
-    )
+    group_in = lax.all_gather(to_relative(normed), ("x", "c"), axis=0, tiled=True)
+    query_width, key_width = query_weight.shape[1], keyvalue_weight.shape[2]
+    pad = -heads_local % 128
+    low_weights = [
+        query_weight,
+        keyvalue_weight[0],
+        keyvalue_weight[1],
+        headgate_weight,
+        jnp.zeros((query_weight.shape[0], pad), jnp.float32),
+    ]
+    project = jnp.concatenate(low_weights, 1).astype(jnp.bfloat16)
+    project_all = jnp.concatenate(wide_gather(project), 0)
+    output_all = jnp.concatenate(wide_gather(output_weight.astype(jnp.bfloat16)), 1)
+    value_from = query_width + key_width
+    gate_from = value_from + key_width
+    expand_low = jnp.concatenate([expand_weight[0], expand_weight[1]], 1).astype(jnp.bfloat16)
+    reduce_low = reduce_weight.astype(jnp.bfloat16)
+    expand_all = [
+        lax.all_gather(piece, ("x", "c"), axis=0, tiled=True)
+        for piece in ring_gather(expand_low, "b")
+    ]
+    reduce_all = [
+        lax.all_gather(piece, ("x", "c"), axis=1, tiled=True)
+        for piece in ring_gather(reduce_low, "b")
+    ]
+    hidden = reduce_low.shape[0]
+    upstream_parts = ring_gather(upstream.astype(jnp.bfloat16), "a")
     group_size = group_in.shape[0]
     places = positions(segment_ids)
-    query_raw = jnp.dot(group_in, query_all, preferred_element_type=jnp.float32)
-    key_raw = jnp.dot(group_in, keyvalue_all[0], preferred_element_type=jnp.float32)
-    value_raw = jnp.dot(group_in, keyvalue_all[1], preferred_element_type=jnp.float32)
-    gate_logit = jnp.dot(group_in, headgate_all, preferred_element_type=jnp.float32)
+    raw = jnp.dot(group_in, project_all, preferred_element_type=jnp.float32)
+    query_raw = raw[:, :query_width]
+    key_raw = raw[:, query_width:value_from]
+    value_raw = raw[:, value_from:gate_from]
+    gate_logit = raw[:, gate_from : gate_from + heads_local]
     query_rot = head_prep(query_raw, query_gain, places).astype(jnp.bfloat16)
     key_low = head_prep(key_raw, key_gain, places).astype(jnp.bfloat16)
     value_low = value_raw.astype(jnp.bfloat16).reshape(group_size, groups_local, HD)
@@ -186,53 +298,60 @@
     gated = (
         (attended * gate_sig[:, :, None]).reshape(group_size, heads_local * HD).astype(jnp.bfloat16)
     )
-    piece = gated
-    residual = inputs + lax.psum_scatter(
-        jnp.dot(piece, output_all, preferred_element_type=jnp.float32),
-        "head",
-        scatter_dimension=0,
-        tiled=True,
+    residual = inputs + from_relative(
+        head_scatter(
+            gated, lambda rows: jnp.dot(rows, output_all, preferred_element_type=jnp.float32)
+        )
     )
     mixed = norm_rows(residual, norm_two).astype(jnp.bfloat16)
-    mixed_all = lax.all_gather(mixed, "wide", axis=0, tiled=True)
-    gate_pre = jnp.dot(mixed_all, expand_all[0], preferred_element_type=jnp.float32)
-    up_pre = jnp.dot(mixed_all, expand_all[1], preferred_element_type=jnp.float32)
-    activation = (jax.nn.silu(gate_pre) * up_pre).astype(jnp.bfloat16)
-    piece = activation
-    block_output = (
-        residual
-        + lax.psum_scatter(
-            jnp.dot(piece, reduce_all, preferred_element_type=jnp.float32).astype(jnp.bfloat16),
-            "wide",
-            scatter_dimension=0,
-            tiled=True,
-        ).astype(jnp.float32)
-    ).astype(jnp.bfloat16)
-    upstream_all = lax.all_gather(upstream.astype(jnp.bfloat16), "wide", axis=0, tiled=True)
-    activation_grad = contract_cols(upstream_all, reduce_all)
-    reduce_grad = contract_rows(activation, upstream_all)
-    gate_grad, up_grad = swiglu_back(activation_grad, gate_pre, up_pre)
-    expand_grad = jnp.stack(
-        [contract_rows(mixed_all, gate_grad), contract_rows(mixed_all, up_grad)]
-    )
-    mixed_grad = lax.psum_scatter(
-        contract_cols(gate_grad, expand_all[0]) + contract_cols(up_grad, expand_all[1]),
-        "wide",
-        scatter_dimension=0,
-        tiled=True,
-    )
+    mixed_parts = ring_gather(mixed, "a")
+    activations = [[] for _ in range(inner)]
+    hidden_grads = [[] for _ in range(inner)]
+    output_parts = []
+    mixed_grad_parts = []
+    for mixed_part, upstream_part in zip(mixed_parts, upstream_parts):
+        output_sum = 0.0
+        mixed_grad_sum = 0.0
+        for j in range(inner):
+            both = jnp.dot(mixed_part, expand_all[j], preferred_element_type=jnp.float32)
+            gate_pre, up_pre = both[:, :hidden], both[:, hidden:]
+            activation = (jax.nn.silu(gate_pre) * up_pre).astype(jnp.bfloat16)
+            activation_grad = contract_cols(upstream_part, reduce_all[j])
+            hidden_grad = jnp.concatenate(swiglu_back(activation_grad, gate_pre, up_pre), 1)
+            output_sum = output_sum + jnp.dot(
+                activation, reduce_all[j], preferred_element_type=jnp.float32
+            )
+            mixed_grad_sum = mixed_grad_sum + contract_cols(hidden_grad, expand_all[j])
+            activations[j].append(activation)
+            hidden_grads[j].append(hidden_grad)
+        output_parts.append(output_sum)
+        mixed_grad_parts.append(mixed_grad_sum)
+    mixed_grad = ring_scatter(mixed_grad_parts, "a")
+    block_output = (residual + ring_scatter(output_parts, "a")).astype(jnp.bfloat16)
+    mixed_all = jnp.concatenate(mixed_parts, 0)
+    upstream_all = jnp.concatenate(upstream_parts, 0)
+    expand_parts = []
+    reduce_parts = []
+    for j in range(inner):
+        expand_grad = contract_rows(mixed_all, jnp.concatenate(hidden_grads[j], 0))
+        reduce_grad = contract_rows(jnp.concatenate(activations[j], 0), upstream_all)
+        expand_parts.append(
+            lax.psum_scatter(
+                expand_grad.astype(jnp.bfloat16), ("x", "c"), scatter_dimension=0, tiled=True
+            ).astype(jnp.float32)
+        )
+        reduce_parts.append(
+            lax.psum_scatter(
+                reduce_grad.astype(jnp.bfloat16), ("x", "c"), scatter_dimension=1, tiled=True
+            ).astype(jnp.float32)
+        )
+    expand_both = ring_scatter(expand_parts, "b")
+    expand_part = jnp.stack([expand_both[:, :hidden], expand_both[:, hidden:]])
+    reduce_part = ring_scatter(reduce_parts, "b")
     _, second_back = jax.vjp(norm_rows, residual, norm_two)
     residual_from, two_grad = second_back(mixed_grad)
     residual_grad = upstream + residual_from
-    expand_part, reduce_part = (
-        lax.psum_scatter(
-            expand_grad.astype(jnp.bfloat16), "head", scatter_dimension=1, tiled=True
-        ).astype(jnp.float32),
-        lax.psum_scatter(
-            reduce_grad.astype(jnp.bfloat16), "head", scatter_dimension=1, tiled=True
-        ).astype(jnp.float32),
-    )
-    residual_all = lax.all_gather(residual_grad.astype(jnp.bfloat16), "head", axis=0, tiled=True)
+    residual_all = head_gather(to_relative(residual_grad.astype(jnp.bfloat16)))
     output_grad = contract_rows(gated, residual_all)
     gated_grad = contract_cols(residual_all, output_all).reshape(group_size, heads_local, HD)
     attended_grad = (gated_grad * gate_sig[:, :, None]).astype(jnp.bfloat16)
@@ -281,43 +400,44 @@
     query_low_grad = query_raw_grad.astype(jnp.bfloat16)
     key_low_grad = key_raw_grad.astype(jnp.bfloat16)
     value_low_grad = value_grad.reshape(group_size, groups_local * HD).astype(jnp.bfloat16)
-    query_wgrad = contract_rows(group_in, query_low_grad)
-    keyvalue_wgrad = jnp.stack(
-        [contract_rows(group_in, key_low_grad), contract_rows(group_in, value_low_grad)]
-    )
-    headgate_wgrad = contract_rows(group_in, logit_grad)
-    total = contract_cols(query_low_grad, query_all)
-    total = total + contract_cols(key_low_grad, keyvalue_all[0])
-    total = total + contract_cols(value_low_grad, keyvalue_all[1])
-    normed_grad = lax.psum_scatter(
-        (total + contract_cols(logit_grad, headgate_all)).astype(jnp.bfloat16),
-        "head",
-        scatter_dimension=0,
-        tiled=True,
-    ).astype(jnp.float32)
+    low_grads = jnp.concatenate(
+        [
+            query_low_grad,
+            key_low_grad,
+            value_low_grad,
+            logit_grad,
+            jnp.zeros((group_size, pad), jnp.bfloat16),
+        ],
+        1,
+    )
+    project_grad = contract_rows(group_in, low_grads)
+    normed_grad = from_relative(
+        head_scatter(low_grads, lambda rows: contract_cols(rows, project_all))
+    )
     _, first_back = jax.vjp(norm_rows, inputs, norm_one)
     input_from, one_grad = first_back(normed_grad)
     input_grad = residual_grad + input_from
-    query_part, keyvalue_part, headgate_part, output_part = (
-        lax.psum_scatter(
-            query_wgrad.astype(jnp.bfloat16), "wide", scatter_dimension=0, tiled=True
-        ).astype(jnp.float32),
-        lax.psum_scatter(
-            keyvalue_wgrad.astype(jnp.bfloat16), "wide", scatter_dimension=1, tiled=True
-        ).astype(jnp.float32),
-        lax.psum_scatter(
-            headgate_wgrad.astype(jnp.bfloat16), "wide", scatter_dimension=0, tiled=True
-        ).astype(jnp.float32),
-        lax.psum_scatter(
-            output_grad.astype(jnp.bfloat16), "wide", scatter_dimension=1, tiled=True
-        ).astype(jnp.float32),
+    depth = project.shape[0]
+    project_part = wide_scatter(
+        [project_grad[i * depth : (i + 1) * depth] for i in range(outer * inner)]
+    )
+    query_part = project_part[:, :query_width]
+    keyvalue_part = jnp.stack(
+        [project_part[:, query_width:value_from], project_part[:, value_from:gate_from]]
+    )
+    headgate_part = project_part[:, gate_from : gate_from + heads_local]
+    output_part = wide_scatter(
+        [output_grad[:, i * depth : (i + 1) * depth] for i in range(outer * inner)]
     )
     gain_partial = jnp.concatenate([one_grad, two_grad, query_gain_grad, key_gain_grad])
     parts = (query_part, keyvalue_part, headgate_part, output_part, expand_part, reduce_part)
     squares = jnp.zeros((), jnp.float32)
     for part_grad in parts:
         squares = squares + jnp.sum(part_grad * part_grad)
-    gains_grad, square_total = lax.psum((gain_partial, squares), ("head", "wide"))
+    totals = jnp.concatenate([gain_partial, squares[None]])
+    for axis in ("c", "x", "b", "a"):
+        totals = all_sum(totals, axis)
+    gains_grad, square_total = totals[:-1], totals[-1]
     grad_norm = jnp.sqrt(square_total + jnp.sum(gains_grad * gains_grad))
     clip = CLIP_NORM / jnp.maximum(grad_norm, CLIP_NORM)
     gains_new = adam_step(gains, gains_grad * clip, gain_first, gain_second, GAIN_RATE, 0.0)
@@ -353,68 +473,35 @@
 
 
 def solution(mesh):
+    heads, wides = mesh.shape["head"], mesh.shape["wide"]
+    outer = 4 if wides % 4 == 0 else wides
+    grid = Mesh(
+        mesh.devices.reshape(heads // 2, 2, outer, wides // outer), ("x", "c", "a", "b")
+    )
+    wide, head = ("a", "b"), ("x", "c")
+    rows = P(wide + head, None)
+    by_wide = P(wide, head)
+    stacked = P(None, wide, head)
+    by_head = P(head, wide)
+    widened = P(None, head, wide)
     return jax.shard_map(
         body,
-        mesh=mesh,
-        in_specs=(
-            P(("wide", "head"), None),
-            P(("wide", "head"), None),
-            P("wide"),
-            P(("wide", "head")),
-            P(),
-            P(),
-            P(),
-            P(),
-            P("wide", "head"),
-            P("wide", "head"),
-            P("wide", "head"),
-            P(None, "wide", "head"),
-            P(None, "wide", "head"),
-            P(None, "wide", "head"),
-            P("wide", "head"),
-            P("wide", "head"),
-            P("wide", "head"),
-            P("head", "wide"),
-            P("head", "wide"),
-            P("head", "wide"),
-            P(None, "head", "wide"),
-            P(None, "head", "wide"),
-            P(None, "head", "wide"),
-            P("wide", "head"),
-            P("wide", "head"),
-            P("wide", "head"),
-        ),
-        out_specs=(
-            P(),
-            P(("wide", "head"), None),
-            P(("wide", "head"), None),
-            P(),
-            P(),
-            P(),
-            P("wide", "head"),
-            P("wide", "head"),
-            P("wide", "head"),
-            P("wide", "head"),
-            P(None, "wide", "head"),
-            P(None, "wide", "head"),
-            P(None, "wide", "head"),
-            P(None, "wide", "head"),
-            P("wide", "head"),
-            P("wide", "head"),
-            P("wide", "head"),
-            P("wide", "head"),
-            P("head", "wide"),
-            P("head", "wide"),
-            P("head", "wide"),
-            P("head", "wide"),
-            P(None, "head", "wide"),
-            P(None, "head", "wide"),
-            P(None, "head", "wide"),
-            P(None, "head", "wide"),
-            P("wide", "head"),
-            P("wide", "head"),
-            P("wide", "head"),
-            P("wide", "head"),
-        ),
+        mesh=grid,
+        in_specs=(rows, rows, P(wide), P(wide + head))
+        + (P(),) * 4
+        + (by_wide,) * 3
+        + (stacked,) * 3
+        + (by_wide,) * 3
+        + (by_head,) * 3
+        + (widened,) * 3
+        + (by_wide,) * 3,
+        out_specs=(P(), rows, rows)
+        + (P(),) * 3
+        + (by_wide,) * 4
+        + (stacked,) * 4
+        + (by_wide,) * 4
+        + (by_head,) * 4
+        + (widened,) * 4
+        + (by_wide,) * 4,
         check_vma=False,
     )

time: 1650 us -> 961 us (0.58)
  waiting for transfers between devices: 1190 us -> 277 us
  local copies, waits for them, and re-layouts: 62.3 us -> 173 us
  starting transfers between devices: 1.2 us -> 111 us
  blocking collectives: 68 us -> 0 us
  other arithmetic: 93.3 us -> 138 us
  matrix products: 200 us -> 222 us
    reduce_scatter x9 -> x4, waiting for transfers between devices: 730 us -> 0.05 us  [the longest x2 0.04 us: body(): lax.psum_scatter(reduce_grad.astype(jnp.bfloat16), ('x', 'c'), scatter_di...]
    all_gather x9 -> x5, waiting for transfers between devices: 406 us -> 0.02 us  [the longest x2 0.02 us: body(): lax.all_gather(piece, ('x', 'c'), axis=0, tiled=True)]
    ppermute x0 -> x57, waiting for transfers between devices: none -> 277 us  [the longest x55 276 us: hop(): return lax.ppermute(value, axis, [(i, (i - 1) % size) for i in range(size)])]
    ppermute x0 -> x57, starting transfers between devices: none -> 110 us  [the longest x55 110 us: hop(): return lax.ppermute(value, axis, [(i, (i - 1) % size) for i in range(size)])]
    unnamed x215 -> x355, local copies, waits for them, and re-layouts: 17.7 us -> 67.6 us
    unnamed x20 -> x9, waiting for transfers between devices: 50 us -> 0.15 us
    psum x1 -> x0, blocking collectives: 40 us -> none  [body(): lax.psum((gain_partial, squares), ('head', 'wide'))]
    concatenate x1 -> x9, other arithmetic: 0.01 us -> 28.1 us  [the longest x8 28 us: rolled(): jnp.concatenate([values, values], axis)]
  transfers between devices with their start and end apart: 19 -> 66, of which waited for: 15 -> 29; matrix products, arithmetic and copies ran while one was open for 15% -> 48% of each run, Pallas kernels for 0% -> 0%
where the time goes in v1:
time: 961 us; the launch traced here: 951 us
  waiting for transfers between devices  277 us (29%)
  matrix products  222 us (23%)
  local copies, waits for them, and re-layouts  173 us (18%)
  other arithmetic  138 us (14%)
  starting transfers between devices  111 us (12%)
  between operations  22.9 us (2%)
    ppermute x55, waiting for transfers between devices, hop(): return lax.ppermute(value, axis, [(i, (i - 1) % size) for i in range(size)])  276 us
    ppermute x55, starting transfers between devices, hop(): return lax.ppermute(value, axis, [(i, (i - 1) % size) for i in range(size)])  110 us
    unnamed x355, local copies, waits for them, and re-layouts  67.6 us
    dot_general x19, matrix products, contract_cols(): lax.dot_general(left, right, (((1,), (1,)), ((), ())), preferred_element_...  66.8 us
    dot_general x6, matrix products, contract_rows(): lax.dot_general(left, right, (((0,), (0,)), ((), ())), preferred_element_...  52.7 us
    concatenate x8, other arithmetic, rolled(): jnp.concatenate([values, values], axis)  28 us
    dot_general x8, matrix products, body(): jnp.dot(mixed_part, expand_all[j], preferred_element_type=jnp.float32)  27.8 us
    convert_element_type x6, other arithmetic, body(): updated.astype(jnp.bfloat16)  20.3 us
  transfers between devices with their start and end apart: 66, of which 29 were waited for; matrix products, arithmetic and copies ran while one was open for 48% of the time, Pallas kernels for 0%

profile of v1, /device:TPU:0, one launch (start us, length us, event | category | flops | bytes accessed | tf_op | source)
XLA Modules:
  0.0 951.4 jit_solution(3631561956924290057)
XLA Ops:
  15.1 4.6 fusion.145
  26.0 34.5 %collective-permute-done.17 = bf16[512,1536]{1,0:T(8,128)(2,1)} collective-permute-done((bf16[512,1536]{1,0:T(8,128)(2,1)S(1)}, bf16[512,1536]{1,0:T(8,128)(2,1)}, u32[]{:S(2)}, u32[]{:S(2)}) %collective-permute-start.17) | collective-permute-done | bytes 1572896 | tf_op jit(solution)/shard_map/ppermute | solution.py:93
  63.3 17.2 %collective-permute-done.16 = bf16[768,512]{1,0:T(8,128)(2,1)S(1)} collective-permute-done((bf16[768,512]{1,0:T(8,128)(2,1)}, bf16[768,512]{1,0:T(8,128)(2,1)S(1)}, u32[]{:S(2)}, u32[]{:S(2)}) %collective-permute-start.16) | collective-permute-done | bytes 786464 | tf_op jit(solution)/shard_map/ppermute | solution.py:93
  94.5 11.1 %collective-permute-done.8 = bf16[512,256]{1,0:T(8,128)(2,1)} collective-permute-done((bf16[512,256]{1,0:T(8,128)(2,1)}, bf16[512,256]{1,0:T(8,128)(2,1)}, u32[]{:S(2)}, u32[]{:S(2)}) %collective-permute-start.8) | collective-permute-done | bytes 262176 | tf_op jit(solution)/shard_map/ppermute | solution.py:93
  106.1 4.3 collective-permute-start.10
  116.1 4.3 collective-permute-start.12
  129.9 5.5 collective-permute-done.3
  135.4 4.3 collective-permute-start.5
  148.6 7.5 collective-permute-done.4
  157.8 6.9 collective-permute-done.6
  165.6 8.8 fusion.227
  205.4 23.3 %while.28 = (s32[]{:T(128)}, f32[2,512,2,2,128]{4,1,3,2,0:T(8,128)}, f32[2,2,2,512]{3,2,1,0:T(2,128)S(1)}, s32[2]{0:T(128)S(1)}, s32[1024]{0:T(1024)S(1)}, /*ind...) while((s32[]{:T(128)}, ...), condition=%wide.region_9.10_spmd.clone, body=%wide.region_6.9_spmd.clone.sunk | while | flops 1100478976 | bytes 29964972 | solution.py:295
  228.7 5.3 copy.408
  234.1 3.9 reshape.351
  260.4 16.0 %collective-permute-done.18 = bf16[256,2048]{1,0:T(8,128)(2,1)} collective-permute-done((bf16[256,2048]{1,0:T(8,128)(2,1)}, bf16[256,2048]{1,0:T(8,128)(2,1)}, u32[]{:S(2)}, u32[]{:S(2)}) %collective-permute-start.18) | collective-permute-done | bytes 1048608 | tf_op jit(solution)/shard_map/ppermute | solution.py:93
  276.3 4.4 collective-permute-start.19
  304.6 4.3 collective-permute-start.20
  308.9 18.1 %collective-permute-done.21 = bf16[256,2048]{1,0:T(8,128)(2,1)} collective-permute-done((bf16[256,2048]{1,0:T(8,128)(2,1)S(1)}, bf16[256,2048]{1,0:T(8,128)(2,1)}, u32[]{:S(2)}, u32[]{:S(2)}) %collective-permute-start.21) | collective-permute-done | bytes 1048608 | tf_op jit(solution)/shard_map/ppermute | solution.py:93
  327.0 4.4 collective-permute-start.22
  331.3 6.2 fusion.235
  340.5 4.9 multiply_convert_fusion.12
  349.0 21.7 %collective-permute-done.22 = bf16[256,2048]{1,0:T(8,128)(2,1)} collective-permute-done((bf16[256,2048]{1,0:T(8,128)(2,1)}, bf16[256,2048]{1,0:T(8,128)(2,1)}, u32[]{:S(2)}, u32[]{:S(2)}) %collective-permute-start.22) | collective-permute-done | bytes 1048608 | tf_op jit(solution)/shard_map/ppermute | solution.py:93
  370.7 4.4 collective-permute-start.23
  381.7 15.2 %collective-permute-done.23 = bf16[256,2048]{1,0:T(8,128)(2,1)S(1)} collective-permute-done((bf16[256,2048]{1,0:T(8,128)(2,1)}, bf16[256,2048]{1,0:T(8,128)(2,1)S(1)}, u32[]{:S(2)}, u32[]{:S(2)}) %collective-permute-start.23) | collective-permute-done | bytes 1048608 | tf_op jit(solution)/shard_map/ppermute | solution.py:93
  402.9 7.3 convolution_convert_fusion.2
  410.5 12.1 %convolution_convert_fusion = bf16[2048,1536]{1,0:T(8,128)(2,1)} fusion(bf16[256,768]{1,0:T(8,128)(2,1)} %get-tuple-element.695, bf16[256,768]{1,0:T(8,128)(2,1)} %get-tuple-element.694, bf16[256,768]{1,0:T(8,128)(2,1)} %get-tuple-element.697, bf16[256,768]{1,0:T(8,128)(2,1)} %get-tuple-element.696, bf16[256,768]{1,0:T(8,128)(2,1)} %get-tuple-element.699, ...), kind=kOutput, calls=%fused_computation.65 | convolution fusion | flops 6487539712 | bytes 13631488 | tf_op jit(solution)/shard_map/dot_general | solution.py:62
  423.0 5.7 fusion.228
  428.7 5.3 multiply_convert_fusion.26
  444.5 4.5 collective-permute-start.24
  457.2 13.0 %collective-permute-done.24 = bf16[256,2048]{1,0:T(8,128)(2,1)S(1)} collective-permute-done((bf16[256,2048]{1,0:T(8,128)(2,1)S(1)}, bf16[256,2048]{1,0:T(8,128)(2,1)S(1)}, u32[]{:S(2)}, u32[]{:S(2)}) %collective-permute-start.24) | collective-permute-done | bytes 1048608 | tf_op jit(solution)/shard_map/ppermute | solution.py:93
  473.1 4.3 collective-permute-start.25
  482.6 7.4 convolution_convert_fusion.3
  490.4 5.0 fusion.155
  498.1 4.9 fusion.98
  503.0 4.3 collective-permute-start.26
  513.7 17.3 %collective-permute-done.26 = bf16[256,2048]{1,0:T(8,128)(2,1)S(1)} collective-permute-done((bf16[256,2048]{1,0:T(8,128)(2,1)S(1)}, bf16[256,2048]{1,0:T(8,128)(2,1)S(1)}, u32[]{:S(2)}, u32[]{:S(2)}) %collective-permute-start.26) | collective-permute-done | bytes 1048608 | tf_op jit(solution)/shard_map/ppermute | solution.py:93
  558.8 4.7 collective-permute-start.55
  563.5 9.7 %collective-permute-done.28 = bf16[256,2048]{1,0:T(8,128)(2,1)} collective-permute-done((bf16[256,2048]{1,0:T(8,128)(2,1)}, bf16[256,2048]{1,0:T(8,128)(2,1)}, u32[]{:S(2)}, u32[]{:S(2)}) %collective-permute-start.28) | collective-permute-done | bytes 1048608 | tf_op jit(solution)/shard_map/ppermute | solution.py:93
  573.3 11.3 %convolution_convert_fusion.1 = bf16[2048,1536]{1,0:T(8,128)(2,1)} fusion(bf16[256,768]{1,0:T(8,128)(2,1)} %get-tuple-element.705, bf16[256,768]{1,0:T(8,128)(2,1)} %get-tuple-element.704, bf16[256,768]{1,0:T(8,128)(2,1)} %copy-done.154, bf16[256,768]{1,0:T(8,128)(2,1)S(1)} %copy-done.153, bf16[256,768]{1,0:T(8,128)(2,1)S(1)} %copy-done.151, ...), kind=kOutput, calls=%fused_computation.66 | convolution fusion | flops 6487539712 | bytes 13631488 | tf_op jit(solution)/shard_map/dot_general | solution.py:62
  591.3 4.8 fusion.226
  605.3 4.3 copy.412
  612.5 49.0 %while.29 = (s32[]{:T(128)}, f32[1024,2,128]{0,2,1:T(8,128)S(1)}, f32[1024,2,128]{0,2,1:T(8,128)}, f32[2,512,2,2,128]{4,1,0,3,2:T(8,128)}, bf16[2,512,2,2,128]{4...) while((s32[]{:T(128)}, f32[1024,2,128]{0,2,1:T(8,128)S(1)}, ...), condition=%wide.region_14.15_spmd.clone, body=%wide.region_12.14_spmd.clone.sunk | while | flops 2718956032 | bytes 164175232 | solution.py:393
  632.3 4.6 fusion.351
  656.6 4.9 fusion.351
  676.1 8.4 concatenate.128
  684.5 5.6 reshape.362
  690.1 9.7 %fusion.225 = (bf16[2048,1152]{0,1:T(8,128)(2,1)S(1)}, f32[2048,1152]{0,1:T(8,128)}) fusion(bf16[1024,1152]{0,1:T(8,128)(2,1)} %concatenate.128, bf16[1024,2048]{1,0:T(8,128)(2,1)} %all-gather.6.cloned.1.call-done), kind=kOutput, calls=%fused_computation.439 | convolution fusion | flops 4834197504 | bytes 20709376 | tf_op jit(solution)/shard_map/dot_general | solution.py:62
  701.6 5.9 constant_dynamic-slice_fusion.1
  707.5 5.0 copy.457
  717.0 6.4 convolution_convert_fusion.4
  730.3 5.1 collective-permute-done.44
  741.1 6.6 collective-permute-done.36
  756.6 6.0 copy.456
  766.1 4.5 collective-permute-done.37
  772.4 4.5 collective-permute-start.38
  776.9 5.9 convert_add_fusion
  784.6 19.7 %collective-permute-done.38 = bf16[256,1152]{0,1:T(8,128)(2,1)S(1)} collective-permute-done((bf16[256,1152]{0,1:T(8,128)(2,1)S(1)}, bf16[256,1152]{0,1:T(8,128)(2,1)S(1)}, u32[]{:S(2)}, u32[]{:S(2)}) %collective-permute-start.38) | collective-permute-done | bytes 589856 | tf_op jit(solution)/shard_map/ppermute | solution.py:93
  817.7 4.0 reshape.365
  825.2 4.3 fusion.111
  838.5 25.9 %collective-permute-done.46 = bf16[512,1536]{1,0:T(8,128)(2,1)} collective-permute-done((bf16[512,1536]{1,0:T(8,128)(2,1)}, bf16[512,1536]{1,0:T(8,128)(2,1)}, u32[]{:S(2)}, u32[]{:S(2)}) %collective-permute-start.46) | collective-permute-done | bytes 1572896 | tf_op jit(solution)/shard_map/ppermute | solution.py:93
  890.0 4.5 collective-permute-start.51
  901.8 4.0 collective-permute-start.53
  926.1 8.0 fusion.207
  936.2 4.6 fusion.205
  (696 shorter events, 418.5 us)
Async XLA Ops:
  7.2 158.4 %all-gather.6.cloned.1.call-start = ((), (), s32[]{:S(2)}) async-start(), calls=%async_computation.4 | async-start | bytes 5242880 | tf_op jit(solution)/shard_map/all_gather | solution.py:227
  22.5 308.8 %all-gather.14.cloned.1.call-start = ((), (), s32[]{:S(2)}) async-start(), calls=%async_computation.8 | async-start | bytes 7864320 | tf_op jit(solution)/shard_map/all_gather | solution.py:245
  23.0 37.5 %collective-permute-start.17 = (bf16[512,1536]{1,0:T(8,128)(2,1)S(1)}, bf16[512,1536]{1,0:T(8,128)(2,1)}, u32[]{:S(2)}, u32[]{:S(2)}) collective-permute-start(bf16[512,1536]{1,0:T(8,128)(2,1)S(1)} %pad_maximum_fusion.3), channel_id=1, source_target_pairs={{0,1},{1,0},{2,3},{3,2},{4,5},{5,4},{6,7},{7,6},{8,9},{9,8},{10,11... | collective-permute-start | bytes 4718600 | tf_op jit(solution)/shard_map/ppermute | solution.py:93
  60.5 279.9 %all-gather.12.cloned.1.call-start = ((), (), s32[]{:S(2)}) async-start(), calls=%async_computation.7 | async-start | bytes 3932160 | tf_op jit(solution)/shard_map/all_gather | solution.py:249
  61.6 18.9 %collective-permute-start.16 = (bf16[768,512]{1,0:T(8,128)(2,1)}, bf16[768,512]{1,0:T(8,128)(2,1)S(1)}, u32[]{:S(2)}, u32[]{:S(2)}) collective-permute-start(bf16[768,512]{1,0:T(8,128)(2,1)} %convert_element_type.334), channel_id=1, source_target_pairs={{0,1},{1,0},{2,3},{3,2},{4,5},{5,4},{6,7},{7,6},{8,9},{9,8},{10,11... | collective-permute-start | bytes 2359304 | tf_op jit(solution)/shard_map/ppermute | solution.py:93
  81.4 341.5 %all-gather.10.cloned.1.call-start = ((), (), s32[]{:S(2)}) async-start(), calls=%async_computation.6 | async-start | bytes 7864320 | tf_op jit(solution)/shard_map/all_gather | solution.py:245
  84.2 38.9 %collective-permute-start = (bf16[256,1152]{1,0:T(8,128)(2,1)S(1)}, bf16[256,1152]{1,0:T(8,128)(2,1)}, u32[]{:S(2)}, u32[]{:S(2)}) collective-permute-start(bf16[256,1152]{1,0:T(8,128)(2,1)S(1)} %concatenate.106), channel_id=1, source_target_pairs={{0,1},{1,0},{2,3},{3,2},{4,5},{5,4},{6,7},{7,6},{8,9},{9,8},{10,11... | collective-permute-start | bytes 1769480 | tf_op jit(solution)/shard_map/ppermute | solution.py:93
  85.6 35.7 %collective-permute-start.1 = (bf16[256,1152]{1,0:T(8,128)(2,1)S(1)}, bf16[256,1152]{1,0:T(8,128)(2,1)}, u32[]{:S(2)}, u32[]{:S(2)}) collective-permute-start(bf16[256,1152]{1,0:T(8,128)(2,1)S(1)} %concatenate.106), channel_id=1, source_target_pairs={{0,6},{2,0},{4,2},{6,4},{1,7},{3,1},{5,3},{7,5},{8,14},{10,8},{12,... | collective-permute-start | bytes 1769480 | tf_op jit(solution)/shard_map/ppermute | solution.py:93
  90.0 15.6 %collective-permute-start.8 = (bf16[512,256]{1,0:T(8,128)(2,1)}, bf16[512,256]{1,0:T(8,128)(2,1)}, u32[]{:S(2)}, u32[]{:S(2)}) collective-permute-start(bf16[512,256]{1,0:T(8,128)(2,1)} %get-tuple-element.673), channel_id=1, source_target_pairs={{0,6},{2,0},{4,2},{6,4},{1,7},{3,1},{5,3},{7,5},{8,14},{10,8},{12,... | collective-permute-start | bytes 786440 | tf_op jit(solution)/shard_map/ppermute | solution.py:93
  90.5 21.9 %collective-permute-start.7 = (bf16[512,256]{1,0:T(8,128)(2,1)}, bf16[512,256]{1,0:T(8,128)(2,1)}, u32[]{:S(2)}, u32[]{:S(2)}) collective-permute-start(bf16[512,256]{1,0:T(8,128)(2,1)} %get-tuple-element.673), channel_id=1, source_target_pairs={{0,1},{1,0},{2,3},{3,2},{4,5},{5,4},{6,7},{7,6},{8,9},{9,8},{10,11... | collective-permute-start | bytes 786440 | tf_op jit(solution)/shard_map/ppermute | solution.py:93
  91.0 337.7 %all-gather.8.cloned.1.call-start = ((), (), s32[]{:S(2)}) async-start(), calls=%async_computation.5 | async-start | bytes 3932160 | tf_op jit(solution)/shard_map/all_gather | solution.py:249
  105.6 14.8 %collective-permute-start.9 = (bf16[512,256]{1,0:T(8,128)(2,1)}, bf16[512,256]{1,0:T(8,128)(2,1)}, u32[]{:S(2)}, u32[]{:S(2)}) collective-permute-start(bf16[512,256]{1,0:T(8,128)(2,1)} %collective-permute-done.8), channel_id=1, source_target_pairs={{0,1},{1,0},{2,3},{3,2},{4,5},{5,4},{6,7},{7,6},{8,9},{9,8},{10,11... | collective-permute-start | bytes 786440 | tf_op jit(solution)/shard_map/ppermute | solution.py:93
  106.1 8.5 collective-permute-start.10
  114.6 25.1 %collective-permute-start.11 = (bf16[512,256]{1,0:T(8,128)(2,1)}, bf16[512,256]{1,0:T(8,128)(2,1)S(1)}, u32[]{:S(2)}, u32[]{:S(2)}) collective-permute-start(bf16[512,256]{1,0:T(8,128)(2,1)} %collective-permute-done.10), channel_id=1, source_target_pairs={{0,1},{1,0},{2,3},{3,2},{4,5},{5,4},{6,7},{7,6},{8,9},{9,8},{10,11... | collective-permute-start | bytes 786440 | tf_op jit(solution)/shard_map/ppermute | solution.py:93
  116.1 11.4 %collective-permute-start.12 = (bf16[512,256]{1,0:T(8,128)(2,1)}, bf16[512,256]{1,0:T(8,128)(2,1)S(1)}, u32[]{:S(2)}, u32[]{:S(2)}) collective-permute-start(bf16[512,256]{1,0:T(8,128)(2,1)} %collective-permute-done.10), channel_id=1, source_target_pairs={{0,6},{2,0},{4,2},{6,4},{1,7},{3,1},{5,3},{7,5},{8,14},{10,8},{12,... | collective-permute-start | bytes 786440 | tf_op jit(solution)/shard_map/ppermute | solution.py:93
  121.4 14.0 %collective-permute-start.3 = (bf16[256,1152]{1,0:T(8,128)(2,1)}, bf16[256,1152]{1,0:T(8,128)(2,1)S(1)}, u32[]{:S(2)}, u32[]{:S(2)}) collective-permute-start(bf16[256,1152]{1,0:T(8,128)(2,1)} %collective-permute-done.1), channel_id=1, source_target_pairs={{0,6},{2,0},{4,2},{6,4},{1,7},{3,1},{5,3},{7,5},{8,14},{10,8},{12,... | collective-permute-start | bytes 1769480 | tf_op jit(solution)/shard_map/ppermute | solution.py:93
  122.4 21.0 %collective-permute-start.2 = (bf16[256,1152]{1,0:T(8,128)(2,1)}, bf16[256,1152]{1,0:T(8,128)(2,1)S(1)}, u32[]{:S(2)}, u32[]{:S(2)}) collective-permute-start(bf16[256,1152]{1,0:T(8,128)(2,1)} %collective-permute-done.1), channel_id=1, source_target_pairs={{0,1},{1,0},{2,3},{3,2},{4,5},{5,4},{6,7},{7,6},{8,9},{9,8},{10,11... | collective-permute-start | bytes 1769480 | tf_op jit(solution)/shard_map/ppermute | solution.py:93
  127.5 15.9 %collective-permute-start.13 = (bf16[512,256]{1,0:T(8,128)(2,1)S(1)}, bf16[512,256]{1,0:T(8,128)(2,1)S(1)}, u32[]{:S(2)}, u32[]{:S(2)}) collective-permute-start(bf16[512,256]{1,0:T(8,128)(2,1)S(1)} %collective-permute-done.12), channel_id=1, source_target_pairs={{0,1},{1,0},{2,3},{3,2},{4,5},{5,4},{6,7},{7,6},{8,9},{9,8},{10,11... | collective-permute-start | bytes 786440 | tf_op jit(solution)/shard_map/ppermute | solution.py:93
  135.4 11.9 %collective-permute-start.5 = (bf16[256,1152]{1,0:T(8,128)(2,1)S(1)}, bf16[256,1152]{1,0:T(8,128)(2,1)S(1)}, u32[]{:S(2)}, u32[]{:S(2)}) collective-permute-start(bf16[256,1152]{1,0:T(8,128)(2,1)S(1)} %collective-permute-done.3), channel_id=1, source_target_pairs={{0,6},{2,0},{4,2},{6,4},{1,7},{3,1},{5,3},{7,5},{8,14},{10,8},{12,... | collective-permute-start | bytes 1769480 | tf_op jit(solution)/shard_map/ppermute | solution.py:93
  139.8 16.3 %collective-permute-start.4 = (bf16[256,1152]{1,0:T(8,128)(2,1)S(1)}, bf16[256,1152]{1,0:T(8,128)(2,1)S(1)}, u32[]{:S(2)}, u32[]{:S(2)}) collective-permute-start(bf16[256,1152]{1,0:T(8,128)(2,1)S(1)} %collective-permute-done.3), channel_id=1, source_target_pairs={{0,1},{1,0},{2,3},{3,2},{4,5},{5,4},{6,7},{7,6},{8,9},{9,8},{10,11... | collective-permute-start | bytes 1769480 | tf_op jit(solution)/shard_map/ppermute | solution.py:93
  147.3 17.4 %collective-permute-start.6 = (bf16[256,1152]{1,0:T(8,128)(2,1)S(1)}, bf16[256,1152]{1,0:T(8,128)(2,1)S(1)}, u32[]{:S(2)}, u32[]{:S(2)}) collective-permute-start(bf16[256,1152]{1,0:T(8,128)(2,1)S(1)} %collective-permute-done.5), channel_id=1, source_target_pairs={{0,1},{1,0},{2,3},{3,2},{4,5},{5,4},{6,7},{7,6},{8,9},{9,8},{10,11... | collective-permute-start | bytes 1769480 | tf_op jit(solution)/shard_map/ppermute | solution.py:93
  249.1 4.5 collective-permute-start.14
  250.4 25.9 %collective-permute-start.18 = (bf16[256,2048]{1,0:T(8,128)(2,1)}, bf16[256,2048]{1,0:T(8,128)(2,1)}, u32[]{:S(2)}, u32[]{:S(2)}) collective-permute-start(bf16[256,2048]{1,0:T(8,128)(2,1)} %fusion.117), channel_id=1, source_target_pairs={{0,6},{2,0},{4,2},{6,4},{1,7},{3,1},{5,3},{7,5},{8,14},{10,8},{12,... | collective-permute-start | bytes 3145736 | tf_op jit(solution)/shard_map/ppermute | solution.py:93
  258.7 25.3 %collective-permute-start.15 = (bf16[256,2048]{1,0:T(8,128)(2,1)S(1)}, bf16[256,2048]{1,0:T(8,128)(2,1)S(1)}, u32[]{:S(2)}, u32[]{:S(2)}) collective-permute-start(bf16[256,2048]{1,0:T(8,128)(2,1)S(1)} %dynamic-slice_convert_fusion.1), channel_id=1, source_target_pairs={{0,16},{16,0},{1,17},{17,1},{2,18},{18,2},{3,19},{19,3},{4,20},{20... | collective-permute-start | bytes 3145736 | tf_op jit(solution)/shard_map/ppermute | solution.py:93
  276.3 28.3 %collective-permute-start.19 = (bf16[256,2048]{1,0:T(8,128)(2,1)}, bf16[256,2048]{1,0:T(8,128)(2,1)}, u32[]{:S(2)}, u32[]{:S(2)}) collective-permute-start(bf16[256,2048]{1,0:T(8,128)(2,1)} %collective-permute-done.18), channel_id=1, source_target_pairs={{0,6},{2,0},{4,2},{6,4},{1,7},{3,1},{5,3},{7,5},{8,14},{10,8},{12,... | collective-permute-start | bytes 3145736 | tf_op jit(solution)/shard_map/ppermute | solution.py:93
  300.0 27.0 %collective-permute-start.21 = (bf16[256,2048]{1,0:T(8,128)(2,1)S(1)}, bf16[256,2048]{1,0:T(8,128)(2,1)}, u32[]{:S(2)}, u32[]{:S(2)}) collective-permute-start(bf16[256,2048]{1,0:T(8,128)(2,1)S(1)} %multiply_convert_fusion.1), channel_id=1, source_target_pairs={{0,6},{2,0},{4,2},{6,4},{1,7},{3,1},{5,3},{7,5},{8,14},{10,8},{12,... | collective-permute-start | bytes 3145736 | tf_op jit(solution)/shard_map/ppermute | solution.py:93
  302.2 509.8 %reduce-scatter.11.cloned.1.call-start = ((), (), s32[]{:S(2)}) async-start(), calls=%async_computation.12 | async-start | bytes 3932160 | tf_op jit(solution)/shard_map/reduce_scatter | solution.py:344
  304.6 94.1 %collective-permute-start.20 = (bf16[256,2048]{1,0:T(8,128)(2,1)}, bf16[256,2048]{1,0:T(8,128)(2,1)}, u32[]{:S(2)}, u32[]{:S(2)}) collective-permute-start(bf16[256,2048]{1,0:T(8,128)(2,1)} %collective-permute-done.19), channel_id=1, source_target_pairs={{0,6},{2,0},{4,2},{6,4},{1,7},{3,1},{5,3},{7,5},{8,14},{10,8},{12,... | collective-permute-start | bytes 3145736 | tf_op jit(solution)/shard_map/ppermute | solution.py:93
  327.0 43.8 %collective-permute-start.22 = (bf16[256,2048]{1,0:T(8,128)(2,1)}, bf16[256,2048]{1,0:T(8,128)(2,1)}, u32[]{:S(2)}, u32[]{:S(2)}) collective-permute-start(bf16[256,2048]{1,0:T(8,128)(2,1)} %collective-permute-done.21), channel_id=1, source_target_pairs={{0,6},{2,0},{4,2},{6,4},{1,7},{3,1},{5,3},{7,5},{8,14},{10,8},{12,... | collective-permute-start | bytes 3145736 | tf_op jit(solution)/shard_map/ppermute | solution.py:93
  370.7 26.2 %collective-permute-start.23 = (bf16[256,2048]{1,0:T(8,128)(2,1)}, bf16[256,2048]{1,0:T(8,128)(2,1)S(1)}, u32[]{:S(2)}, u32[]{:S(2)}) collective-permute-start(bf16[256,2048]{1,0:T(8,128)(2,1)} %collective-permute-done.22), channel_id=1, source_target_pairs={{0,6},{2,0},{4,2},{6,4},{1,7},{3,1},{5,3},{7,5},{8,14},{10,8},{12,... | collective-permute-start | bytes 3145736 | tf_op jit(solution)/shard_map/ppermute | solution.py:93
  410.3 403.2 %reduce-scatter.7.cloned.1.call-start = ((), (), s32[]{:S(2)}) async-start(), calls=%async_computation.10 | async-start | bytes 7864320 | tf_op jit(solution)/shard_map/reduce_scatter | solution.py:339
  422.7 413.4 %reduce-scatter.9.cloned.1.call-start = ((), (), s32[]{:S(2)}) async-start(), calls=%async_computation.11 | async-start | bytes 3932160 | tf_op jit(solution)/shard_map/reduce_scatter | solution.py:344
  444.5 25.8 %collective-permute-start.24 = (bf16[256,2048]{1,0:T(8,128)(2,1)S(1)}, bf16[256,2048]{1,0:T(8,128)(2,1)S(1)}, u32[]{:S(2)}, u32[]{:S(2)}) collective-permute-start(bf16[256,2048]{1,0:T(8,128)(2,1)S(1)} %fusion.100), channel_id=1, source_target_pairs={{0,6},{2,0},{4,2},{6,4},{1,7},{3,1},{5,3},{7,5},{8,14},{10,8},{12,... | collective-permute-start | bytes 3145736 | tf_op jit(solution)/shard_map/ppermute | solution.py:93
  473.1 25.0 %collective-permute-start.25 = (bf16[256,2048]{1,0:T(8,128)(2,1)}, bf16[256,2048]{1,0:T(8,128)(2,1)}, u32[]{:S(2)}, u32[]{:S(2)}) collective-permute-start(bf16[256,2048]{1,0:T(8,128)(2,1)} %fusion.99), channel_id=1, source_target_pairs={{0,6},{2,0},{4,2},{6,4},{1,7},{3,1},{5,3},{7,5},{8,14},{10,8},{12,... | collective-permute-start | bytes 3145736 | tf_op jit(solution)/shard_map/ppermute | solution.py:93
  490.1 348.4 %reduce-scatter.5.cloned.1.call-start = ((), (), s32[]{:S(2)}) async-start(), calls=%async_computation.9 | async-start | bytes 7864320 | tf_op jit(solution)/shard_map/reduce_scatter | solution.py:339
  503.0 27.9 %collective-permute-start.26 = (bf16[256,2048]{1,0:T(8,128)(2,1)S(1)}, bf16[256,2048]{1,0:T(8,128)(2,1)S(1)}, u32[]{:S(2)}, u32[]{:S(2)}) collective-permute-start(bf16[256,2048]{1,0:T(8,128)(2,1)S(1)} %fusion.98), channel_id=1, source_target_pairs={{0,6},{2,0},{4,2},{6,4},{1,7},{3,1},{5,3},{7,5},{8,14},{10,8},{12,... | collective-permute-start | bytes 3145736 | tf_op jit(solution)/shard_map/ppermute | solution.py:93
  513.7 41.7 %collective-permute-start.54 = (bf16[256,2048]{1,0:T(8,128)(2,1)}, bf16[256,2048]{1,0:T(8,128)(2,1)}, u32[]{:S(2)}, u32[]{:S(2)}) collective-permute-start(bf16[256,2048]{1,0:T(8,128)(2,1)} %fusion.97), channel_id=1, source_target_pairs={{0,6},{2,0},{4,2},{6,4},{1,7},{3,1},{5,3},{7,5},{8,14},{10,8},{12,... | collective-permute-start | bytes 3145736 | tf_op jit(solution)/shard_map/ppermute | solution.py:93
  544.7 28.5 %collective-permute-start.28 = (bf16[256,2048]{1,0:T(8,128)(2,1)}, bf16[256,2048]{1,0:T(8,128)(2,1)}, u32[]{:S(2)}, u32[]{:S(2)}) collective-permute-start(bf16[256,2048]{1,0:T(8,128)(2,1)} %reshape.357), channel_id=1, source_target_pairs={{0,16},{16,0},{1,17},{17,1},{2,18},{18,2},{3,19},{19,3},{4,20},{20... | collective-permute-start | bytes 3145736 | tf_op jit(solution)/shard_map/ppermute | solution.py:93
  558.8 194.5 %collective-permute-start.55 = (bf16[256,2048]{1,0:T(8,128)(2,1)}, bf16[256,2048]{1,0:T(8,128)(2,1)}, u32[]{:S(2)}, u32[]{:S(2)}) collective-permute-start(bf16[256,2048]{1,0:T(8,128)(2,1)} %fusion.95), channel_id=1, source_target_pairs={{0,6},{2,0},{4,2},{6,4},{1,7},{3,1},{5,3},{7,5},{8,14},{10,8},{12,... | collective-permute-start | bytes 3145736 | tf_op jit(solution)/shard_map/ppermute | solution.py:93
  563.5 23.0 %collective-permute-start.27 = (bf16[256,2048]{1,0:T(8,128)(2,1)}, bf16[256,2048]{1,0:T(8,128)(2,1)S(1)}, u32[]{:S(2)}, u32[]{:S(2)}) collective-permute-start(bf16[256,2048]{1,0:T(8,128)(2,1)} %reshape.357), channel_id=1, source_target_pairs={{0,8},{8,0},{1,9},{9,1},{2,10},{10,2},{3,11},{11,3},{4,12},{12,4},... | collective-permute-start | bytes 3145736 | tf_op jit(solution)/shard_map/ppermute | solution.py:93
  573.2 14.9 %collective-permute-start.29 = (bf16[256,2048]{1,0:T(8,128)(2,1)}, bf16[256,2048]{1,0:T(8,128)(2,1)S(1)}, u32[]{:S(2)}, u32[]{:S(2)}) collective-permute-start(bf16[256,2048]{1,0:T(8,128)(2,1)} %collective-permute-done.28), channel_id=1, source_target_pairs={{0,8},{8,0},{1,9},{9,1},{2,10},{10,2},{3,11},{11,3},{4,12},{12,4},... | collective-permute-start | bytes 3145736 | tf_op jit(solution)/shard_map/ppermute | solution.py:93
  597.1 115.4 %collective-permute-start.42 = (bf16[512,256]{1,0:T(8,128)(2,1)}, bf16[512,256]{1,0:T(8,128)(2,1)}, u32[]{:S(2)}, u32[]{:S(2)}) collective-permute-start(bf16[512,256]{1,0:T(8,128)(2,1)} %get-tuple-element.709), channel_id=1, source_target_pairs={{0,1},{1,0},{2,3},{3,2},{4,5},{5,4},{6,7},{7,6},{8,9},{9,8},{10,11... | collective-permute-start | bytes 786440 | tf_op jit(solution)/shard_map/ppermute | solution.py:93
  598.7 124.8 %collective-permute-start.41 = (bf16[512,256]{1,0:T(8,128)(2,1)}, bf16[512,256]{1,0:T(8,128)(2,1)}, u32[]{:S(2)}, u32[]{:S(2)}) collective-permute-start(bf16[512,256]{1,0:T(8,128)(2,1)} %get-tuple-element.710), channel_id=1, source_target_pairs={{0,1},{1,0},{2,3},{3,2},{4,5},{5,4},{6,7},{7,6},{8,9},{9,8},{10,11... | collective-permute-start | bytes 786440 | tf_op jit(solution)/shard_map/ppermute | solution.py:93
  599.3 129.9 %collective-permute-start.40 = (bf16[512,256]{1,0:T(8,128)(2,1)}, bf16[512,256]{1,0:T(8,128)(2,1)}, u32[]{:S(2)}, u32[]{:S(2)}) collective-permute-start(bf16[512,256]{1,0:T(8,128)(2,1)} %get-tuple-element.711), channel_id=1, source_target_pairs={{0,1},{1,0},{2,3},{3,2},{4,5},{5,4},{6,7},{7,6},{8,9},{9,8},{10,11... | collective-permute-start | bytes 786440 | tf_op jit(solution)/shard_map/ppermute | solution.py:93
  701.1 25.2 %collective-permute-start.35 = (bf16[256,1152]{0,1:T(8,128)(2,1)S(1)}, bf16[256,1152]{0,1:T(8,128)(2,1)S(1)}, u32[]{:S(2)}, u32[]{:S(2)}) collective-permute-start(bf16[256,1152]{0,1:T(8,128)(2,1)S(1)} %get-tuple-element.679), channel_id=1, source_target_pairs={{0,1},{1,0},{2,3},{3,2},{4,5},{5,4},{6,7},{7,6},{8,9},{9,8},{10,11... | collective-permute-start | bytes 1769480 | tf_op jit(solution)/shard_map/ppermute | solution.py:93
  713.7 11.3 %collective-permute-start.43 = (bf16[512,256]{1,0:T(8,128)(2,1)S(1)}, bf16[512,256]{1,0:T(8,128)(2,1)S(1)}, u32[]{:S(2)}, u32[]{:S(2)}) collective-permute-start(bf16[512,256]{1,0:T(8,128)(2,1)S(1)} %fusion.180), channel_id=1, source_target_pairs={{0,6},{2,0},{4,2},{6,4},{1,7},{3,1},{5,3},{7,5},{8,14},{10,8},{12,... | collective-permute-start | bytes 786440 | tf_op jit(solution)/shard_map/ppermute | solution.py:93
  723.5 15.2 %collective-permute-start.34 = (bf16[256,1152]{0,1:T(8,128)(2,1)}, bf16[256,1152]{0,1:T(8,128)(2,1)S(1)}, u32[]{:S(2)}, u32[]{:S(2)}) collective-permute-start(bf16[256,1152]{0,1:T(8,128)(2,1)} %get-tuple-element.680), channel_id=1, source_target_pairs={{0,1},{1,0},{2,3},{3,2},{4,5},{5,4},{6,7},{7,6},{8,9},{9,8},{10,11... | collective-permute-start | bytes 1769480 | tf_op jit(solution)/shard_map/ppermute | solution.py:93
  725.0 51.8 %collective-permute-start.30 = (bf16[512,2048]{1,0:T(8,128)(2,1)}, bf16[512,2048]{1,0:T(8,128)(2,1)}, u32[]{:S(2)}, u32[]{:S(2)}) collective-permute-start(bf16[512,2048]{1,0:T(8,128)(2,1)} %convolution_convert_fusion.4), channel_id=1, source_target_pairs={{0,8},{8,0},{1,9},{9,1},{2,10},{10,2},{3,11},{11,3},{4,12},{12,4},... | collective-permute-start | bytes 6291464 | tf_op jit(solution)/shard_map/ppermute | solution.py:175
  726.2 9.2 collective-permute-start.44
  729.2 18.5 %collective-permute-start.36 = (bf16[256,1152]{0,1:T(8,128)(2,1)S(1)}, bf16[256,1152]{0,1:T(8,128)(2,1)S(1)}, u32[]{:S(2)}, u32[]{:S(2)}) collective-permute-start(bf16[256,1152]{0,1:T(8,128)(2,1)S(1)} %fusion.135), channel_id=1, source_target_pairs={{0,6},{2,0},{4,2},{6,4},{1,7},{3,1},{5,3},{7,5},{8,14},{10,8},{12,... | collective-permute-start | bytes 1769480 | tf_op jit(solution)/shard_map/ppermute | solution.py:93
  735.4 27.3 %collective-permute-start.39 = (bf16[512,256]{1,0:T(8,128)(2,1)}, bf16[512,256]{1,0:T(8,128)(2,1)S(1)}, u32[]{:S(2)}, u32[]{:S(2)}) collective-permute-start(bf16[512,256]{1,0:T(8,128)(2,1)} %get-tuple-element.708), channel_id=1, source_target_pairs={{0,1},{1,0},{2,3},{3,2},{4,5},{5,4},{6,7},{7,6},{8,9},{9,8},{10,11... | collective-permute-start | bytes 786440 | tf_op jit(solution)/shard_map/ppermute | solution.py:93
  738.7 27.4 %collective-permute-start.33 = (bf16[256,1152]{0,1:T(8,128)(2,1)}, bf16[256,1152]{0,1:T(8,128)(2,1)}, u32[]{:S(2)}, u32[]{:S(2)}) collective-permute-start(bf16[256,1152]{0,1:T(8,128)(2,1)} %get-tuple-element.681), channel_id=1, source_target_pairs={{0,1},{1,0},{2,3},{3,2},{4,5},{5,4},{6,7},{7,6},{8,9},{9,8},{10,11... | collective-permute-start | bytes 1769480 | tf_op jit(solution)/shard_map/ppermute | solution.py:93
  747.7 15.1 %collective-permute-start.45 = (bf16[512,256]{1,0:T(8,128)(2,1)}, bf16[512,256]{1,0:T(8,128)(2,1)}, u32[]{:S(2)}, u32[]{:S(2)}) collective-permute-start(bf16[512,256]{1,0:T(8,128)(2,1)} %fusion.184), channel_id=1, source_target_pairs={{0,6},{2,0},{4,2},{6,4},{1,7},{3,1},{5,3},{7,5},{8,14},{10,8},{12,... | collective-permute-start | bytes 786440 | tf_op jit(solution)/shard_map/ppermute | solution.py:93
  753.3 17.3 %collective-permute-start.37 = (bf16[256,1152]{0,1:T(8,128)(2,1)}, bf16[256,1152]{0,1:T(8,128)(2,1)}, u32[]{:S(2)}, u32[]{:S(2)}) collective-permute-start(bf16[256,1152]{0,1:T(8,128)(2,1)} %fusion.137), channel_id=1, source_target_pairs={{0,6},{2,0},{4,2},{6,4},{1,7},{3,1},{5,3},{7,5},{8,14},{10,8},{12,... | collective-permute-start | bytes 1769480 | tf_op jit(solution)/shard_map/ppermute | solution.py:93
  762.7 131.9 %collective-permute-start.56 = (bf16[256,2048]{1,0:T(8,128)(2,1)}, bf16[256,2048]{1,0:T(8,128)(2,1)}, u32[]{:S(2)}, u32[]{:S(2)}) collective-permute-start(bf16[256,2048]{1,0:T(8,128)(2,1)} %fusion.96), channel_id=1, source_target_pairs={{0,6},{2,0},{4,2},{6,4},{1,7},{3,1},{5,3},{7,5},{8,14},{10,8},{12,... | collective-permute-start | bytes 3145736 | tf_op jit(solution)/shard_map/ppermute | solution.py:93
  762.8 21.9 %collective-permute-start.32 = (bf16[256,1152]{0,1:T(8,128)(2,1)}, bf16[256,1152]{0,1:T(8,128)(2,1)S(1)}, u32[]{:S(2)}, u32[]{:S(2)}) collective-permute-start(bf16[256,1152]{0,1:T(8,128)(2,1)} %get-tuple-element.678), channel_id=1, source_target_pairs={{0,1},{1,0},{2,3},{3,2},{4,5},{5,4},{6,7},{7,6},{8,9},{9,8},{10,11... | collective-permute-start | bytes 1769480 | tf_op jit(solution)/shard_map/ppermute | solution.py:93
  772.4 31.9 %collective-permute-start.38 = (bf16[256,1152]{0,1:T(8,128)(2,1)S(1)}, bf16[256,1152]{0,1:T(8,128)(2,1)S(1)}, u32[]{:S(2)}, u32[]{:S(2)}) collective-permute-start(bf16[256,1152]{0,1:T(8,128)(2,1)S(1)} %fusion.139), channel_id=1, source_target_pairs={{0,6},{2,0},{4,2},{6,4},{1,7},{3,1},{5,3},{7,5},{8,14},{10,8},{12,... | collective-permute-start | bytes 1769480 | tf_op jit(solution)/shard_map/ppermute | solution.py:93
  784.1 30.0 %collective-permute-start.31 = (bf16[256,2048]{1,0:T(8,128)(2,1)}, bf16[256,2048]{1,0:T(8,128)(2,1)}, u32[]{:S(2)}, u32[]{:S(2)}) collective-permute-start(bf16[256,2048]{1,0:T(8,128)(2,1)} %dynamic-slice_convert_fusion), channel_id=1, source_target_pairs={{0,16},{16,0},{1,17},{17,1},{2,18},{18,2},{3,19},{19,3},{4,20},{20... | collective-permute-start | bytes 3145736 | tf_op jit(solution)/shard_map/ppermute | solution.py:93
  812.0 24.1 %collective-permute-start.47 = (bf16[768,512]{1,0:T(8,128)(2,1)}, bf16[768,512]{1,0:T(8,128)(2,1)}, u32[]{:S(2)}, u32[]{:S(2)}) collective-permute-start(bf16[768,512]{1,0:T(8,128)(2,1)} %reduce-scatter.11.cloned.1.call-done), channel_id=1, source_target_pairs={{0,1},{1,0},{2,3},{3,2},{4,5},{5,4},{6,7},{7,6},{8,9},{9,8},{10,11... | collective-permute-start | bytes 2359304 | tf_op jit(solution)/shard_map/ppermute | solution.py:93
  813.5 50.9 %collective-permute-start.46 = (bf16[512,1536]{1,0:T(8,128)(2,1)}, bf16[512,1536]{1,0:T(8,128)(2,1)}, u32[]{:S(2)}, u32[]{:S(2)}) collective-permute-start(bf16[512,1536]{1,0:T(8,128)(2,1)} %reduce-scatter.7.cloned.1.call-done), channel_id=1, source_target_pairs={{0,1},{1,0},{2,3},{3,2},{4,5},{5,4},{6,7},{7,6},{8,9},{9,8},{10,11... | collective-permute-start | bytes 4718600 | tf_op jit(solution)/shard_map/ppermute | solution.py:93
  872.6 12.7 %collective-permute-start.49 = (f32[4353]{0:T(1024)S(1)}, f32[4353]{0:T(1024)S(1)}, u32[]{:S(2)}, u32[]{:S(2)}) collective-permute-start(f32[4353]{0:T(1024)S(1)} %add.595), channel_id=1, source_target_pairs={{0,16},{16,0},{1,17},{17,1},{2,18},{18,2},{3,19},{19,3},{4,20},{20... | collective-permute-start | bytes 52244 | tf_op jit(solution)/shard_map/ppermute | solution.py:93
  885.4 4.6 collective-permute-start.50
  890.0 8.0 collective-permute-start.51
  901.8 5.9 collective-permute-start.53
  (172 other events, 2089.3 us)
Sparse Core Ops, SparseCore 0:
  22.6 37.1 all-gather.5
  61.4 47.1 all-gather.13
  110.7 28.5 all-gather.11
  141.2 46.3 all-gather.9
  302.4 26.2 all-gather.7
  410.4 39.3 reduce-scatter.10
  452.4 58.3 reduce-scatter.6
  513.9 46.5 reduce-scatter.8
  584.8 58.5 reduce-scatter.4

commit v2 on v1

v2 whole, which is shorter than its diff:
```python
import functools

import jax
import jax.numpy as jnp
from jax import lax
from jax.experimental import pallas as pl
from jax.experimental.layout import Layout, with_layout_constraint
from jax.experimental.pallas import tpu as pltpu
from jax.sharding import Mesh
from jax.sharding import PartitionSpec as P

D = 2048
H = 16
HD = 128
KVH = 8
NDOM = 8
STEP = 10


NORM_EPS = 1e-06
ROPE_BASE = 1000000.0
MASK_FILL = -1e30
CLIP_NORM = 1.0
WEIGHT_RATE = 0.02
OUTPUT_RATE = 0.12
GAIN_RATE = 0.7
BETA_FIRST = 0.9
BETA_SECOND = 0.95
ADAM_EPS = 1e-08
WEIGHT_DECAY = 0.1
LOG2E = 1.4426950408889634


def rms_scale(values):
    return values * lax.rsqrt(jnp.mean(values * values, -1, keepdims=True) + NORM_EPS)


def norm_rows(values, gain):
    return rms_scale(values) * gain


def positions(segments):
    length = segments.shape[0]
    places = jnp.arange(length, dtype=jnp.int32)
    starts = jnp.concatenate([jnp.ones((1,), dtype=bool), segments[1:] != segments[:-1]])
    return places - lax.cummax(jnp.where(starts, places, 0), axis=0)


def contract_rows(left, right):
    return lax.dot_general(
        left, right, (((0,), (0,)), ((), ())), preferred_element_type=jnp.float32
    )


def contract_cols(left, right):
    return lax.dot_general(
        left, right, (((1,), (1,)), ((), ())), preferred_element_type=jnp.float32
    )


def swiglu_back(activation_grad, gate_pre, up_pre):
    gate_sigmoid = jax.nn.sigmoid(gate_pre)
    gate_grad = (
        activation_grad * up_pre * gate_sigmoid * (1.0 + gate_pre * (1.0 - gate_sigmoid))
    ).astype(jnp.bfloat16)
    up_grad = (activation_grad * gate_pre * gate_sigmoid).astype(jnp.bfloat16)
    return (gate_grad, up_grad)


def adam_step(weight, grad, first, second, rate, decay):
    first_new = BETA_FIRST * first + (1.0 - BETA_FIRST) * grad
    second_new = BETA_SECOND * second + (1.0 - BETA_SECOND) * grad * grad
    first_hat = first_new / (1.0 - BETA_FIRST**STEP)
    second_hat = second_new / (1.0 - BETA_SECOND**STEP)
    updated = weight - rate * (first_hat / (jnp.sqrt(second_hat) + ADAM_EPS) + decay * weight)
    return (updated, first_new, second_new)


def turn(values, cosine, sine):
    return values * cosine + pltpu.roll(values, HD // 2, 1) * sine


def dot_cols(left, right):
    return lax.dot_general(
        left, right, (((1,), (1,)), ((), ())), preferred_element_type=jnp.float32
    )


def dot_rows(left, right):
    return lax.dot_general(
        left, right, (((0,), (0,)), ((), ())), preferred_element_type=jnp.float32
    )


def allowed_keys(start, first, block, length, repeat):
    keys = lax.broadcasted_iota(jnp.int32, (block, length), 1)
    queries = first + lax.broadcasted_iota(jnp.int32, (block, length), 0)
    allowed = (keys >= start) & (keys <= queries)
    return jnp.concatenate([allowed] * repeat, 0)


def attend_kernel(
    heads,
    groups,
    block,
    slots,
    raw,
    start,
    cosine,
    sine,
    gain,
    query,
    key,
    value,
    attended,
    total_log,
    gated,
    gated_near,
):
    length = raw.shape[0]
    repeat = heads // groups
    key_from, value_from, gate_from = heads * HD, (heads + groups) * HD, (heads + 2 * groups) * HD
    cos, sin = cosine[...], sine[...]

    def prepared(column, gain_row):
        part = raw[:, column : column + HD]
        scale = lax.rsqrt(jnp.mean(part * part, -1, keepdims=True) + NORM_EPS)
        return turn(part * scale * gain_row, cos, sin).astype(jnp.bfloat16)

    for g in range(groups):
        key[:, g * HD : (g + 1) * HD] = prepared(key_from + g * HD, gain[1:2, :])
        value[:, g * HD : (g + 1) * HD] = raw[
            :, value_from + g * HD : value_from + (g + 1) * HD
        ].astype(jnp.bfloat16)
    for h in range(heads):
        query[:, h * HD : (h + 1) * HD] = prepared(h * HD, gain[0:1, :])
    total_log[...] = jnp.zeros(total_log.shape, jnp.float32)
    for i in range(length // block):
        rows = slice(i * block, (i + 1) * block)
        near = pl.ds(pl.multiple_of(slots[i] * block, block), block)
        seen = (i + 1) * block
        mask = allowed_keys(start[rows, :], i * block, block, seen, repeat)
        for g in range(groups):
            columns = slice(g * HD, (g + 1) * HD)
            hs = range(g * repeat, (g + 1) * repeat)
            queries = jnp.concatenate([query[rows, h * HD : (h + 1) * HD] for h in hs], 0)
            scores = dot_cols(queries, key[:seen, columns]) * (HD**-0.5 * LOG2E)
            scores = jnp.where(mask, scores, MASK_FILL)
            largest = jnp.max(scores, -1, keepdims=True)
            exponent = jnp.exp2(scores - largest)
            total = jnp.sum(exponent, -1, keepdims=True)
            result = jnp.dot(
                exponent.astype(jnp.bfloat16), value[:seen, columns], preferred_element_type=jnp.float32
            ) / total
            logs = largest + jnp.log2(total)
            for r, h in enumerate(hs):
                part = result[r * block : (r + 1) * block, :]
                gate = jax.nn.sigmoid(raw[rows, gate_from + h : gate_from + h + 1])
                attended[rows, h * HD : (h + 1) * HD] = part
                part_low = (part * gate).astype(jnp.bfloat16)
                gated[rows, h * HD : (h + 1) * HD] = part_low
                gated_near[near, h * HD : (h + 1) * HD] = part_low
                total_log[rows, h : h + 1] = logs[r * block : (r + 1) * block, :]


def in_vmem(count):
    return [pl.BlockSpec(memory_space=pltpu.SMEM)] + [pl.BlockSpec(memory_space=pltpu.VMEM)] * count


def attend(slots, raw, start, cosine, sine, gain, heads, groups):
    length = raw.shape[0]
    low = jnp.bfloat16
    return pl.pallas_call(
        functools.partial(attend_kernel, heads, groups, length // slots.shape[0]),
        in_specs=in_vmem(5),
        out_shape=(
            jax.ShapeDtypeStruct((length, heads * HD), low),
            jax.ShapeDtypeStruct((length, groups * HD), low),
            jax.ShapeDtypeStruct((length, groups * HD), low),
            jax.ShapeDtypeStruct((length, heads * HD), jnp.float32),
            jax.ShapeDtypeStruct((length, HD), jnp.float32),
            jax.ShapeDtypeStruct((length, heads * HD), low),
            jax.ShapeDtypeStruct((length, heads * HD), low),
        ),
        compiler_params=pltpu.CompilerParams(vmem_limit_bytes=56 * 2**20),
        cost_estimate=pl.CostEstimate(
            flops=4 * heads * length * length * HD,
            bytes_accessed=raw.size * 4 + length * heads * HD * 10,
            transcendentals=heads * length * length,
        ),
    )(slots, raw, start, cosine, sine, gain)


def attend_back_kernel(
    heads,
    groups,
    block,
    slots,
    gated_grad,
    raw,
    start,
    cosine,
    sine,
    gain,
    query,
    key,
    value,
    attended,
    total_log,
    grads,
    grads_near,
    gain_grads,
    low_grad,
    delta,
    query_sum,
    key_sum,
    value_sum,
):
    length = raw.shape[0]
    repeat = heads // groups
    key_from, value_from, gate_from = heads * HD, (heads + groups) * HD, (heads + 2 * groups) * HD
    cos, sin = cosine[...], sine[...]
    scale = HD**-0.5
    nears = [
        pl.ds(pl.multiple_of(slots[i] * block, block), block) for i in range(length // block)
    ]

    def unprepared(grad, column, gain_row):
        part = raw[:, column : column + HD]
        inverse = lax.rsqrt(jnp.mean(part * part, -1, keepdims=True) + NORM_EPS)
        unit = part * inverse
        back = grad * cos - pltpu.roll(grad, HD // 2, 1) * sin
        inner = back * gain_row
        mean = jnp.mean(inner * unit, -1, keepdims=True)
        result = inverse * (inner - unit * mean)
        return result.astype(jnp.bfloat16), jnp.sum(back * unit, 0, keepdims=True)

    grads[:, gate_from:] = jnp.zeros((length, grads.shape[1] - gate_from), jnp.bfloat16)
    for h in range(heads):
        columns = slice(h * HD, (h + 1) * HD)
        gate = jax.nn.sigmoid(raw[:, gate_from + h : gate_from + h + 1])
        outer = jnp.concatenate([gated_grad[near, columns] for near in nears], 0)
        result = attended[:, columns]
        low = (outer * gate).astype(jnp.bfloat16)
        low_grad[:, columns] = low
        logit = jnp.sum(outer * result, -1, keepdims=True) * gate * (1.0 - gate)
        grads[:, gate_from + h : gate_from + h + 1] = logit.astype(jnp.bfloat16)
        delta[:, h : h + 1] = jnp.sum(low.astype(jnp.float32) * result, -1, keepdims=True)
    key_sum[...] = jnp.zeros(key_sum.shape, jnp.float32)
    value_sum[...] = jnp.zeros(value_sum.shape, jnp.float32)
    for i in range(length // block):
        rows = slice(i * block, (i + 1) * block)
        seen = (i + 1) * block
        mask = allowed_keys(start[rows, :], i * block, block, seen, repeat)
        for g in range(groups):
            columns = slice(g * HD, (g + 1) * HD)
            hs = range(g * repeat, (g + 1) * repeat)
            queries = jnp.concatenate([query[rows, h * HD : (h + 1) * HD] for h in hs], 0)
            outers = jnp.concatenate([low_grad[rows, h * HD : (h + 1) * HD] for h in hs], 0)
            logs = jnp.concatenate([total_log[rows, h : h + 1] for h in hs], 0)
            deltas = jnp.concatenate([delta[rows, h : h + 1] for h in hs], 0)
            keys, values = key[:seen, columns], value[:seen, columns]
            scores = dot_cols(queries, keys) * (scale * LOG2E)
            probs = jnp.exp2(jnp.where(mask, scores - logs, MASK_FILL))
            prob_grad = dot_cols(outers, values)
            score_grad = (probs * (prob_grad - deltas)).astype(jnp.bfloat16)
            moved = jnp.dot(score_grad, keys, preferred_element_type=jnp.float32) * scale
            for r, h in enumerate(hs):
                query_sum[rows, h * HD : (h + 1) * HD] = moved[r * block : (r + 1) * block, :]
            key_sum[:seen, columns] += dot_rows(score_grad, queries)
            value_sum[:seen, columns] += dot_rows(probs.astype(jnp.bfloat16), outers)
    gain_grads[...] = jnp.zeros(gain_grads.shape, jnp.float32)
    for h in range(heads):
        part, gain_part = unprepared(query_sum[:, h * HD : (h + 1) * HD], h * HD, gain[0:1, :])
        grads[:, h * HD : (h + 1) * HD] = part
        gain_grads[0:1, :] += gain_part
    for g in range(groups):
        columns = slice(g * HD, (g + 1) * HD)
        part, gain_part = unprepared(
            key_sum[:, columns] * scale, key_from + g * HD, gain[1:2, :]
        )
        grads[:, key_from + g * HD : key_from + (g + 1) * HD] = part
        gain_grads[1:2, :] += gain_part
        grads[:, value_from + g * HD : value_from + (g + 1) * HD] = value_sum[:, columns].astype(
            jnp.bfloat16
        )
    for i, near in enumerate(nears):
        grads_near[near, :] = grads[i * block : (i + 1) * block, :]


def attend_back(slots, gated_grad, raw, start, cosine, sine, gain, saved, heads, groups):
    length = raw.shape[0]
    query, key, value, attended, total_log = saved
    return pl.pallas_call(
        functools.partial(attend_back_kernel, heads, groups, length // slots.shape[0]),
        in_specs=in_vmem(11),
        out_shape=(
            jax.ShapeDtypeStruct(raw.shape, jnp.bfloat16),
            jax.ShapeDtypeStruct(raw.shape, jnp.bfloat16),
            jax.ShapeDtypeStruct((2, HD), jnp.float32),
        ),
        scratch_shapes=[
            pltpu.VMEM((length, heads * HD), jnp.bfloat16),
            pltpu.VMEM((length, HD), jnp.float32),
            pltpu.VMEM((length, heads * HD), jnp.float32),
            pltpu.VMEM((length, groups * HD), jnp.float32),
            pltpu.VMEM((length, groups * HD), jnp.float32),
        ],
        compiler_params=pltpu.CompilerParams(vmem_limit_bytes=56 * 2**20),
        cost_estimate=pl.CostEstimate(
            flops=10 * heads * length * length * HD,
            bytes_accessed=raw.size * 6 + length * heads * HD * 12,
            transcendentals=heads * length * length,
        ),
    )(slots, gated_grad, raw, start, cosine, sine, gain, query, key, value, attended, total_log)


def rope_tables(places):
    half = HD // 2
    freqs = ROPE_BASE ** (-2.0 * jnp.arange(half, dtype=jnp.float32) / HD)
    angles = places.astype(jnp.float32)[:, None] * freqs[None, :]
    cosine, sine = jnp.cos(angles), jnp.sin(angles)
    return jnp.concatenate([cosine, cosine], 1), jnp.concatenate([-sine, sine], 1)


def tie(*values):
    return lax.optimization_barrier(values)


TEAM = 4


def swapped(value, axis, flip):
    size = lax.axis_size(axis)
    return lax.ppermute(value, axis, [(i, i ^ flip) for i in range(size)])


def hop(value, axis):
    size = lax.axis_size(axis)
    return lax.ppermute(value, axis, [(i, (i - 1) % size) for i in range(size)])


def ring_gather(value, axis):
    pieces = [value]
    for _ in range(lax.axis_size(axis) - 1):
        pieces.append(hop(pieces[-1], axis))
    return pieces


def ring_scatter(parts, axis):
    size = lax.axis_size(axis)
    total = parts[1 % size]
    for step in range(1, size):
        total = parts[(step + 1) % size] + hop(total.astype(jnp.bfloat16), axis).astype(jnp.float32)
    return total


def wide_shape():
    size = lax.axis_size("w")
    return TEAM, size // TEAM


def wide_from(value, outer_step, inner_step):
    outer, inner = wide_shape()
    pairs = []
    for a in range(outer):
        for b in range(inner):
            source = (a + outer_step) % outer * inner + (b + inner_step) % inner
            pairs.append((source, a * inner + b))
    return lax.ppermute(value, "w", pairs)


def inner_gather(value):
    pieces = [value]
    for _ in range(wide_shape()[1] - 1):
        pieces.append(wide_from(pieces[-1], 0, 1))
    return pieces


def inner_scatter(parts):
    size = wide_shape()[1]
    total = parts[1 % size]
    for step in range(1, size):
        moved = wide_from(total.astype(jnp.bfloat16), 0, 1)
        total = parts[(step + 1) % size] + moved.astype(jnp.float32)
    return total


def wide_slots():
    outer, inner = wide_shape()
    me = lax.axis_index("w")
    a_me, b_me = me // inner, lax.rem(me, inner)
    return [
        [lax.rem(a_me + i, outer) * inner + lax.rem(b_me + j, inner) for j in range(inner)]
        for i in range(outer)
    ]


def outer_shift(value, step):
    return wide_from(value, step, 0)


def all_sum(value, axis):
    size = lax.axis_size(axis)
    if size & (size - 1):
        return lax.psum(value, axis)
    step = 1
    while step < size:
        value = value + swapped(value, axis, step)
        step = 2 * step
    return value


def assemble(pieces, axis):
    first = pieces[0][0]
    size = first.shape[axis]
    shape = list(first.shape)
    shape[axis] = size * len(pieces) * len(pieces[0])
    result = jnp.zeros(shape, first.dtype)
    for row, slots in zip(pieces, wide_slots()):
        for piece, slot in zip(row, slots):
            result = lax.dynamic_update_slice_in_dim(result, piece, slot * size, axis)
    return result


def near_slots():
    x_size = lax.axis_size("x")
    x_me, c_me = lax.axis_index("x"), lax.axis_index("c")
    return jnp.stack(
        [
            (core ^ c_me) * x_size + lax.rem(x + x_size - x_me, x_size)
            for x in range(x_size)
            for core in range(2)
        ]
    ).astype(jnp.int32)


def pinned(values):
    return with_layout_constraint(values, Layout(tuple(range(values.ndim))))


def by_x(total):
    x_size = lax.axis_size("x")
    rows = total.shape[0] // x_size
    return [total[i * rows : (i + 1) * rows] for i in range(x_size)]


def body(
    tokens,
    cotangent,
    segment_ids,
    domain_ids,
    domain_weights,
    gains,
    gain_first,
    gain_second,
    query_weight,
    query_first,
    query_second,
    keyvalue_weight,
    keyvalue_first,
    keyvalue_second,
    headgate_weight,
    headgate_first,
    headgate_second,
    output_weight,
    output_first,
    output_second,
    expand_weight,
    expand_first,
    expand_second,
    reduce_weight,
    reduce_first,
    reduce_second,
):
    head_devices = lax.axis_size("x") * lax.axis_size("c")
    core = lax.axis_index("c")
    outer, inner = wide_shape()
    heads = H // head_devices
    groups = KVH // head_devices
    low = jnp.bfloat16
    wide = jnp.float32
    labels = jnp.arange(NDOM, dtype=jnp.int32)
    onehot = domain_ids[:, None] == labels[None, :]
    token_weight = jnp.sum(jnp.where(onehot, domain_weights[None, :], 0.0), -1)
    upstream = cotangent.astype(wide) * token_weight[:, None]
    norm_one = gains[:D]
    norm_two = gains[D : 2 * D]
    head_gains = gains[2 * D :].reshape(2, HD)
    inputs = tokens.astype(wide)
    normed = norm_rows(inputs, norm_one).astype(low)
    depth = query_weight.shape[0]
    query_width, key_width = query_weight.shape[1], keyvalue_weight.shape[2]
    value_from = query_width + key_width
    gate_from = value_from + key_width
    project = jnp.concatenate(
        [
            query_weight,
            keyvalue_weight[0],
            keyvalue_weight[1],
            headgate_weight,
            jnp.zeros((depth, -heads % 128), wide),
        ],
        1,
    ).astype(low)
    group_in = lax.all_gather(normed, ("x", "c"), axis=0, tiled=True)
    output_low = output_weight.astype(low)
    upstream_low = upstream.astype(low)
    expand_low = jnp.concatenate([expand_weight[0], expand_weight[1]], 1).astype(low)
    reduce_low = reduce_weight.astype(low)
    hidden = reduce_low.shape[0]

    def expand_whole(piece):
        return lax.all_gather(piece, ("x", "c"), axis=0, tiled=True)

    def reduce_whole(piece):
        return lax.all_gather(piece, ("x", "c"), axis=1, tiled=True)

    expand_all = [expand_whole(expand_low)]
    reduce_all = [reduce_whole(reduce_low)]

    group_size = group_in.shape[0]
    places = positions(segment_ids)
    starts = (jnp.arange(group_size, dtype=jnp.int32) - places)[:, None]
    cosine, sine = rope_tables(places)

    near = near_slots()
    x_size = lax.axis_size("x")

    row = project
    project_pieces = []
    for _ in range(outer - 1):
        moved, across, starts, cosine, sine = tie(
            wide_from(row, 1, 0), inner_gather(row), starts, cosine, sine
        )
        project_pieces.append(across)
        row = moved
    row, output_low, upstream_low = tie(row, output_low, upstream_low)
    output_rows = [output_low] + [wide_from(output_low, i, 0) for i in range(1, outer)]
    sides = [expand_low[:, :hidden], expand_low[:, hidden:]]
    across, output_rows, upstream_low, sides = tie(
        inner_gather(row), output_rows, upstream_low, sides
    )
    project_pieces.append(across)
    output_pieces = [inner_gather(piece) for piece in output_rows]
    upstream_parts = [upstream_low, outer_shift(upstream_low, 1)]
    project_all = assemble(project_pieces, 0)
    raw = jnp.dot(group_in, project_all, preferred_element_type=wide)
    raw, output_pieces, upstream_parts, sides = tie(raw, output_pieces, upstream_parts, sides)
    gate_pieces = inner_gather(sides[0])
    upstream_parts.append(outer_shift(upstream_parts[-1], 1))
    output_all = assemble(output_pieces, 1)
    kept = attend(near, raw, starts, cosine, sine, head_gains, heads, groups)
    kept, output_all, upstream_parts, gate_pieces, sides = tie(
        kept, output_all, upstream_parts, gate_pieces, sides
    )
    up_pieces = inner_gather(sides[1])
    upstream_parts.append(outer_shift(upstream_parts[-1], 1))
    query, key, value, attended, total_log, gated, gated_near = kept
    half = gated.shape[0] // 2

    def projected(rows):
        return jnp.dot(rows, output_all, preferred_element_type=wide)

    received = swapped(projected(gated_near[half:]).astype(low), "c", 1)
    attention = projected(gated_near[:half]) + received.astype(wide)
    attention = by_x(attention)
    split = attention[0].shape[0] // 2
    first = ring_scatter([part[:split] for part in attention], "x")
    second = ring_scatter([part[split:] for part in attention], "x")
    first, up_pieces, reduce_low, upstream_parts = tie(
        first, up_pieces, reduce_low, upstream_parts
    )
    expand_all = expand_all + [
        expand_whole(jnp.concatenate(pair, 1)) for pair in zip(gate_pieces[1:], up_pieces[1:])
    ]
    reduce_pieces = inner_gather(reduce_low)
    attention = jnp.concatenate([first, second], 0)
    residual = inputs + attention
    mixed = norm_rows(residual, norm_two).astype(low)

    def hidden_part(k, j):
        both = jnp.dot(mixed_parts[k], expand_all[j], preferred_element_type=wide)
        gate_pre, up_pre = both[:, :hidden], both[:, hidden:]
        activation = (jax.nn.silu(gate_pre) * up_pre).astype(low)
        activation_grad = contract_cols(upstream_parts[k], reduce_all[j])
        return activation, jnp.concatenate(swiglu_back(activation_grad, gate_pre, up_pre), 1)

    def mixed_back(parts, j):
        return contract_cols(parts[1], expand_all[j])

    def lowered(parts, j):
        return jnp.dot(parts[0], reduce_all[j], preferred_element_type=wide)

    done = {}
    grad_sums = {}
    output_sums = {}

    def begin(k):
        done[k, 0] = hidden_part(k, 0)
        grad_sums[k] = mixed_back(done[k, 0], 0)
        output_sums[k] = lowered(done[k, 0], 0)

    def rest(k):
        for j in range(1, inner):
            done[k, j] = hidden_part(k, j)
            grad_sums[k] = grad_sums[k] + mixed_back(done[k, j], j)

    def joined(which, j):
        return jnp.concatenate([done[k, j][which] for k in range(outer)], 0)

    def expand_back(j):
        return lax.psum_scatter(
            contract_rows(mixed_all, joined(1, j)).astype(low),
            ("x", "c"),
            scatter_dimension=0,
            tiled=True,
        )

    def reduce_back(j):
        return lax.psum_scatter(
            contract_rows(joined(0, j), upstream_all).astype(low),
            ("x", "c"),
            scatter_dimension=1,
            tiled=True,
        )

    mixed_parts = [mixed]
    moved = outer_shift(mixed, 1)
    begin(0)
    moved, done, grad_sums, output_sums, reduce_pieces = tie(
        moved, done, grad_sums, output_sums, reduce_pieces
    )
    reduce_all = reduce_all + [reduce_whole(piece) for piece in reduce_pieces[1:]]
    mixed_parts.append(moved)
    moved = outer_shift(moved, 1)
    begin(1)
    moved, done, grad_sums, output_sums = tie(moved, done, grad_sums, output_sums)
    mixed_parts.append(moved)
    moved = outer_shift(moved, 1)
    begin(2)
    rest(1)
    moved, done, grad_sums, output_sums = tie(moved, done, grad_sums, output_sums)
    mixed_parts.append(moved)
    moved = outer_shift(grad_sums[1].astype(low), 1)
    rest(2)
    begin(3)
    moved, done, grad_sums, output_sums = tie(moved, done, grad_sums, output_sums)
    moved = outer_shift((grad_sums[2] + moved.astype(wide)).astype(low), 1)
    rest(3)
    rest(0)
    mixed_all = jnp.concatenate(mixed_parts, 0)
    upstream_all = jnp.concatenate(upstream_parts, 0)
    moved, done, grad_sums, output_sums, mixed_all, upstream_all = tie(
        moved, done, grad_sums, output_sums, mixed_all, upstream_all
    )
    sent = (grad_sums[3] + moved.astype(wide)).astype(low)
    early, late = outer_shift(sent[:split], 1), outer_shift(sent[split:], 1)
    for k in range(outer):
        for j in range(1, inner):
            output_sums[k] = output_sums[k] + lowered(done[k, j], j)
    early, done, upstream_all, mixed_all = tie(early, done, upstream_all, mixed_all)
    expand_wide = [None] * inner
    reduce_wide = [None] * inner
    for j in range(1, inner):
        expand_wide[j] = expand_back(j)
    late, done, upstream_all, mixed_all = tie(late, done, upstream_all, mixed_all)
    moved = jnp.concatenate([early, late], 0)
    mixed_grad = grad_sums[0] + moved.astype(wide)
    _, second_back = jax.vjp(norm_rows, residual, norm_two)
    residual_from, two_grad = second_back(mixed_grad)
    residual_grad = upstream + residual_from
    residual_low = residual_grad.astype(low)
    output_total = outer_shift(output_sums[1].astype(low), 1)
    early_row = ring_gather(residual_low[:split], "x")
    late_row = ring_gather(residual_low[split:], "x")
    early_row, done, upstream_all, mixed_all = tie(early_row, done, upstream_all, mixed_all)
    for j in range(1, inner):
        reduce_wide[j] = reduce_back(j)
    expand_wide[0] = expand_back(0)
    late_row, output_total, done, upstream_all = tie(late_row, output_total, done, upstream_all)
    residual_row = [jnp.concatenate(pair, 0) for pair in zip(early_row, late_row)]
    residual_all = jnp.concatenate(
        residual_row + [swapped(piece, "c", 1) for piece in residual_row], 0
    )
    slots = wide_slots()

    def wide_parts(whole, axis, i):
        return [lax.dynamic_slice_in_dim(whole, slot * depth, depth, axis) for slot in slots[i]]

    gated_grad = contract_cols(residual_all, output_all)
    output_total = outer_shift((output_sums[2] + output_total.astype(wide)).astype(low), 1)
    back = attend_back(
        near,
        gated_grad,
        raw,
        starts,
        cosine,
        sine,
        head_gains,
        (query, key, value, attended, total_log),
        heads,
        groups,
    )
    expand_both = inner_scatter([part.astype(wide) for part in expand_wide])
    back, output_total, expand_both, done, residual_all = tie(
        back, output_total, expand_both, done, residual_all
    )
    low_grads, low_near, head_gain_grads = back
    output_total = outer_shift((output_sums[3] + output_total.astype(wide)).astype(low), 1)
    project_grad = pinned(contract_rows(group_in, low_grads))
    project_wide = [None] * outer
    order = [(step + 1) % outer for step in range(outer)]
    project_wide[order[0]] = inner_scatter(wide_parts(project_grad, 0, order[0]))
    output_grad = contract_rows(gated_near, residual_all)

    def output_rows_of(i):
        return jnp.concatenate(wide_parts(output_grad, 1, i), 1)

    def normed_back(rows):
        return contract_cols(rows, project_all)

    received = swapped(normed_back(low_near[half:]).astype(low), "c", 1)
    normed_grad = normed_back(low_near[:half]) + received.astype(wide)
    normed_grad, project_wide[order[0]], project_grad, output_total = tie(
        normed_grad, project_wide[order[0]], project_grad, output_total
    )
    normed_grad = ring_scatter(by_x(normed_grad), "x")
    project_total = project_wide[order[0]]
    output_part = output_rows_of(order[0])
    for i in order[1:]:
        moved, output_new, across = tie(
            outer_shift(project_total.astype(low), 1),
            outer_shift(output_part.astype(low), 1),
            inner_scatter(wide_parts(project_grad, 0, i)),
        )
        project_total = across + moved.astype(wide)
        output_part = output_rows_of(i) + output_new.astype(wide)
    project_part = pinned(project_total)
    output_part = inner_scatter([output_part[:, j * depth : (j + 1) * depth] for j in range(inner)])
    reduce_wide[0] = reduce_back(0)
    block_output = (residual + output_sums[0] + output_total.astype(wide)).astype(low)
    _, first_back = jax.vjp(norm_rows, inputs, norm_one)
    input_from, one_grad = first_back(normed_grad)
    input_grad = residual_grad + input_from
    reduce_part = inner_scatter([part.astype(wide) for part in reduce_wide])
    expand_part = jnp.stack([expand_both[:, :hidden], expand_both[:, hidden:]])
    query_part = project_part[:, :query_width]
    keyvalue_part = jnp.stack(
        [project_part[:, query_width:value_from], project_part[:, value_from:gate_from]]
    )
    headgate_part = project_part[:, gate_from : gate_from + heads]
    gain_partial = jnp.concatenate([one_grad, two_grad, head_gain_grads.reshape(-1)])
    parts = (query_part, keyvalue_part, headgate_part, output_part, expand_part, reduce_part)
    squares = jnp.zeros((), jnp.float32)
    for part_grad in parts:
        squares = squares + jnp.sum(part_grad * part_grad)
    totals = jnp.concatenate([gain_partial, squares[None]])
    for axis in ("c", "x", "w"):
        totals = all_sum(totals, axis)
    gains_grad, square_total = totals[:-1], totals[-1]
    grad_norm = jnp.sqrt(square_total + jnp.sum(gains_grad * gains_grad))
    clip = CLIP_NORM / jnp.maximum(grad_norm, CLIP_NORM)
    gains_new = adam_step(gains, gains_grad * clip, gain_first, gain_second, GAIN_RATE, 0.0)
    masters = (
        query_weight,
        keyvalue_weight,
        headgate_weight,
        output_weight,
        expand_weight,
        reduce_weight,
    )
    states = (
        (query_first, query_second),
        (keyvalue_first, keyvalue_second),
        (headgate_first, headgate_second),
        (output_first, output_second),
        (expand_first, expand_second),
        (reduce_first, reduce_second),
    )
    results = [grad_norm, block_output, input_grad, gains_new[0], gains_new[1], gains_new[2]]
    for index in range(6):
        rate = OUTPUT_RATE if index == 3 else WEIGHT_RATE
        updated, first_new, second_new = adam_step(
            masters[index],
            parts[index] * clip,
            states[index][0],
            states[index][1],
            rate,
            WEIGHT_DECAY,
        )
        results = results + [updated, first_new, second_new, updated.astype(low)]
    return tuple(results)


def solution(mesh):
    heads, wides = mesh.shape["head"], mesh.shape["wide"]
    grid = Mesh(mesh.devices.reshape(heads // 2, 2, wides), ("x", "c", "w"))
    wide, head = ("w",), ("x", "c")
    rows = P(wide + head, None)
    by_wide = P(wide, head)
    stacked = P(None, wide, head)
    by_head = P(head, wide)
    widened = P(None, head, wide)
    return jax.shard_map(
        body,
        mesh=grid,
        in_specs=(rows, rows, P(wide), P(wide + head))
        + (P(),) * 4
        + (by_wide,) * 3
        + (stacked,) * 3
        + (by_wide,) * 3
        + (by_head,) * 3
        + (widened,) * 3
        + (by_wide,) * 3,
        out_specs=(P(), rows, rows)
        + (P(),) * 3
        + (by_wide,) * 4
        + (stacked,) * 4
        + (by_wide,) * 4
        + (by_head,) * 4
        + (widened,) * 4
        + (by_wide,) * 4,
        check_vma=False,
    )
```

time: 961 us -> 724 us (0.75)
  local copies, waits for them, and re-layouts: 173 us -> 50.1 us
  matrix products: 222 us -> 170 us
  waiting for transfers between devices: 277 us -> 233 us
  Pallas kernels: 0 us -> 41.8 us
  other arithmetic: 138 us -> 99.7 us
  starting transfers between devices: 111 us -> 98.8 us
    ppermute x55 -> x5, waiting for transfers between devices: 276 us -> 50.2 us  [hop(): return lax.ppermute(value, axis, [(i, (i - 1) % size) for i in range(size)])]
    ppermute x2 -> x52, waiting for transfers between devices: 0.99 us -> 170 us  [the longest x43 162 us: wide_from(): return lax.ppermute(value, 'w', pairs)]
    ppermute x55 -> x5, starting transfers between devices: 110 us -> 4.62 us  [hop(): return lax.ppermute(value, axis, [(i, (i - 1) % size) for i in range(size)])]
    ppermute x2 -> x52, starting transfers between devices: 0.01 us -> 93.4 us  [the longest x43 87.6 us: wide_from(): return lax.ppermute(value, 'w', pairs)]
    unnamed x355 -> x296, local copies, waits for them, and re-layouts: 67.6 us -> 17.3 us
    reshape x17 -> x0, local copies, waits for them, and re-layouts: 45.2 us -> none  [the longest x3 8.94 us: body(): contract_cols(residual_all, output_all).reshape(group_size, heads_local, HD)]
    pallas_call x0 -> x2, Pallas kernels: none -> 41.8 us  [the longest x1 21.7 us: attend_back(): pl.pallas_call(functools.partial(attend_back_kernel, heads, groups, lengt...]
    dot_general x33 -> x19, matrix products: 102 us -> 69.7 us  [the longest x8 35.5 us: hidden_part(): both = jnp.dot(mixed_parts[k], expand_all[j], preferred_element_type=wide)]
  transfers between devices with their start and end apart: 66 -> 66, of which waited for: 29 -> 31; matrix products, arithmetic and copies ran while one was open for 48% -> 37% of each run, Pallas kernels for 0% -> 6%
where the time goes in v2:
time: 724 us; the launch traced here: 716 us
  waiting for transfers between devices  233 us (32%)
  matrix products  170 us (23%)
  other arithmetic  99.7 us (14%)
  starting transfers between devices  98.8 us (14%)
  local copies, waits for them, and re-layouts  50.1 us (7%)
  Pallas kernels  41.8 us (6%)
  between operations  22.8 us (3%)
    ppermute x43, waiting for transfers between devices, wide_from(): return lax.ppermute(value, 'w', pairs)  162 us
    ppermute x43, starting transfers between devices, wide_from(): return lax.ppermute(value, 'w', pairs)  87.6 us
    dot_general x19, matrix products, contract_cols(): lax.dot_general(left, right, (((1,), (1,)), ((), ())), preferred_element_...  64.2 us
    ppermute x5, waiting for transfers between devices, hop(): return lax.ppermute(value, axis, [(i, (i - 1) % size) for i in range(size)])  50.2 us
    dot_general x6, matrix products, contract_rows(): lax.dot_general(left, right, (((0,), (0,)), ((), ())), preferred_element_...  36.4 us
    dot_general x8, matrix products, hidden_part(): both = jnp.dot(mixed_parts[k], expand_all[j], preferred_element_type=wide)  35.5 us
    pallas_call x1, Pallas kernels, attend_back(): pl.pallas_call(functools.partial(attend_back_kernel, heads, groups, lengt...  21.7 us
    convert_element_type x6, other arithmetic, body(): results = results + [updated, first_new, second_new, updated.astype(low)]  20.6 us
  transfers between devices with their start and end apart: 66, of which 31 were waited for; matrix products, arithmetic and copies ran while one was open for 37% of the time, Pallas kernels for 6%

profile of v2, /device:TPU:0, one launch (start us, length us, event | category | flops | bytes accessed | tf_op | source)
XLA Modules:
  0.0 716.4 jit_solution(17970892247474650352)
XLA Ops:
  16.9 5.1 collective-permute-start
  41.4 9.7 %collective-permute-done.2 = bf16[256,1152]{1,0:T(8,128)(2,1)S(1)} collective-permute-done((bf16[256,1152]{1,0:T(8,128)(2,1)}, bf16[256,1152]{1,0:T(8,128)(2,1)S(1)}, u32[]{:S(2)}, u32[]{:S(2)}) %collective-permute-start.2) | collective-permute-done | bytes 589856 | tf_op jit(solution)/shard_map/ppermute | solution.py:370
  75.0 4.5 collective-permute-done.7
  79.5 13.0 %collective-permute-done.8 = bf16[512,256]{1,0:T(8,128)(2,1)S(1)} collective-permute-done((bf16[512,256]{1,0:T(8,128)(2,1)S(1)}, bf16[512,256]{1,0:T(8,128)(2,1)S(1)}, u32[]{:S(2)}, u32[]{:S(2)}) %collective-permute-start.8) | collective-permute-done | bytes 262176 | tf_op jit(solution)/shard_map/ppermute | solution.py:370
  98.3 10.2 %fusion.88.raw = f32[1024,1152]{1,0:T(8,128)} fusion(bf16[1024,2048]{1,0:T(8,128)(2,1)} %all-gather.6.cloned.1.call-done, bf16[2048,1152]{1,0:T(8,128)(2,1)} %constant_dynamic-update-slice_fusion.14), kind=kOutput, calls=%fused_computation.272 | convolution fusion | flops 4831838208 | bytes 13631488 | tf_op jit(solution)/shard_map/dot_general | solution.py:548
  114.0 4.2 collective-permute-done.14
  127.1 20.1 %shard_map.481 = (bf16[1024,512]{1,0:T(8,128)(2,1)}, bf16[1024,256]{1,0:T(8,128)(2,1)}, bf16[1024,256]{1,0:T(8,128)(2,1)}, f32[1024,512]{1,0:T(8,128)}, f32[1024...) custom-call(s32[4]{0:T(128)} %pad_add_fusion.slots, f32[1024,1152]{1,0:T(8,128)} %fusion.88.raw, ...), custom_call_target="tpu_custom_call" | custom-call | flops 2147483648 | bytes 9961472 | tf_op jit(solution)/shard_map/pallas_call | solution.py:173
  149.9 4.1 collective-permute-done.17
  161.9 8.6 %collective-permute-done.18 = bf16[128,2048]{1,0:T(8,128)(2,1)S(1)} collective-permute-done((bf16[128,2048]{1,0:T(8,128)(2,1)S(1)}, bf16[128,2048]{1,0:T(8,128)(2,1)S(1)}, u32[]{:S(2)}, u32[]{:S(2)}) %collective-permute-start.18) | collective-permute-done | bytes 524320 | tf_op jit(solution)/shard_map/ppermute | solution.py:340
  170.5 10.4 %collective-permute-done.21 = bf16[128,2048]{1,0:T(8,128)(2,1)S(1)} collective-permute-done((bf16[128,2048]{1,0:T(8,128)(2,1)S(1)}, bf16[128,2048]{1,0:T(8,128)(2,1)S(1)}, u32[]{:S(2)}, u32[]{:S(2)}) %collective-permute-start.21) | collective-permute-done | bytes 524320 | tf_op jit(solution)/shard_map/ppermute | solution.py:340
  187.4 4.3 collective-permute-start.22
  193.3 3.5 pad_maximum_fusion.1
  196.8 6.2 fusion.89
  203.0 4.0 multiply_convert_fusion.23
  211.0 3.1 fusion.67
  214.2 3.2 collective-permute-start.24
  217.5 5.1 fusion.91
  231.8 6.4 collective-permute-done.24
  238.2 4.3 collective-permute-start.25
  242.5 3.3 fusion.94
  253.6 6.1 fusion.93
  259.7 3.5 all-gather.14.cloned.1.call-done
  263.2 4.8 multiply_convert_fusion.17
  270.3 3.8 collective-permute-start.26
  274.1 4.9 fusion.96
  281.2 3.2 fusion.97
  290.0 4.7 fusion.63
  294.7 4.9 fusion.100
  310.2 4.8 fusion.61
  318.9 15.1 %collective-permute-done.27 = bf16[256,2048]{1,0:T(8,128)(2,1)S(1)} collective-permute-done((bf16[256,2048]{1,0:T(8,128)(2,1)S(1)}, bf16[256,2048]{1,0:T(8,128)(2,1)S(1)}, u32[]{:S(2)}, u32[]{:S(2)}) %collective-permute-start.27) | collective-permute-done | bytes 1048608 | tf_op jit(solution)/shard_map/ppermute | solution.py:370
  337.4 10.3 %collective-permute-done.28 = bf16[128,2048]{1,0:T(8,128)(2,1)S(1)} collective-permute-done((bf16[128,2048]{1,0:T(8,128)(2,1)S(1)}, bf16[128,2048]{1,0:T(8,128)(2,1)S(1)}, u32[]{:S(2)}, u32[]{:S(2)}) %collective-permute-start.28) | collective-permute-done | bytes 524320 | tf_op jit(solution)/shard_map/ppermute | solution.py:370
  347.7 9.1 %convolution_convert_fusion = bf16[2048,1536]{1,0:T(8,128)(2,1)} fusion(bf16[1024,2048]{1,0:T(8,128)(2,1)S(1)} %pad_maximum_fusion, bf16[256,1536]{1,0:T(8,128)(2,1)S(1)} %pad_maximum_fusion.14, bf16[256,1536]{1,0:T(8,128)(2,1)S(1)} %pad_maximum_fusion.11, bf16[256,1536]{1,0:T(8,128)(2,1)S(1)} %pad_maximum_fusion.9, bf16[256,1536]{1,0:T(8,128)(2,1)S(1)} %pad_maximum_fusion.13), kind=kOutput, calls=%fused_computation | convolution fusion | flops 6458179584 | bytes 13631488 | tf_op jit(solution)/shard_map/dot_general | solution.py:50
  356.9 4.3 collective-permute-start.29
  361.3 9.4 %collective-permute-done.29 = bf16[128,2048]{1,0:T(8,128)(2,1)S(1)} collective-permute-done((bf16[128,2048]{1,0:T(8,128)(2,1)S(1)}, bf16[128,2048]{1,0:T(8,128)(2,1)S(1)}, u32[]{:S(2)}, u32[]{:S(2)}) %collective-permute-start.29) | collective-permute-done | bytes 524320 | tf_op jit(solution)/shard_map/ppermute | solution.py:370
  376.0 20.0 %collective-permute-done.30 = bf16[128,2048]{1,0:T(8,128)(2,1)S(1)} collective-permute-done((bf16[128,2048]{1,0:T(8,128)(2,1)S(1)}, bf16[128,2048]{1,0:T(8,128)(2,1)S(1)}, u32[]{:S(2)}, u32[]{:S(2)}) %collective-permute-start.30) | collective-permute-done | bytes 524320 | tf_op jit(solution)/shard_map/ppermute | solution.py:340
  396.8 9.3 %convolution_convert_fusion.1 = bf16[2048,1536]{1,0:T(8,128)(2,1)} fusion(bf16[1024,2048]{1,0:T(8,128)(2,1)S(1)} %copy-done.40, bf16[256,1536]{1,0:T(8,128)(2,1)S(1)} %copy-done.83, bf16[256,1536]{1,0:T(8,128)(2,1)S(1)} %copy-done.82, bf16[256,1536]{1,0:T(8,128)(2,1)S(1)} %copy-done.81, bf16[256,1536]{1,0:T(8,128)(2,1)S(1)} %copy-done.80), kind=kOutput, calls=%fused_computation.1 | convolution fusion | flops 6458179584 | bytes 13631488 | tf_op jit(solution)/shard_map/dot_general | solution.py:50
  409.7 5.1 collective-permute-start.32
  420.4 11.2 %collective-permute-done.31 = bf16[128,2048]{1,0:T(8,128)(2,1)S(1)} collective-permute-done((bf16[128,2048]{1,0:T(8,128)(2,1)S(1)}, bf16[128,2048]{1,0:T(8,128)(2,1)S(1)}, u32[]{:S(2)}, u32[]{:S(2)}) %collective-permute-start.31) | collective-permute-done | bytes 524320 | tf_op jit(solution)/shard_map/ppermute | solution.py:340
  434.4 4.9 convolution_convert_fusion.2
  439.3 4.2 add_convert_fusion.2
  444.3 4.5 collective-permute-start.35
  458.0 6.1 fusion.102.gated_grad
  464.1 21.7 %shard_map.482 = (bf16[1024,1152]{1,0:T(8,128)(2,1)}, bf16[1024,1152]{1,0:T(8,128)(2,1)}, f32[2,128]{1,0:T(2,128)}) custom-call(s32[4]{0:T(128)} %pad_add_fusion.slots, f32[1024,512]{1,0:T(8,128)} %fusion.102.gated_grad, f32[1024,1152]{1,0:T(8,128)} %fusion.88.raw, s32[1024,1]{1,0:T(8,128)} %subtract_subtract_fusion.start, ...), custom_call_target="tpu_custom_call" | custom-call | flops 5368709120 | bytes 13369344 | tf_op jit(solution)/shard_map/pallas_call | solution.py:294
  485.8 8.9 %reduce-scatter.5.cloned.1.call-done = bf16[512,1536]{1,0:T(8,128)(2,1)} async-done(((bf16[2048,1536]{1,0:T(8,128)(2,1)}), bf16[512,1536]{1,0:T(8,128)(2,1)}) %reduce-scatter.5.cloned.1.call-update) | async-done | bytes 1572880 | tf_op jit(solution)/shard_map/reduce_scatter | solution.py:613
  494.7 4.1 convert_add_fusion.3
  498.9 6.6 convolution_convert_fusion.4
  505.5 5.7 fusion.104
  513.8 3.9 add_convert_fusion.1
  517.7 3.4 collective-permute-start.39
  521.1 5.1 convolution_convert_fusion.3
  530.1 7.4 %convert_add_fusion = f32[512,2048]{1,0:T(8,128)} fusion(bf16[512,2048]{1,0:T(8,128)(2,1)} %collective-permute-done.37, bf16[2048,1152]{1,0:T(8,128)(2,1)} %constant_dynamic-update-slice_fusion.14, bf16[1024,1152]{1,0:T(8,128)(2,1)S(1)} %copy-done.130), kind=kOutput, calls=%fused_computation.5 | convolution fusion | flops 2418016256 | bytes 12189696 | tf_op jit(solution)/shard_map/dot_general | solution.py:56
  537.5 6.6 collective-permute-done.39
  549.4 4.4 collective-permute-start.42
  555.4 5.3 collective-permute-done.49
  560.6 12.6 %collective-permute-done.46 = bf16[256,1152]{1,0:T(8,128)(2,1)S(1)} collective-permute-done((bf16[256,1152]{1,0:T(8,128)(2,1)S(1)}, bf16[256,1152]{1,0:T(8,128)(2,1)S(1)}, u32[]{:S(2)}, u32[]{:S(2)}) %collective-permute-start.46) | collective-permute-done | bytes 589856 | tf_op jit(solution)/shard_map/ppermute | solution.py:370
  573.3 11.3 %collective-permute-done.43 = bf16[256,1152]{1,0:T(8,128)(2,1)S(1)} collective-permute-done((bf16[256,1152]{1,0:T(8,128)(2,1)S(1)}, bf16[256,1152]{1,0:T(8,128)(2,1)S(1)}, u32[]{:S(2)}, u32[]{:S(2)}) %collective-permute-start.43) | collective-permute-done | bytes 589856 | tf_op jit(solution)/shard_map/ppermute | solution.py:370
  586.9 4.4 collective-permute-start.44
  595.7 18.7 %collective-permute-done.45 = bf16[512,512]{1,0:T(8,128)(2,1)} collective-permute-done((bf16[512,512]{1,0:T(8,128)(2,1)}, bf16[512,512]{1,0:T(8,128)(2,1)}, u32[]{:S(2)}, u32[]{:S(2)}) %collective-permute-start.45) | collective-permute-done | bytes 524320 | tf_op jit(solution)/shard_map/ppermute | solution.py:370
  615.7 4.3 collective-permute-start.47
  626.5 15.3 %collective-permute-done.48 = bf16[512,512]{1,0:T(8,128)(2,1)S(1)} collective-permute-done((bf16[512,512]{1,0:T(8,128)(2,1)S(1)}, bf16[512,512]{1,0:T(8,128)(2,1)S(1)}, u32[]{:S(2)}, u32[]{:S(2)}) %collective-permute-start.48) | collective-permute-done | bytes 524320 | tf_op jit(solution)/shard_map/ppermute | solution.py:370
  667.2 3.5 add_convert_fusion
  670.9 3.7 collective-permute-done.55
  693.7 7.4 %fusion.70 = (bf16[2,512,768]{2,1,0:T(8,128)(2,1)}, f32[2,512,768]{2,1,0:T(8,128)}, f32[2,512,768]{2,1,0:T(8,128)}, f32[2,512,768]{2,1,0:T(8,128)}) fusion(f32[2,512,768]{2,1,0:T(8,128)S(1)} %copy-done.13, f32[]{:T(128)S(6)} %div.202, f32[1,512,768]{2,1,0:T(8,128)S(1)} %copy-done.11, f32[1,512,768]{2,1,0:T(8,128)S(1)} %copy-done.9, ...), kind=kLoop, calls=%fused_computation.261 | loop fusion | flops 14155776 | bytes 23592964 | tf_op jit(solution)/shard_map/convert_element_type | solution.py:792
  703.8 4.5 fusion.68
  (559 shorter events, 237.4 us)
Async XLA Ops:
  7.2 91.1 %all-gather.6.cloned.1.call-start = ((), (), s32[]{:S(2)}) async-start(), calls=%async_computation.4 | async-start | bytes 5242880 | tf_op jit(solution)/shard_map/all_gather | solution.py:506
  12.2 184.6 %all-gather.8.cloned.1.call-start = ((), (), s32[]{:S(2)}) async-start(), calls=%async_computation.5 | async-start | bytes 7864320 | tf_op jit(solution)/shard_map/all_gather | solution.py:514
  14.7 188.2 %all-gather.10.cloned.1.call-start = ((), (), s32[]{:S(2)}) async-start(), calls=%async_computation.6 | async-start | bytes 3932160 | tf_op jit(solution)/shard_map/all_gather | solution.py:517
  16.9 17.7 %collective-permute-start = (bf16[256,1152]{1,0:T(8,128)(2,1)S(1)}, bf16[256,1152]{1,0:T(8,128)(2,1)}, u32[]{:S(2)}, u32[]{:S(2)}) collective-permute-start(bf16[256,1152]{1,0:T(8,128)(2,1)S(1)} %concatenate.96), channel_id=1, source_target_pairs={{2,0},{3,1},{4,2},{5,3},{6,4},{7,5},{0,6},{1,7},{10,8},{11,9},{12,... | collective-permute-start | bytes 1769480 | tf_op jit(solution)/shard_map/ppermute | solution.py:370
  22.0 14.9 %collective-permute-start.1 = (bf16[256,1152]{1,0:T(8,128)(2,1)S(1)}, bf16[256,1152]{1,0:T(8,128)(2,1)}, u32[]{:S(2)}, u32[]{:S(2)}) collective-permute-start(bf16[256,1152]{1,0:T(8,128)(2,1)S(1)} %concatenate.96), channel_id=1, source_target_pairs={{1,0},{0,1},{3,2},{2,3},{5,4},{4,5},{7,6},{6,7},{9,8},{8,9},{11,10... | collective-permute-start | bytes 1769480 | tf_op jit(solution)/shard_map/ppermute | solution.py:370
  24.6 229.1 %all-gather.12.cloned.1.call-start = ((), (), s32[]{:S(2)}) async-start(), calls=%async_computation.7 | async-start | bytes 7864320 | tf_op jit(solution)/shard_map/all_gather | solution.py:514
  36.9 14.1 %collective-permute-start.2 = (bf16[256,1152]{1,0:T(8,128)(2,1)}, bf16[256,1152]{1,0:T(8,128)(2,1)S(1)}, u32[]{:S(2)}, u32[]{:S(2)}) collective-permute-start(bf16[256,1152]{1,0:T(8,128)(2,1)} %collective-permute-done), channel_id=1, source_target_pairs={{2,0},{3,1},{4,2},{5,3},{6,4},{7,5},{0,6},{1,7},{10,8},{11,9},{12,... | collective-permute-start | bytes 1769480 | tf_op jit(solution)/shard_map/ppermute | solution.py:370
  39.0 14.1 %collective-permute-start.3 = (bf16[256,1152]{1,0:T(8,128)(2,1)}, bf16[256,1152]{1,0:T(8,128)(2,1)S(1)}, u32[]{:S(2)}, u32[]{:S(2)}) collective-permute-start(bf16[256,1152]{1,0:T(8,128)(2,1)} %collective-permute-done), channel_id=1, source_target_pairs={{1,0},{0,1},{3,2},{2,3},{5,4},{4,5},{7,6},{6,7},{9,8},{8,9},{11,10... | collective-permute-start | bytes 1769480 | tf_op jit(solution)/shard_map/ppermute | solution.py:370
  53.1 13.0 %collective-permute-start.4 = (bf16[256,1152]{1,0:T(8,128)(2,1)S(1)}, bf16[256,1152]{1,0:T(8,128)(2,1)S(1)}, u32[]{:S(2)}, u32[]{:S(2)}) collective-permute-start(bf16[256,1152]{1,0:T(8,128)(2,1)S(1)} %collective-permute-done.2), channel_id=1, source_target_pairs={{2,0},{3,1},{4,2},{5,3},{6,4},{7,5},{0,6},{1,7},{10,8},{11,9},{12,... | collective-permute-start | bytes 1769480 | tf_op jit(solution)/shard_map/ppermute | solution.py:370
  55.2 13.4 %collective-permute-start.5 = (bf16[256,1152]{1,0:T(8,128)(2,1)S(1)}, bf16[256,1152]{1,0:T(8,128)(2,1)S(1)}, u32[]{:S(2)}, u32[]{:S(2)}) collective-permute-start(bf16[256,1152]{1,0:T(8,128)(2,1)S(1)} %collective-permute-done.2), channel_id=1, source_target_pairs={{1,0},{0,1},{3,2},{2,3},{5,4},{4,5},{7,6},{6,7},{9,8},{8,9},{11,10... | collective-permute-start | bytes 1769480 | tf_op jit(solution)/shard_map/ppermute | solution.py:370
  68.6 23.8 %collective-permute-start.6 = (bf16[256,1152]{1,0:T(8,128)(2,1)S(1)}, bf16[256,1152]{1,0:T(8,128)(2,1)S(1)}, u32[]{:S(2)}, u32[]{:S(2)}) collective-permute-start(bf16[256,1152]{1,0:T(8,128)(2,1)S(1)} %collective-permute-done.4), channel_id=1, source_target_pairs={{1,0},{0,1},{3,2},{2,3},{5,4},{4,5},{7,6},{6,7},{9,8},{8,9},{11,10... | collective-permute-start | bytes 1769480 | tf_op jit(solution)/shard_map/ppermute | solution.py:370
  71.0 8.5 %collective-permute-start.7 = (bf16[512,256]{1,0:T(8,128)(2,1)S(1)}, bf16[512,256]{1,0:T(8,128)(2,1)}, u32[]{:S(2)}, u32[]{:S(2)}) collective-permute-start(bf16[512,256]{1,0:T(8,128)(2,1)S(1)} %copy-done.71), channel_id=1, source_target_pairs={{2,0},{3,1},{4,2},{5,3},{6,4},{7,5},{0,6},{1,7},{10,8},{11,9},{12,... | collective-permute-start | bytes 786440 | tf_op jit(solution)/shard_map/ppermute | solution.py:370
  72.7 19.7 %collective-permute-start.8 = (bf16[512,256]{1,0:T(8,128)(2,1)S(1)}, bf16[512,256]{1,0:T(8,128)(2,1)S(1)}, u32[]{:S(2)}, u32[]{:S(2)}) collective-permute-start(bf16[512,256]{1,0:T(8,128)(2,1)S(1)} %copy-done.71), channel_id=1, source_target_pairs={{4,0},{5,1},{6,2},{7,3},{0,4},{1,5},{2,6},{3,7},{12,8},{13,9},{14,... | collective-permute-start | bytes 786440 | tf_op jit(solution)/shard_map/ppermute | solution.py:370
  72.7 19.7 %collective-permute-start.9 = (bf16[512,256]{1,0:T(8,128)(2,1)S(1)}, bf16[512,256]{1,0:T(8,128)(2,1)S(1)}, u32[]{:S(2)}, u32[]{:S(2)}) collective-permute-start(bf16[512,256]{1,0:T(8,128)(2,1)S(1)} %copy-done.71), channel_id=1, source_target_pairs={{6,0},{7,1},{0,2},{1,3},{2,4},{3,5},{4,6},{5,7},{14,8},{15,9},{8,1... | collective-permute-start | bytes 786440 | tf_op jit(solution)/shard_map/ppermute | solution.py:370
  92.4 16.0 %collective-permute-start.10 = (bf16[512,256]{1,0:T(8,128)(2,1)S(1)}, bf16[512,256]{1,0:T(8,128)(2,1)}, u32[]{:S(2)}, u32[]{:S(2)}) collective-permute-start(bf16[512,256]{1,0:T(8,128)(2,1)S(1)} %copy-done.71), channel_id=1, source_target_pairs={{1,0},{0,1},{3,2},{2,3},{5,4},{4,5},{7,6},{6,7},{9,8},{8,9},{11,10... | collective-permute-start | bytes 786440 | tf_op jit(solution)/shard_map/ppermute | solution.py:370
  92.9 15.6 %collective-permute-start.11 = (bf16[512,256]{1,0:T(8,128)(2,1)}, bf16[512,256]{1,0:T(8,128)(2,1)}, u32[]{:S(2)}, u32[]{:S(2)}) collective-permute-start(bf16[512,256]{1,0:T(8,128)(2,1)} %collective-permute-done.7), channel_id=1, source_target_pairs={{1,0},{0,1},{3,2},{2,3},{5,4},{4,5},{7,6},{6,7},{9,8},{8,9},{11,10... | collective-permute-start | bytes 786440 | tf_op jit(solution)/shard_map/ppermute | solution.py:370
  94.5 16.8 %collective-permute-start.12 = (bf16[512,256]{1,0:T(8,128)(2,1)S(1)}, bf16[512,256]{1,0:T(8,128)(2,1)}, u32[]{:S(2)}, u32[]{:S(2)}) collective-permute-start(bf16[512,256]{1,0:T(8,128)(2,1)S(1)} %collective-permute-done.8), channel_id=1, source_target_pairs={{1,0},{0,1},{3,2},{2,3},{5,4},{4,5},{7,6},{6,7},{9,8},{8,9},{11,10... | collective-permute-start | bytes 786440 | tf_op jit(solution)/shard_map/ppermute | solution.py:370
  94.9 19.1 %collective-permute-start.13 = (bf16[512,256]{1,0:T(8,128)(2,1)S(1)}, bf16[512,256]{1,0:T(8,128)(2,1)}, u32[]{:S(2)}, u32[]{:S(2)}) collective-permute-start(bf16[512,256]{1,0:T(8,128)(2,1)S(1)} %collective-permute-done.9), channel_id=1, source_target_pairs={{1,0},{0,1},{3,2},{2,3},{5,4},{4,5},{7,6},{6,7},{9,8},{8,9},{11,10... | collective-permute-start | bytes 786440 | tf_op jit(solution)/shard_map/ppermute | solution.py:370
  96.5 21.7 %collective-permute-start.14 = (bf16[256,2048]{1,0:T(8,128)(2,1)S(1)}, bf16[256,2048]{1,0:T(8,128)(2,1)}, u32[]{:S(2)}, u32[]{:S(2)}) collective-permute-start(bf16[256,2048]{1,0:T(8,128)(2,1)S(1)} %fusion.23), channel_id=1, source_target_pairs={{2,0},{3,1},{4,2},{5,3},{6,4},{7,5},{0,6},{1,7},{10,8},{11,9},{12,... | collective-permute-start | bytes 3145736 | tf_op jit(solution)/shard_map/ppermute | solution.py:370
  118.2 28.9 %collective-permute-start.15 = (bf16[256,2048]{1,0:T(8,128)(2,1)}, bf16[256,2048]{1,0:T(8,128)(2,1)S(1)}, u32[]{:S(2)}, u32[]{:S(2)}) collective-permute-start(bf16[256,2048]{1,0:T(8,128)(2,1)} %collective-permute-done.14), channel_id=1, source_target_pairs={{2,0},{3,1},{4,2},{5,3},{6,4},{7,5},{0,6},{1,7},{10,8},{11,9},{12,... | collective-permute-start | bytes 3145736 | tf_op jit(solution)/shard_map/ppermute | solution.py:370
  121.3 25.8 %collective-permute-start.16 = (bf16[512,768]{1,0:T(8,128)(2,1)S(1)}, bf16[512,768]{1,0:T(8,128)(2,1)S(1)}, u32[]{:S(2)}, u32[]{:S(2)}) collective-permute-start(bf16[512,768]{1,0:T(8,128)(2,1)S(1)} %copy-done.48), channel_id=1, source_target_pairs={{1,0},{0,1},{3,2},{2,3},{5,4},{4,5},{7,6},{6,7},{9,8},{8,9},{11,10... | collective-permute-start | bytes 2359304 | tf_op jit(solution)/shard_map/ppermute | solution.py:370
  149.9 4.2 collective-permute-start.17
  155.5 15.0 %collective-permute-start.18 = (bf16[128,2048]{1,0:T(8,128)(2,1)S(1)}, bf16[128,2048]{1,0:T(8,128)(2,1)S(1)}, u32[]{:S(2)}, u32[]{:S(2)}) collective-permute-start(bf16[128,2048]{1,0:T(8,128)(2,1)S(1)} %get-tuple-element.677), channel_id=1, source_target_pairs={{0,16},{16,0},{1,17},{17,1},{2,18},{18,2},{3,19},{19,3},{4,20},{20... | collective-permute-start | bytes 1572872 | tf_op jit(solution)/shard_map/ppermute | solution.py:340
  157.2 23.7 %collective-permute-start.21 = (bf16[128,2048]{1,0:T(8,128)(2,1)S(1)}, bf16[128,2048]{1,0:T(8,128)(2,1)S(1)}, u32[]{:S(2)}, u32[]{:S(2)}) collective-permute-start(bf16[128,2048]{1,0:T(8,128)(2,1)S(1)} %get-tuple-element.678), channel_id=1, source_target_pairs={{0,16},{16,0},{1,17},{17,1},{2,18},{18,2},{3,19},{19,3},{4,20},{20... | collective-permute-start | bytes 1572872 | tf_op jit(solution)/shard_map/ppermute | solution.py:340
  157.7 24.8 %collective-permute-start.20 = (bf16[256,2048]{1,0:T(8,128)(2,1)S(1)}, bf16[256,2048]{1,0:T(8,128)(2,1)S(1)}, u32[]{:S(2)}, u32[]{:S(2)}) collective-permute-start(bf16[256,2048]{1,0:T(8,128)(2,1)S(1)} %collective-permute-done.15), channel_id=1, source_target_pairs={{2,0},{3,1},{4,2},{5,3},{6,4},{7,5},{0,6},{1,7},{10,8},{11,9},{12,... | collective-permute-start | bytes 3145736 | tf_op jit(solution)/shard_map/ppermute | solution.py:370
  160.3 22.1 %collective-permute-start.19 = (bf16[512,768]{1,0:T(8,128)(2,1)S(1)}, bf16[512,768]{1,0:T(8,128)(2,1)S(1)}, u32[]{:S(2)}, u32[]{:S(2)}) collective-permute-start(bf16[512,768]{1,0:T(8,128)(2,1)S(1)} %get-tuple-element.308), channel_id=1, source_target_pairs={{1,0},{0,1},{3,2},{2,3},{5,4},{4,5},{7,6},{6,7},{9,8},{8,9},{11,10... | collective-permute-start | bytes 2359304 | tf_op jit(solution)/shard_map/ppermute | solution.py:370
  184.8 78.4 %all-gather.14.cloned.1.call-start = ((), (), s32[]{:S(2)}) async-start(), calls=%async_computation.8 | async-start | bytes 3932160 | tf_op jit(solution)/shard_map/all_gather | solution.py:517
  187.4 26.8 %collective-permute-start.22 = (bf16[256,2048]{1,0:T(8,128)(2,1)S(1)}, bf16[256,2048]{1,0:T(8,128)(2,1)}, u32[]{:S(2)}, u32[]{:S(2)}) collective-permute-start(bf16[256,2048]{1,0:T(8,128)(2,1)S(1)} %multiply_convert_fusion), channel_id=1, source_target_pairs={{2,0},{3,1},{4,2},{5,3},{6,4},{7,5},{0,6},{1,7},{10,8},{11,9},{12,... | collective-permute-start | bytes 3145736 | tf_op jit(solution)/shard_map/ppermute | solution.py:370
  191.7 22.4 %collective-permute-start.23 = (bf16[768,512]{1,0:T(8,128)(2,1)}, bf16[768,512]{1,0:T(8,128)(2,1)}, u32[]{:S(2)}, u32[]{:S(2)}) collective-permute-start(bf16[768,512]{1,0:T(8,128)(2,1)} %convert_element_type.285), channel_id=1, source_target_pairs={{1,0},{0,1},{3,2},{2,3},{5,4},{4,5},{7,6},{6,7},{9,8},{8,9},{11,10... | collective-permute-start | bytes 2359304 | tf_op jit(solution)/shard_map/ppermute | solution.py:370
  214.2 24.1 %collective-permute-start.24 = (bf16[256,2048]{1,0:T(8,128)(2,1)}, bf16[256,2048]{1,0:T(8,128)(2,1)}, u32[]{:S(2)}, u32[]{:S(2)}) collective-permute-start(bf16[256,2048]{1,0:T(8,128)(2,1)} %collective-permute-done.22), channel_id=1, source_target_pairs={{2,0},{3,1},{4,2},{5,3},{6,4},{7,5},{0,6},{1,7},{10,8},{11,9},{12,... | collective-permute-start | bytes 3145736 | tf_op jit(solution)/shard_map/ppermute | solution.py:370
  217.4 234.4 %reduce-scatter.7.cloned.1.call-start = ((), (), s32[]{:S(2)}) async-start(), calls=%async_computation.10 | async-start | bytes 7864320 | tf_op jit(solution)/shard_map/reduce_scatter | solution.py:613
  238.2 32.0 %collective-permute-start.25 = (bf16[256,2048]{1,0:T(8,128)(2,1)}, bf16[256,2048]{1,0:T(8,128)(2,1)}, u32[]{:S(2)}, u32[]{:S(2)}) collective-permute-start(bf16[256,2048]{1,0:T(8,128)(2,1)} %collective-permute-done.24), channel_id=1, source_target_pairs={{2,0},{3,1},{4,2},{5,3},{6,4},{7,5},{0,6},{1,7},{10,8},{11,9},{12,... | collective-permute-start | bytes 3145736 | tf_op jit(solution)/shard_map/ppermute | solution.py:370
  270.3 38.3 %collective-permute-start.26 = (bf16[256,2048]{1,0:T(8,128)(2,1)S(1)}, bf16[256,2048]{1,0:T(8,128)(2,1)S(1)}, u32[]{:S(2)}, u32[]{:S(2)}) collective-permute-start(bf16[256,2048]{1,0:T(8,128)(2,1)S(1)} %add.511), channel_id=1, source_target_pairs={{2,0},{3,1},{4,2},{5,3},{6,4},{7,5},{0,6},{1,7},{10,8},{11,9},{12,... | collective-permute-start | bytes 3145736 | tf_op jit(solution)/shard_map/ppermute | solution.py:370
  308.9 25.1 %collective-permute-start.27 = (bf16[256,2048]{1,0:T(8,128)(2,1)S(1)}, bf16[256,2048]{1,0:T(8,128)(2,1)S(1)}, u32[]{:S(2)}, u32[]{:S(2)}) collective-permute-start(bf16[256,2048]{1,0:T(8,128)(2,1)S(1)} %add_convert_fusion.5), channel_id=1, source_target_pairs={{2,0},{3,1},{4,2},{5,3},{6,4},{7,5},{0,6},{1,7},{10,8},{11,9},{12,... | collective-permute-start | bytes 3145736 | tf_op jit(solution)/shard_map/ppermute | solution.py:370
  334.5 13.2 %collective-permute-start.28 = (bf16[128,2048]{1,0:T(8,128)(2,1)S(1)}, bf16[128,2048]{1,0:T(8,128)(2,1)S(1)}, u32[]{:S(2)}, u32[]{:S(2)}) collective-permute-start(bf16[128,2048]{1,0:T(8,128)(2,1)S(1)} %get-tuple-element.695), channel_id=1, source_target_pairs={{2,0},{3,1},{4,2},{5,3},{6,4},{7,5},{0,6},{1,7},{10,8},{11,9},{12,... | collective-permute-start | bytes 1572872 | tf_op jit(solution)/shard_map/ppermute | solution.py:370
  356.8 137.9 %reduce-scatter.5.cloned.1.call-start = ((), (), s32[]{:S(2)}) async-start(), calls=%async_computation.9 | async-start | bytes 7864320 | tf_op jit(solution)/shard_map/reduce_scatter | solution.py:613
  356.9 13.7 %collective-permute-start.29 = (bf16[128,2048]{1,0:T(8,128)(2,1)S(1)}, bf16[128,2048]{1,0:T(8,128)(2,1)S(1)}, u32[]{:S(2)}, u32[]{:S(2)}) collective-permute-start(bf16[128,2048]{1,0:T(8,128)(2,1)S(1)} %get-tuple-element.696), channel_id=1, source_target_pairs={{2,0},{3,1},{4,2},{5,3},{6,4},{7,5},{0,6},{1,7},{10,8},{11,9},{12,... | collective-permute-start | bytes 1572872 | tf_op jit(solution)/shard_map/ppermute | solution.py:370
  375.4 20.6 %collective-permute-start.30 = (bf16[128,2048]{1,0:T(8,128)(2,1)S(1)}, bf16[128,2048]{1,0:T(8,128)(2,1)S(1)}, u32[]{:S(2)}, u32[]{:S(2)}) collective-permute-start(bf16[128,2048]{1,0:T(8,128)(2,1)S(1)} %get-tuple-element.425), channel_id=1, source_target_pairs={{0,16},{16,0},{1,17},{17,1},{2,18},{18,2},{3,19},{19,3},{4,20},{20... | collective-permute-start | bytes 1572872 | tf_op jit(solution)/shard_map/ppermute | solution.py:340
  406.1 186.7 %reduce-scatter.11.cloned.1.call-start = ((), (), s32[]{:S(2)}) async-start(), calls=%async_computation.12 | async-start | bytes 3932160 | tf_op jit(solution)/shard_map/reduce_scatter | solution.py:621
  409.7 21.9 %collective-permute-start.32 = (bf16[256,2048]{1,0:T(8,128)(2,1)S(1)}, bf16[256,2048]{1,0:T(8,128)(2,1)S(1)}, u32[]{:S(2)}, u32[]{:S(2)}) collective-permute-start(bf16[256,2048]{1,0:T(8,128)(2,1)S(1)} %add_convert_fusion.3), channel_id=1, source_target_pairs={{2,0},{3,1},{4,2},{5,3},{6,4},{7,5},{0,6},{1,7},{10,8},{11,9},{12,... | collective-permute-start | bytes 3145736 | tf_op jit(solution)/shard_map/ppermute | solution.py:370
  414.8 16.8 %collective-permute-start.31 = (bf16[128,2048]{1,0:T(8,128)(2,1)S(1)}, bf16[128,2048]{1,0:T(8,128)(2,1)S(1)}, u32[]{:S(2)}, u32[]{:S(2)}) collective-permute-start(bf16[128,2048]{1,0:T(8,128)(2,1)S(1)} %get-tuple-element.440), channel_id=1, source_target_pairs={{0,16},{16,0},{1,17},{17,1},{2,18},{18,2},{3,19},{19,3},{4,20},{20... | collective-permute-start | bytes 1572872 | tf_op jit(solution)/shard_map/ppermute | solution.py:340
  432.7 20.6 %collective-permute-start.33 = (bf16[256,2048]{1,0:T(8,128)(2,1)}, bf16[256,2048]{1,0:T(8,128)(2,1)}, u32[]{:S(2)}, u32[]{:S(2)}) collective-permute-start(bf16[256,2048]{1,0:T(8,128)(2,1)} %pad_maximum_fusion.5), channel_id=1, source_target_pairs={{0,8},{8,0},{1,9},{9,1},{2,10},{10,2},{3,11},{11,3},{4,12},{12,4},... | collective-permute-start | bytes 3145736 | tf_op jit(solution)/shard_map/ppermute | solution.py:335
  433.8 21.8 %collective-permute-start.34 = (bf16[256,2048]{1,0:T(8,128)(2,1)}, bf16[256,2048]{1,0:T(8,128)(2,1)}, u32[]{:S(2)}, u32[]{:S(2)}) collective-permute-start(bf16[256,2048]{1,0:T(8,128)(2,1)} %pad_maximum_fusion.6), channel_id=1, source_target_pairs={{0,8},{8,0},{1,9},{9,1},{2,10},{10,2},{3,11},{11,3},{4,12},{12,4},... | collective-permute-start | bytes 3145736 | tf_op jit(solution)/shard_map/ppermute | solution.py:335
  444.3 54.6 %collective-permute-start.35 = (bf16[256,2048]{1,0:T(8,128)(2,1)}, bf16[256,2048]{1,0:T(8,128)(2,1)}, u32[]{:S(2)}, u32[]{:S(2)}) collective-permute-start(bf16[256,2048]{1,0:T(8,128)(2,1)} %add_convert_fusion.2), channel_id=1, source_target_pairs={{2,0},{3,1},{4,2},{5,3},{6,4},{7,5},{0,6},{1,7},{10,8},{11,9},{12,... | collective-permute-start | bytes 3145736 | tf_op jit(solution)/shard_map/ppermute | solution.py:370
  448.8 204.1 %reduce-scatter.9.cloned.1.call-start = ((), (), s32[]{:S(2)}) async-start(), calls=%async_computation.11 | async-start | bytes 3932160 | tf_op jit(solution)/shard_map/reduce_scatter | solution.py:621
  451.8 42.9 %collective-permute-start.36 = (bf16[512,1536]{1,0:T(8,128)(2,1)}, bf16[512,1536]{1,0:T(8,128)(2,1)}, u32[]{:S(2)}, u32[]{:S(2)}) collective-permute-start(bf16[512,1536]{1,0:T(8,128)(2,1)} %reduce-scatter.7.cloned.1.call-done), channel_id=1, source_target_pairs={{1,0},{0,1},{3,2},{2,3},{5,4},{4,5},{7,6},{6,7},{9,8},{8,9},{11,10... | collective-permute-start | bytes 4718600 | tf_op jit(solution)/shard_map/ppermute | solution.py:370
  505.5 24.6 %collective-permute-start.37 = (bf16[512,2048]{1,0:T(8,128)(2,1)}, bf16[512,2048]{1,0:T(8,128)(2,1)}, u32[]{:S(2)}, u32[]{:S(2)}) collective-permute-start(bf16[512,2048]{1,0:T(8,128)(2,1)} %convolution_convert_fusion.4), channel_id=1, source_target_pairs={{0,8},{8,0},{1,9},{9,1},{2,10},{10,2},{3,11},{11,3},{4,12},{12,4},... | collective-permute-start | bytes 6291464 | tf_op jit(solution)/shard_map/ppermute | solution.py:335
  512.3 16.1 %collective-permute-start.38 = (bf16[256,1152]{1,0:T(8,128)(2,1)}, bf16[256,1152]{1,0:T(8,128)(2,1)}, u32[]{:S(2)}, u32[]{:S(2)}) collective-permute-start(bf16[256,1152]{1,0:T(8,128)(2,1)} %dynamic-slice_convert_fusion.3), channel_id=1, source_target_pairs={{1,0},{0,1},{3,2},{2,3},{5,4},{4,5},{7,6},{6,7},{9,8},{8,9},{11,10... | collective-permute-start | bytes 1769480 | tf_op jit(solution)/shard_map/ppermute | solution.py:370
  517.7 26.4 %collective-permute-start.39 = (bf16[256,2048]{1,0:T(8,128)(2,1)S(1)}, bf16[256,2048]{1,0:T(8,128)(2,1)}, u32[]{:S(2)}, u32[]{:S(2)}) collective-permute-start(bf16[256,2048]{1,0:T(8,128)(2,1)S(1)} %add_convert_fusion.1), channel_id=1, source_target_pairs={{2,0},{3,1},{4,2},{5,3},{6,4},{7,5},{0,6},{1,7},{10,8},{11,9},{12,... | collective-permute-start | bytes 3145736 | tf_op jit(solution)/shard_map/ppermute | solution.py:370
  544.3 16.3 %collective-permute-start.49 = (bf16[256,1152]{1,0:T(8,128)(2,1)S(1)}, bf16[256,1152]{1,0:T(8,128)(2,1)S(1)}, u32[]{:S(2)}, u32[]{:S(2)}) collective-permute-start(bf16[256,1152]{1,0:T(8,128)(2,1)S(1)} %get-tuple-element.646), channel_id=1, source_target_pairs={{1,0},{0,1},{3,2},{2,3},{5,4},{4,5},{7,6},{6,7},{9,8},{8,9},{11,10... | collective-permute-start | bytes 1769480 | tf_op jit(solution)/shard_map/ppermute | solution.py:370
  544.9 28.4 %collective-permute-start.46 = (bf16[256,1152]{1,0:T(8,128)(2,1)S(1)}, bf16[256,1152]{1,0:T(8,128)(2,1)S(1)}, u32[]{:S(2)}, u32[]{:S(2)}) collective-permute-start(bf16[256,1152]{1,0:T(8,128)(2,1)S(1)} %get-tuple-element.647), channel_id=1, source_target_pairs={{1,0},{0,1},{3,2},{2,3},{5,4},{4,5},{7,6},{6,7},{9,8},{8,9},{11,10... | collective-permute-start | bytes 1769480 | tf_op jit(solution)/shard_map/ppermute | solution.py:370
  546.4 38.1 %collective-permute-start.43 = (bf16[256,1152]{1,0:T(8,128)(2,1)S(1)}, bf16[256,1152]{1,0:T(8,128)(2,1)S(1)}, u32[]{:S(2)}, u32[]{:S(2)}) collective-permute-start(bf16[256,1152]{1,0:T(8,128)(2,1)S(1)} %get-tuple-element.648), channel_id=1, source_target_pairs={{1,0},{0,1},{3,2},{2,3},{5,4},{4,5},{7,6},{6,7},{9,8},{8,9},{11,10... | collective-permute-start | bytes 1769480 | tf_op jit(solution)/shard_map/ppermute | solution.py:370
  549.4 36.6 %collective-permute-start.42 = (bf16[512,512]{1,0:T(8,128)(2,1)S(1)}, bf16[512,512]{1,0:T(8,128)(2,1)S(1)}, u32[]{:S(2)}, u32[]{:S(2)}) collective-permute-start(bf16[512,512]{1,0:T(8,128)(2,1)S(1)} %pad_maximum_fusion.17), channel_id=1, source_target_pairs={{2,0},{3,1},{4,2},{5,3},{6,4},{7,5},{0,6},{1,7},{10,8},{11,9},{12,... | collective-permute-start | bytes 1572872 | tf_op jit(solution)/shard_map/ppermute | solution.py:370
  555.4 30.6 %collective-permute-start.41 = (bf16[256,1152]{1,0:T(8,128)(2,1)S(1)}, bf16[256,1152]{1,0:T(8,128)(2,1)S(1)}, u32[]{:S(2)}, u32[]{:S(2)}) collective-permute-start(bf16[256,1152]{1,0:T(8,128)(2,1)S(1)} %convert_add_fusion.11), channel_id=1, source_target_pairs={{2,0},{3,1},{4,2},{5,3},{6,4},{7,5},{0,6},{1,7},{10,8},{11,9},{12,... | collective-permute-start | bytes 1769480 | tf_op jit(solution)/shard_map/ppermute | solution.py:370
  586.9 27.4 %collective-permute-start.44 = (bf16[256,1152]{1,0:T(8,128)(2,1)}, bf16[256,1152]{1,0:T(8,128)(2,1)}, u32[]{:S(2)}, u32[]{:S(2)}) collective-permute-start(bf16[256,1152]{1,0:T(8,128)(2,1)} %add_convert_fusion.7), channel_id=1, source_target_pairs={{2,0},{3,1},{4,2},{5,3},{6,4},{7,5},{0,6},{1,7},{10,8},{11,9},{12,... | collective-permute-start | bytes 1769480 | tf_op jit(solution)/shard_map/ppermute | solution.py:370
  592.2 22.1 %collective-permute-start.45 = (bf16[512,512]{1,0:T(8,128)(2,1)}, bf16[512,512]{1,0:T(8,128)(2,1)}, u32[]{:S(2)}, u32[]{:S(2)}) collective-permute-start(bf16[512,512]{1,0:T(8,128)(2,1)} %fusion.42), channel_id=1, source_target_pairs={{2,0},{3,1},{4,2},{5,3},{6,4},{7,5},{0,6},{1,7},{10,8},{11,9},{12,... | collective-permute-start | bytes 1572872 | tf_op jit(solution)/shard_map/ppermute | solution.py:370
  592.8 60.1 %collective-permute-start.51 = (bf16[768,512]{1,0:T(8,128)(2,1)}, bf16[768,512]{1,0:T(8,128)(2,1)}, u32[]{:S(2)}, u32[]{:S(2)}) collective-permute-start(bf16[768,512]{1,0:T(8,128)(2,1)} %reduce-scatter.11.cloned.1.call-done), channel_id=1, source_target_pairs={{1,0},{0,1},{3,2},{2,3},{5,4},{4,5},{7,6},{6,7},{9,8},{8,9},{11,10... | collective-permute-start | bytes 2359304 | tf_op jit(solution)/shard_map/ppermute | solution.py:370
  594.9 28.4 %collective-permute-start.40 = (bf16[256,2048]{1,0:T(8,128)(2,1)S(1)}, bf16[256,2048]{1,0:T(8,128)(2,1)S(1)}, u32[]{:S(2)}, u32[]{:S(2)}) collective-permute-start(bf16[256,2048]{1,0:T(8,128)(2,1)S(1)} %slice.366), channel_id=1, source_target_pairs={{0,16},{16,0},{1,17},{17,1},{2,18},{18,2},{3,19},{19,3},{4,20},{20... | collective-permute-start | bytes 3145736 | tf_op jit(solution)/shard_map/ppermute | solution.py:340
  615.7 26.1 %collective-permute-start.47 = (bf16[256,1152]{1,0:T(8,128)(2,1)S(1)}, bf16[256,1152]{1,0:T(8,128)(2,1)S(1)}, u32[]{:S(2)}, u32[]{:S(2)}) collective-permute-start(bf16[256,1152]{1,0:T(8,128)(2,1)S(1)} %add_convert_fusion.6), channel_id=1, source_target_pairs={{2,0},{3,1},{4,2},{5,3},{6,4},{7,5},{0,6},{1,7},{10,8},{11,9},{12,... | collective-permute-start | bytes 1769480 | tf_op jit(solution)/shard_map/ppermute | solution.py:370
  621.2 20.6 %collective-permute-start.48 = (bf16[512,512]{1,0:T(8,128)(2,1)S(1)}, bf16[512,512]{1,0:T(8,128)(2,1)S(1)}, u32[]{:S(2)}, u32[]{:S(2)}) collective-permute-start(bf16[512,512]{1,0:T(8,128)(2,1)S(1)} %fusion.43), channel_id=1, source_target_pairs={{2,0},{3,1},{4,2},{5,3},{6,4},{7,5},{0,6},{1,7},{10,8},{11,9},{12,... | collective-permute-start | bytes 1572872 | tf_op jit(solution)/shard_map/ppermute | solution.py:370
  643.0 6.7 collective-permute-start.50
  656.6 4.4 collective-permute-start.52
  665.9 4.8 collective-permute-start.54
  674.6 4.9 collective-permute-start.56
  (145 other events, 1415.6 us)
Sparse Core Ops, SparseCore 0:
  12.3 37.1 all-gather.5
  51.7 46.3 all-gather.7
  100.2 28.5 all-gather.9
  184.9 48.2 all-gather.11
  234.7 28.5 all-gather.13
  356.9 73.7 reduce-scatter.6
  433.4 61.2 reduce-scatter.4
  497.8 40.5 reduce-scatter.10
  541.7 37.9 reduce-scatter.8

commit v3 on v2

--- a/solution.py
+++ b/solution.py
@@ -145,14 +145,12 @@
             hs = range(g * repeat, (g + 1) * repeat)
             queries = jnp.concatenate([query[rows, h * HD : (h + 1) * HD] for h in hs], 0)
             scores = dot_cols(queries, key[:seen, columns]) * (HD**-0.5 * LOG2E)
-            scores = jnp.where(mask, scores, MASK_FILL)
-            largest = jnp.max(scores, -1, keepdims=True)
-            exponent = jnp.exp2(scores - largest)
+            exponent = jnp.exp2(jnp.where(mask, scores, MASK_FILL))
             total = jnp.sum(exponent, -1, keepdims=True)
             result = jnp.dot(
                 exponent.astype(jnp.bfloat16), value[:seen, columns], preferred_element_type=jnp.float32
             ) / total
-            logs = largest + jnp.log2(total)
+            logs = jnp.log2(total)
             for r, h in enumerate(hs):
                 part = result[r * block : (r + 1) * block, :]
                 gate = jax.nn.sigmoid(raw[rows, gate_from + h : gate_from + h + 1])
@@ -400,14 +398,17 @@
     return wide_from(value, step, 0)
 
 
-def all_sum(value, axis):
-    size = lax.axis_size(axis)
-    if size & (size - 1):
-        return lax.psum(value, axis)
-    step = 1
-    while step < size:
-        value = value + swapped(value, axis, step)
-        step = 2 * step
+def all_sum(value):
+    for axis in ("x", "c", "w"):
+        size = lax.axis_size(axis)
+        step = 1
+        while step < size:
+            flips = [step, 2 * step, 3 * step] if 4 * step <= size else [step]
+            moved = [value] + [swapped(value, axis, flip) for flip in flips]
+            while len(moved) > 1:
+                moved = [moved[i] + moved[i + 1] for i in range(0, len(moved), 2)]
+            value = moved[0]
+            step = step * (len(flips) + 1)
     return value
 
 
@@ -433,6 +434,22 @@
             for core in range(2)
         ]
     ).astype(jnp.int32)
+
+
+def near_columns(values):
+    x_size = lax.axis_size("x")
+    x_me, c_me = lax.axis_index("x"), lax.axis_index("c")
+    width = values.shape[1] // (2 * x_size)
+    return jnp.concatenate(
+        [
+            lax.dynamic_slice_in_dim(
+                values, (lax.rem(x_me + x, x_size) * 2 + (c_me ^ core)) * width, width, 1
+            )
+            for core in range(2)
+            for x in range(x_size)
+        ],
+        1,
+    )
 
 
 def pinned(values):
@@ -488,7 +505,6 @@
     norm_two = gains[D : 2 * D]
     head_gains = gains[2 * D :].reshape(2, HD)
     inputs = tokens.astype(wide)
-    normed = norm_rows(inputs, norm_one).astype(low)
     depth = query_weight.shape[0]
     query_width, key_width = query_weight.shape[1], keyvalue_weight.shape[2]
     value_from = query_width + key_width
@@ -503,21 +519,18 @@
         ],
         1,
     ).astype(low)
+    project, tokens_in = tie(project, tokens)
+    normed = norm_rows(tokens_in.astype(wide), norm_one).astype(low)
     group_in = lax.all_gather(normed, ("x", "c"), axis=0, tiled=True)
     output_low = output_weight.astype(low)
     upstream_low = upstream.astype(low)
-    expand_low = jnp.concatenate([expand_weight[0], expand_weight[1]], 1).astype(low)
-    reduce_low = reduce_weight.astype(low)
-    hidden = reduce_low.shape[0]
+    hidden = reduce_weight.shape[0]
 
     def expand_whole(piece):
         return lax.all_gather(piece, ("x", "c"), axis=0, tiled=True)
 
     def reduce_whole(piece):
         return lax.all_gather(piece, ("x", "c"), axis=1, tiled=True)
-
-    expand_all = [expand_whole(expand_low)]
-    reduce_all = [reduce_whole(reduce_low)]
 
     group_size = group_in.shape[0]
     places = positions(segment_ids)
@@ -529,7 +542,14 @@
 
     row = project
     project_pieces = []
-    for _ in range(outer - 1):
+    masters_in = (expand_weight, reduce_weight)
+    for step in range(outer - 1):
+        if step == 1:
+            row, masters_in = tie(row, masters_in)
+            expand_low = jnp.concatenate([masters_in[0][0], masters_in[0][1]], 1).astype(low)
+            reduce_low = masters_in[1].astype(low)
+            expand_all = [expand_whole(expand_low)]
+            reduce_all = [reduce_whole(reduce_low)]
         moved, across, starts, cosine, sine = tie(
             wide_from(row, 1, 0), inner_gather(row), starts, cosine, sine
         )
@@ -537,44 +557,37 @@
         row = moved
     row, output_low, upstream_low = tie(row, output_low, upstream_low)
     output_rows = [output_low] + [wide_from(output_low, i, 0) for i in range(1, outer)]
-    sides = [expand_low[:, :hidden], expand_low[:, hidden:]]
-    across, output_rows, upstream_low, sides = tie(
-        inner_gather(row), output_rows, upstream_low, sides
-    )
+    across, upstream_low, expand_low = tie(inner_gather(row), upstream_low, expand_low)
     project_pieces.append(across)
-    output_pieces = [inner_gather(piece) for piece in output_rows]
-    upstream_parts = [upstream_low, outer_shift(upstream_low, 1)]
     project_all = assemble(project_pieces, 0)
     raw = jnp.dot(group_in, project_all, preferred_element_type=wide)
-    raw, output_pieces, upstream_parts, sides = tie(raw, output_pieces, upstream_parts, sides)
-    gate_pieces = inner_gather(sides[0])
+    raw, output_rows, expand_low, upstream_low = tie(raw, output_rows, expand_low, upstream_low)
+    upstream_parts = [upstream_low, outer_shift(upstream_low, 1)]
+    output_pieces = [inner_gather(piece) for piece in output_rows]
+    kept = attend(near, raw, starts, cosine, sine, head_gains, heads, groups)
+    kept, output_pieces, upstream_parts, expand_low = tie(
+        kept, output_pieces, upstream_parts, expand_low
+    )
+    query, key, value, attended, total_log, gated, gated_near = kept
+    expand_pieces = inner_gather(expand_low)
     upstream_parts.append(outer_shift(upstream_parts[-1], 1))
     output_all = assemble(output_pieces, 1)
-    kept = attend(near, raw, starts, cosine, sine, head_gains, heads, groups)
-    kept, output_all, upstream_parts, gate_pieces, sides = tie(
-        kept, output_all, upstream_parts, gate_pieces, sides
-    )
-    up_pieces = inner_gather(sides[1])
-    upstream_parts.append(outer_shift(upstream_parts[-1], 1))
-    query, key, value, attended, total_log, gated, gated_near = kept
     half = gated.shape[0] // 2
 
     def projected(rows):
         return jnp.dot(rows, output_all, preferred_element_type=wide)
 
     received = swapped(projected(gated_near[half:]).astype(low), "c", 1)
-    attention = projected(gated_near[:half]) + received.astype(wide)
-    attention = by_x(attention)
+    attention = by_x(projected(gated_near[:half]) + received.astype(wide))
     split = attention[0].shape[0] // 2
     first = ring_scatter([part[:split] for part in attention], "x")
     second = ring_scatter([part[split:] for part in attention], "x")
-    first, up_pieces, reduce_low, upstream_parts = tie(
-        first, up_pieces, reduce_low, upstream_parts
-    )
-    expand_all = expand_all + [
-        expand_whole(jnp.concatenate(pair, 1)) for pair in zip(gate_pieces[1:], up_pieces[1:])
-    ]
+    first, upstream_parts, expand_pieces, reduce_low = tie(
+        first, upstream_parts, expand_pieces, reduce_low
+    )
+    expand_all = expand_all + [expand_whole(piece) for piece in expand_pieces[1:]]
     reduce_pieces = inner_gather(reduce_low)
+    upstream_parts.append(outer_shift(upstream_parts[-1], 1))
     attention = jnp.concatenate([first, second], 0)
     residual = inputs + attention
     mixed = norm_rows(residual, norm_two).astype(low)
@@ -594,102 +607,120 @@
 
     done = {}
     grad_sums = {}
-    output_sums = {}
 
     def begin(k):
         done[k, 0] = hidden_part(k, 0)
         grad_sums[k] = mixed_back(done[k, 0], 0)
-        output_sums[k] = lowered(done[k, 0], 0)
 
     def rest(k):
         for j in range(1, inner):
             done[k, j] = hidden_part(k, j)
             grad_sums[k] = grad_sums[k] + mixed_back(done[k, j], j)
 
+    def summed(k):
+        total = lowered(done[k, 0], 0)
+        for j in range(1, inner):
+            total = total + lowered(done[k, j], j)
+        return total.astype(low) if k else total
+
     def joined(which, j):
         return jnp.concatenate([done[k, j][which] for k in range(outer)], 0)
 
-    def expand_back(j):
-        return lax.psum_scatter(
-            contract_rows(mixed_all, joined(1, j)).astype(low),
-            ("x", "c"),
-            scatter_dimension=0,
-            tiled=True,
-        )
-
-    def reduce_back(j):
-        return lax.psum_scatter(
-            contract_rows(joined(0, j), upstream_all).astype(low),
-            ("x", "c"),
-            scatter_dimension=1,
-            tiled=True,
-        )
+    def expand_far(j):
+        return contract_rows(mixed_near[:, D // 2 :], joined(1, j)).astype(low)
+
+    def expand_term(j, x, far):
+        rows = slice(x * D // head_devices, (x + 1) * D // head_devices)
+        return contract_rows(mixed_near[:, rows], joined(1, j)) + far[rows].astype(wide)
+
+    def reduce_far(j):
+        return contract_rows(joined(0, j), upstream_near[:, D // 2 :]).astype(low)
+
+    def reduce_term(j, x, far):
+        columns = slice(x * D // head_devices, (x + 1) * D // head_devices)
+        return contract_rows(joined(0, j), upstream_near[:, columns]) + far[:, columns].astype(wide)
+
+    def x_finish(term, j, far, moved):
+        for step in range(1, x_size):
+            total = term(j, (step + 1) % x_size, far) + moved.astype(wide)
+            if step + 1 < x_size:
+                moved = hop(total.astype(low), "x")
+        return total
 
     mixed_parts = [mixed]
     moved = outer_shift(mixed, 1)
     begin(0)
-    moved, done, grad_sums, output_sums, reduce_pieces = tie(
-        moved, done, grad_sums, output_sums, reduce_pieces
+    moved, done, grad_sums, reduce_pieces, upstream_parts = tie(
+        moved, done, grad_sums, reduce_pieces, upstream_parts
     )
     reduce_all = reduce_all + [reduce_whole(piece) for piece in reduce_pieces[1:]]
     mixed_parts.append(moved)
     moved = outer_shift(moved, 1)
     begin(1)
-    moved, done, grad_sums, output_sums = tie(moved, done, grad_sums, output_sums)
+    upstream_all = jnp.concatenate(upstream_parts, 0)
+    moved, done, grad_sums, upstream_all = tie(moved, done, grad_sums, upstream_all)
     mixed_parts.append(moved)
     moved = outer_shift(moved, 1)
     begin(2)
     rest(1)
-    moved, done, grad_sums, output_sums = tie(moved, done, grad_sums, output_sums)
+    upstream_near = near_columns(upstream_all)
+    moved, done, grad_sums, upstream_near = tie(moved, done, grad_sums, upstream_near)
     mixed_parts.append(moved)
     moved = outer_shift(grad_sums[1].astype(low), 1)
     rest(2)
     begin(3)
-    moved, done, grad_sums, output_sums = tie(moved, done, grad_sums, output_sums)
+    mixed_all = jnp.concatenate(mixed_parts, 0)
+    moved, done, grad_sums, mixed_all, mixed_parts = tie(
+        moved, done, grad_sums, mixed_all, mixed_parts
+    )
     moved = outer_shift((grad_sums[2] + moved.astype(wide)).astype(low), 1)
     rest(3)
     rest(0)
-    mixed_all = jnp.concatenate(mixed_parts, 0)
-    upstream_all = jnp.concatenate(upstream_parts, 0)
-    moved, done, grad_sums, output_sums, mixed_all, upstream_all = tie(
-        moved, done, grad_sums, output_sums, mixed_all, upstream_all
-    )
-    sent = (grad_sums[3] + moved.astype(wide)).astype(low)
-    early, late = outer_shift(sent[:split], 1), outer_shift(sent[split:], 1)
-    for k in range(outer):
-        for j in range(1, inner):
-            output_sums[k] = output_sums[k] + lowered(done[k, j], j)
-    early, done, upstream_all, mixed_all = tie(early, done, upstream_all, mixed_all)
-    expand_wide = [None] * inner
-    reduce_wide = [None] * inner
-    for j in range(1, inner):
-        expand_wide[j] = expand_back(j)
-    late, done, upstream_all, mixed_all = tie(late, done, upstream_all, mixed_all)
-    moved = jnp.concatenate([early, late], 0)
+    moved, done, grad_sums, mixed_all, upstream_all = tie(
+        moved, done, grad_sums, mixed_all, upstream_all
+    )
+    moved = outer_shift((grad_sums[3] + moved.astype(wide)).astype(low), 1)
+    late = range(1, inner)
+    mixed_near = near_columns(mixed_all)
+    expand_fars = [None] + [expand_far(j) for j in late]
+    output_sums = {1: summed(1)}
+    expand_own = contract_rows(mixed_all, joined(1, 0)).astype(low)
+    moved, done, mixed_near, expand_fars, output_sums, upstream_near, expand_own, upstream_all = tie(
+        moved, done, mixed_near, expand_fars, output_sums, upstream_near, expand_own, upstream_all
+    )
     mixed_grad = grad_sums[0] + moved.astype(wide)
     _, second_back = jax.vjp(norm_rows, residual, norm_two)
     residual_from, two_grad = second_back(mixed_grad)
     residual_grad = upstream + residual_from
-    residual_low = residual_grad.astype(low)
-    output_total = outer_shift(output_sums[1].astype(low), 1)
-    early_row = ring_gather(residual_low[:split], "x")
-    late_row = ring_gather(residual_low[split:], "x")
-    early_row, done, upstream_all, mixed_all = tie(early_row, done, upstream_all, mixed_all)
-    for j in range(1, inner):
-        reduce_wide[j] = reduce_back(j)
-    expand_wide[0] = expand_back(0)
-    late_row, output_total, done, upstream_all = tie(late_row, output_total, done, upstream_all)
-    residual_row = [jnp.concatenate(pair, 0) for pair in zip(early_row, late_row)]
-    residual_all = jnp.concatenate(
-        residual_row + [swapped(piece, "c", 1) for piece in residual_row], 0
-    )
+    residual_row = ring_gather(residual_grad.astype(low), "x")
+    output_total = outer_shift(output_sums[1], 1)
+    expand_fars = [None] + [swapped(expand_fars[j], "c", 1) for j in late]
+    expand_lead = [None] + [
+        expand_term(j, 1 % x_size, expand_fars[j]).astype(low) for j in late
+    ]
+    reduce_fars = [None] + [reduce_far(j) for j in late]
+    output_sums[2] = summed(2)
+    output_sums[3] = summed(3)
+    residual_row, output_total, expand_fars, expand_lead, reduce_fars, done, output_sums = tie(
+        residual_row, output_total, expand_fars, expand_lead, reduce_fars, done, output_sums
+    )
+    residual_far = [swapped(piece, "c", 1) for piece in residual_row]
+    reduce_fars = [None] + [swapped(reduce_fars[j], "c", 1) for j in late]
+    expand_moved = [None] + [hop(expand_lead[j], "x") for j in late]
+    residual_all = jnp.concatenate(residual_row + residual_far, 0)
+    residual_all, reduce_fars, done = tie(residual_all, reduce_fars, done)
     slots = wide_slots()
 
     def wide_parts(whole, axis, i):
         return [lax.dynamic_slice_in_dim(whole, slot * depth, depth, axis) for slot in slots[i]]
 
+    order = [(step + 1) % outer for step in range(outer)]
+
+    def output_rows_of(i):
+        return jnp.concatenate(wide_parts(output_grad, 1, i), 1)
+
     gated_grad = contract_cols(residual_all, output_all)
-    output_total = outer_shift((output_sums[2] + output_total.astype(wide)).astype(low), 1)
+    output_total = outer_shift(output_sums[2] + output_total, 1)
     back = attend_back(
         near,
         gated_grad,
@@ -702,62 +733,99 @@
         heads,
         groups,
     )
-    expand_both = inner_scatter([part.astype(wide) for part in expand_wide])
-    back, output_total, expand_both, done, residual_all = tie(
-        back, output_total, expand_both, done, residual_all
-    )
+    back, output_total, done, residual_all, expand_moved, expand_own, upstream_all = tie(
+        back, output_total, done, residual_all, expand_moved, expand_own, upstream_all
+    )
+    expand_own = lax.psum_scatter(expand_own, ("x", "c"), scatter_dimension=0, tiled=True)
     low_grads, low_near, head_gain_grads = back
-    output_total = outer_shift((output_sums[3] + output_total.astype(wide)).astype(low), 1)
-    project_grad = pinned(contract_rows(group_in, low_grads))
-    project_wide = [None] * outer
-    order = [(step + 1) % outer for step in range(outer)]
-    project_wide[order[0]] = inner_scatter(wide_parts(project_grad, 0, order[0]))
-    output_grad = contract_rows(gated_near, residual_all)
-
-    def output_rows_of(i):
-        return jnp.concatenate(wide_parts(output_grad, 1, i), 1)
 
     def normed_back(rows):
         return contract_cols(rows, project_all)
 
-    received = swapped(normed_back(low_near[half:]).astype(low), "c", 1)
-    normed_grad = normed_back(low_near[:half]) + received.astype(wide)
-    normed_grad, project_wide[order[0]], project_grad, output_total = tie(
-        normed_grad, project_wide[order[0]], project_grad, output_total
-    )
-    normed_grad = ring_scatter(by_x(normed_grad), "x")
-    project_total = project_wide[order[0]]
+    output_total = outer_shift(output_sums[3] + output_total, 1)
+    project_grad = pinned(contract_rows(group_in, low_grads))
+    project_grad, low_near, done, upstream_all, residual_all, expand_moved, reduce_fars = tie(
+        project_grad, low_near, done, upstream_all, residual_all, expand_moved, reduce_fars
+    )
+
+    def spread(parts):
+        total = parts[0]
+        for part in parts[1:]:
+            total = (part.astype(wide) + wide_from(total, 0, 1).astype(wide)).astype(low)
+        return wide_from(total, 0, 1)
+
+    project_total = inner_scatter(wide_parts(project_grad, 0, order[0]))
+    output_grad = contract_rows(gated_near, residual_all)
     output_part = output_rows_of(order[0])
-    for i in order[1:]:
-        moved, output_new, across = tie(
-            outer_shift(project_total.astype(low), 1),
-            outer_shift(output_part.astype(low), 1),
-            inner_scatter(wide_parts(project_grad, 0, i)),
-        )
+    expand_wide = [
+        x_finish(expand_term, j, expand_fars[j], expand_moved[j]) for j in late
+    ]
+    reduce_lead = [None] + [
+        reduce_term(j, 1 % x_size, reduce_fars[j]).astype(low) for j in late
+    ]
+    middle = len(expand_wide[0]) // 2
+    expand_early = [part[:middle].astype(low) for part in expand_wide]
+    expand_late = [part[middle:].astype(low) for part in expand_wide]
+    normed_far = normed_back(low_near[half:]).astype(low)
+    state = (project_total, output_part, output_grad, expand_early, expand_late, reduce_lead)
+    state, project_grad, low_near, done, upstream_all, normed_far, output_total = tie(
+        state, project_grad, low_near, done, upstream_all, normed_far, output_total
+    )
+    project_total, output_part, output_grad, expand_early, expand_late, reduce_lead = state
+    for step, i in enumerate(order[1:]):
+        moved = outer_shift(project_total.astype(low), 1)
+        across = inner_scatter(wide_parts(project_grad, 0, i))
+        output_new = outer_shift(output_part.astype(low), 1)
+        if step == 0:
+            normed_far = swapped(normed_far, "c", 1)
+            reduce_moved = [None] + [hop(reduce_lead[j], "x") for j in late]
+            expand_early = spread(expand_early)
+            normed_grad = normed_back(low_near[:half]) + normed_far.astype(wide)
+            reduce_own = contract_rows(joined(0, 0), upstream_all).astype(low)
+            reduce_wide = ()
+        if step == 1:
+            reduce_own = lax.psum_scatter(reduce_own, ("x", "c"), scatter_dimension=1, tiled=True)
+            normed_grad = ring_scatter(by_x(normed_grad), "x")
+            expand_late = spread(expand_late)
+            reduce_wide = [
+                x_finish(reduce_term, j, reduce_fars[j], reduce_moved[j]).astype(low) for j in late
+            ]
+        if step == 2:
+            reduce_wide = spread(reduce_wide)
+        state = (moved, across, project_grad, output_new, output_grad, reduce_wide)
+        if step == 0:
+            state, expand_early, reduce_own, reduce_moved, expand_late, normed_grad = tie(
+                state, expand_early, reduce_own, reduce_moved, expand_late, normed_grad
+            )
+        elif step == 1:
+            state, expand_own, expand_late = tie(state, expand_own, expand_late)
+        else:
+            state, normed_grad = tie(state, normed_grad)
+        moved, across, project_grad, output_new, output_grad, reduce_wide = state
         project_total = across + moved.astype(wide)
         output_part = output_rows_of(i) + output_new.astype(wide)
+    output_part = inner_scatter([output_part[:, j * depth : (j + 1) * depth] for j in range(inner)])
+    expand_both = jnp.concatenate([expand_early, expand_late], 0).astype(wide)
+    expand_both = expand_both + expand_own.astype(wide)
+    reduce_part = reduce_wide.astype(wide) + reduce_own.astype(wide)
     project_part = pinned(project_total)
-    output_part = inner_scatter([output_part[:, j * depth : (j + 1) * depth] for j in range(inner)])
-    reduce_wide[0] = reduce_back(0)
-    block_output = (residual + output_sums[0] + output_total.astype(wide)).astype(low)
+    block_output = (residual + summed(0) + output_total.astype(wide)).astype(low)
     _, first_back = jax.vjp(norm_rows, inputs, norm_one)
     input_from, one_grad = first_back(normed_grad)
     input_grad = residual_grad + input_from
-    reduce_part = inner_scatter([part.astype(wide) for part in reduce_wide])
     expand_part = jnp.stack([expand_both[:, :hidden], expand_both[:, hidden:]])
     query_part = project_part[:, :query_width]
     keyvalue_part = jnp.stack(
         [project_part[:, query_width:value_from], project_part[:, value_from:gate_from]]
     )
-    headgate_part = project_part[:, gate_from : gate_from + heads]
+    headgate_part = pinned(project_part[:, gate_from : gate_from + heads].T)
     gain_partial = jnp.concatenate([one_grad, two_grad, head_gain_grads.reshape(-1)])
     parts = (query_part, keyvalue_part, headgate_part, output_part, expand_part, reduce_part)
     squares = jnp.zeros((), jnp.float32)
     for part_grad in parts:
         squares = squares + jnp.sum(part_grad * part_grad)
     totals = jnp.concatenate([gain_partial, squares[None]])
-    for axis in ("c", "x", "w"):
-        totals = all_sum(totals, axis)
+    totals = all_sum(totals)
     gains_grad, square_total = totals[:-1], totals[-1]
     grad_norm = jnp.sqrt(square_total + jnp.sum(gains_grad * gains_grad))
     clip = CLIP_NORM / jnp.maximum(grad_norm, CLIP_NORM)
@@ -765,7 +833,7 @@
     masters = (
         query_weight,
         keyvalue_weight,
-        headgate_weight,
+        headgate_weight.T,
         output_weight,
         expand_weight,
         reduce_weight,
@@ -773,7 +841,7 @@
     states = (
         (query_first, query_second),
         (keyvalue_first, keyvalue_second),
-        (headgate_first, headgate_second),
+        (headgate_first.T, headgate_second.T),
         (output_first, output_second),
         (expand_first, expand_second),
         (reduce_first, reduce_second),
@@ -789,7 +857,8 @@
             rate,
             WEIGHT_DECAY,
         )
-        results = results + [updated, first_new, second_new, updated.astype(low)]
+        made = [updated, first_new, second_new, updated.astype(low)]
+        results = results + ([item.T for item in made] if index == 2 else made)
     return tuple(results)
 
 

time: 724 us -> 629 us (0.87)
  waiting for transfers between devices: 233 us -> 174 us
  starting transfers between devices: 98.8 us -> 79.2 us
    ppermute x43 -> x42, waiting for transfers between devices: 162 us -> 94.5 us  [wide_from(): return lax.ppermute(value, 'w', pairs)]
    ppermute x43 -> x42, starting transfers between devices: 87.6 us -> 69.2 us  [wide_from(): return lax.ppermute(value, 'w', pairs)]
    ppermute x5 -> x6, waiting for transfers between devices: 50.2 us -> 67.5 us  [hop(): return lax.ppermute(value, axis, [(i, (i - 1) % size) for i in range(size)])]
    convert_element_type x18 -> x14, other arithmetic: 42.8 us -> 31.3 us  [the longest x5 17.7 us: body(): made = [updated, first_new, second_new, updated.astype(low)]]
    reduce_scatter x4 -> x2, waiting for transfers between devices: 8.93 us -> 0.04 us  [the longest x1 0.02 us: body(): lax.psum_scatter(reduce_own, ('x', 'c'), scatter_dimension=1, tiled=True)]
    dot_general x6 -> x10, matrix products: 36.4 us -> 41.1 us  [contract_rows(): lax.dot_general(left, right, (((0,), (0,)), ((), ())), preferred_element_...]
    unnamed x296 -> x271, local copies, waits for them, and re-layouts: 17.3 us -> 16 us
  transfers between devices with their start and end apart: 66 -> 67, of which waited for: 31 -> 35; matrix products, arithmetic and copies ran while one was open for 37% -> 43% of each run, Pallas kernels for 6% -> 6%
where the time goes in v3:
time: 629 us; the launch traced here: 621 us
  waiting for transfers between devices  174 us (28%)
  matrix products  166 us (26%)
  other arithmetic  94.1 us (15%)
  starting transfers between devices  79.2 us (13%)
  local copies, waits for them, and re-layouts  49.1 us (8%)
  Pallas kernels  35.8 us (6%)
  between operations  23.2 us (4%)
    ppermute x42, waiting for transfers between devices, wide_from(): return lax.ppermute(value, 'w', pairs)  94.5 us
    ppermute x42, starting transfers between devices, wide_from(): return lax.ppermute(value, 'w', pairs)  69.2 us
    ppermute x6, waiting for transfers between devices, hop(): return lax.ppermute(value, axis, [(i, (i - 1) % size) for i in range(size)])  67.5 us
    dot_general x19, matrix products, contract_cols(): lax.dot_general(left, right, (((1,), (1,)), ((), ())), preferred_element_...  66.4 us
    dot_general x10, matrix products, contract_rows(): lax.dot_general(left, right, (((0,), (0,)), ((), ())), preferred_element_...  41.1 us
    dot_general x8, matrix products, hidden_part(): both = jnp.dot(mixed_parts[k], expand_all[j], preferred_element_type=wide)  32.1 us
    pallas_call x1, Pallas kernels, attend_back(): pl.pallas_call(functools.partial(attend_back_kernel, heads, groups, lengt...  21.7 us
    convert_element_type x5, other arithmetic, body(): made = [updated, first_new, second_new, updated.astype(low)]  17.7 us
  transfers between devices with their start and end apart: 67, of which 35 were waited for; matrix products, arithmetic and copies ran while one was open for 43% of the time, Pallas kernels for 6%

profile of v3, /device:TPU:0, one launch (start us, length us, event | category | flops | bytes accessed | tf_op | source)
XLA Modules:
  0.0 621.2 jit_solution(13635568984474310495)
XLA Ops:
  13.1 3.0 collective-permute-start.1
  16.1 3.6 collective-permute-start
  24.8 4.7 collective-permute-done.1
  34.4 4.4 collective-permute-start.2
  40.1 7.9 %collective-permute-done.3 = bf16[256,1152]{1,0:T(8,128)(2,1)S(1)} collective-permute-done((bf16[256,1152]{1,0:T(8,128)(2,1)}, bf16[256,1152]{1,0:T(8,128)(2,1)S(1)}, u32[]{:S(2)}, u32[]{:S(2)}) %collective-permute-start.3) | collective-permute-done | bytes 589856 | tf_op jit(solution)/shard_map/ppermute | solution.py:368
  51.8 4.2 collective-permute-start.4
  62.9 5.1 collective-permute-done.4
  68.9 4.8 collective-permute-start.8
  79.7 10.3 %fusion.152.raw = f32[1024,1152]{1,0:T(8,128)} fusion(bf16[1024,2048]{1,0:T(8,128)(2,1)} %all-gather.6.cloned.1.call-done, bf16[2048,1152]{1,0:T(8,128)(2,1)} %constant_dynamic-update-slice_fusion.8), kind=kOutput, calls=%fused_computation.336 | convolution fusion | flops 4831838208 | bytes 13631488 | tf_op jit(solution)/shard_map/dot_general | solution.py:563
  90.0 4.4 collective-permute-start.14
  101.7 14.2 %shard_map.481 = (bf16[1024,512]{1,0:T(8,128)(2,1)}, bf16[1024,256]{1,0:T(8,128)(2,1)}, bf16[1024,256]{1,0:T(8,128)(2,1)}, f32[1024,512]{1,0:T(8,128)}, f32[1024...) custom-call(s32[4]{0:T(128)} %pad_add_fusion.slots, f32[1024,1152]{1,0:T(8,128)} %fusion.152.raw, ...), custom_call_target="tpu_custom_call" | custom-call | flops 2147483648 | bytes 9961472 | tf_op jit(solution)/shard_map/pallas_call | solution.py:171
  124.1 3.1 collective-permute-done.15
  131.6 11.7 %collective-permute-done.16 = bf16[128,2048]{1,0:T(8,128)(2,1)S(1)} collective-permute-done((bf16[128,2048]{1,0:T(8,128)(2,1)S(1)}, bf16[128,2048]{1,0:T(8,128)(2,1)S(1)}, u32[]{:S(2)}, u32[]{:S(2)}) %collective-permute-start.16) | collective-permute-done | bytes 524320 | tf_op jit(solution)/shard_map/ppermute | solution.py:338
  143.4 10.4 %collective-permute-done.19 = bf16[128,2048]{1,0:T(8,128)(2,1)S(1)} collective-permute-done((bf16[128,2048]{1,0:T(8,128)(2,1)S(1)}, bf16[128,2048]{1,0:T(8,128)(2,1)S(1)}, u32[]{:S(2)}, u32[]{:S(2)}) %collective-permute-start.19) | collective-permute-done | bytes 524320 | tf_op jit(solution)/shard_map/ppermute | solution.py:338
  155.6 4.2 collective-permute-done.18
  165.7 2.7 collective-permute-start.22
  168.4 6.8 %fusion.153 = f32[256,1536]{1,0:T(8,128)} fusion(bf16[256,2048]{1,0:T(8,128)(2,1)S(1)} %multiply_convert_fusion, bf16[2048,1536]{1,0:T(8,128)(2,1)} %all-gather.8.cloned.1.call-done), kind=kOutput, calls=%fused_computation.337 | convolution fusion | flops 1610612736 | bytes 8912896 | tf_op jit(solution)/shard_map/dot_general | solution.py:596
  175.3 4.9 multiply_convert_fusion.23
  181.0 3.1 fusion.134
  184.2 6.3 %collective-permute-done.20 = bf16[256,2048]{1,0:T(8,128)(2,1)} collective-permute-done((bf16[256,2048]{1,0:T(8,128)(2,1)S(1)}, bf16[256,2048]{1,0:T(8,128)(2,1)}, u32[]{:S(2)}, u32[]{:S(2)}) %collective-permute-start.20) | collective-permute-done | bytes 1048608 | tf_op jit(solution)/shard_map/ppermute | solution.py:368
  190.5 20.0 %collective-permute-done.22 = bf16[256,2048]{1,0:T(8,128)(2,1)} collective-permute-done((bf16[256,2048]{1,0:T(8,128)(2,1)}, bf16[256,2048]{1,0:T(8,128)(2,1)}, u32[]{:S(2)}, u32[]{:S(2)}) %collective-permute-start.22) | collective-permute-done | bytes 1048608 | tf_op jit(solution)/shard_map/ppermute | solution.py:368
  210.5 3.2 collective-permute-start.23
  213.7 5.0 fusion.154
  218.8 2.8 multiply_convert_fusion.20
  224.9 3.1 fusion.133
  228.0 6.1 collective-permute-done.23
  234.1 4.5 collective-permute-start.24
  239.1 3.0 fusion.156
  242.2 3.3 multiply_convert_fusion.14
  248.8 3.1 fusion.131
  251.9 6.1 fusion.155
  258.0 4.8 multiply_convert_fusion.17
  266.2 3.2 fusion.157
  269.4 3.5 multiply_convert_fusion.11
  275.6 3.2 fusion.158
  278.8 3.4 multiply_convert_fusion.8
  292.3 3.3 multiply_convert_fusion.5
  299.0 3.0 fusion.160
  302.1 3.3 multiply_convert_fusion.2
  311.6 3.0 collective-permute-start.27
  316.7 9.0 %convolution_convert_fusion = bf16[2048,1536]{1,0:T(8,128)(2,1)} fusion(bf16[1024,2048]{1,0:T(8,128)(2,1)S(1)} %pad_maximum_fusion.2, bf16[256,1536]{1,0:T(8,128)(2,1)S(1)} %pad_maximum_fusion.13, bf16[256,1536]{1,0:T(8,128)(2,1)S(1)} %copy-done.78, bf16[256,1536]{1,0:T(8,128)(2,1)S(1)} %copy-done.77, bf16[256,1536]{1,0:T(8,128)(2,1)S(1)} %copy-done.74), kind=kOutput, calls=%fused_computation | convolution fusion | flops 6458179584 | bytes 13631488 | tf_op jit(solution)/shard_map/dot_general | solution.py:50
  325.7 3.1 fusion.161
  332.9 3.5 convolution_convert_fusion.1
  346.2 3.0 fusion.57
  352.4 12.7 %collective-permute-done.28 = bf16[256,2048]{1,0:T(8,128)(2,1)S(1)} collective-permute-done((bf16[256,2048]{1,0:T(8,128)(2,1)S(1)}, bf16[256,2048]{1,0:T(8,128)(2,1)S(1)}, u32[]{:S(2)}, u32[]{:S(2)}) %collective-permute-start.28) | collective-permute-done | bytes 1048608 | tf_op jit(solution)/shard_map/ppermute | solution.py:338
  375.8 3.7 fusion.164.gated_grad
  379.5 21.7 %shard_map.482 = (bf16[1024,1152]{1,0:T(8,128)(2,1)}, bf16[1024,1152]{1,0:T(8,128)(2,1)}, f32[2,128]{1,0:T(2,128)}) custom-call(s32[4]{0:T(128)} %pad_add_fusion.slots, f32[1024,512]{1,0:T(8,128)} %fusion.164.gated_grad, f32[1024,1152]{1,0:T(8,128)} %fusion.152.raw, s32[1024,1]{1,0:T(8,128)} %subtract_subtract_fusion.start, ...), custom_call_target="tpu_custom_call" | custom-call | flops 5368709120 | bytes 13369344 | tf_op jit(solution)/shard_map/pallas_call | solution.py:292
  401.1 2.8 collective-permute-done.35
  407.9 8.0 %fusion.165 = f32[2048,1152]{1,0:T(8,128)S(1)} fusion(bf16[1024,2048]{1,0:T(8,128)(2,1)} %all-gather.6.cloned.1.call-done, bf16[1024,1152]{1,0:T(8,128)(2,1)S(1)} %copy-done.130), kind=kOutput, calls=%fused_computation.349 | convolution fusion | flops 4831838208 | bytes 15990784 | tf_op jit(solution)/shard_map/dot_general | solution.py:50
  426.1 6.6 %convolution_convert_fusion.3 = bf16[512,2048]{1,0:T(8,128)(2,1)} fusion(bf16[2048,1152]{1,0:T(8,128)(2,1)} %constant_dynamic-update-slice_fusion.8, bf16[1024,1152]{1,0:T(8,128)(2,1)S(1)} %copy-done.129), kind=kOutput, calls=%fused_computation.57 | convolution fusion | flops 2416967680 | bytes 7995392 | tf_op jit(solution)/shard_map/dot_general | solution.py:56
  432.8 3.7 fusion.33
  446.1 5.1 convolution_convert_fusion.2
  451.3 6.7 %collective-permute-done.39 = bf16[256,1152]{1,0:T(8,128)(2,1)} collective-permute-done((bf16[256,1152]{1,0:T(8,128)(2,1)}, bf16[256,1152]{1,0:T(8,128)(2,1)}, u32[]{:S(2)}, u32[]{:S(2)}) %collective-permute-start.39) | collective-permute-done | bytes 589856 | tf_op jit(solution)/shard_map/ppermute | solution.py:368
  460.7 8.3 %convert_add_fusion = f32[512,2048]{1,0:T(8,128)} fusion(bf16[512,2048]{1,0:T(8,128)(2,1)} %collective-permute-done.43, bf16[2048,1152]{1,0:T(8,128)(2,1)} %constant_dynamic-update-slice_fusion.8, bf16[1024,1152]{1,0:T(8,128)(2,1)} %get-tuple-element.543), kind=kOutput, calls=%fused_computation.7 | convolution fusion | flops 2418016256 | bytes 12189696 | tf_op jit(solution)/shard_map/dot_general | solution.py:56
  469.0 4.9 collective-permute-done.41
  481.7 3.4 collective-permute-start.44
  492.0 3.1 collective-permute-done.45
  497.7 27.5 %collective-permute-done.52 = bf16[256,2048]{1,0:T(8,128)(2,1)S(1)} collective-permute-done((bf16[256,2048]{1,0:T(8,128)(2,1)S(1)}, bf16[256,2048]{1,0:T(8,128)(2,1)S(1)}, u32[]{:S(2)}, u32[]{:S(2)}) %collective-permute-start.52) | collective-permute-done | bytes 1048608 | tf_op jit(solution)/shard_map/ppermute | solution.py:338
  538.2 6.4 %collective-permute-done.49 = bf16[256,1152]{1,0:T(8,128)(2,1)S(1)} collective-permute-done((bf16[256,1152]{1,0:T(8,128)(2,1)S(1)}, bf16[256,1152]{1,0:T(8,128)(2,1)S(1)}, u32[]{:S(2)}, u32[]{:S(2)}) %collective-permute-start.49) | collective-permute-done | bytes 589856 | tf_op jit(solution)/shard_map/ppermute | solution.py:368
  546.0 4.6 collective-permute-done.50
  550.6 3.1 collective-permute-done.51
  574.0 3.1 fusion.167
  599.2 7.4 %fusion.137 = (bf16[2,512,768]{2,1,0:T(8,128)(2,1)}, f32[2,512,768]{2,1,0:T(8,128)}, f32[2,512,768]{2,1,0:T(8,128)}, f32[2,512,768]{2,1,0:T(8,128)}) fusion(f32[2,512,768]{2,1,0:T(8,128)S(1)} %copy-done.20, f32[]{:T(128)S(6)} %div.205, f32[1,512,768]{2,1,0:T(8,128)S(1)} %copy-done.18, f32[1,512,768]{2,1,0:T(8,128)S(1)} %copy-done.16, ...), kind=kLoop, calls=%fused_computation.327 | loop fusion | flops 14155776 | bytes 23592964 | tf_op jit(solution)/shard_map/convert_element_type | solution.py:860
  609.4 3.4 fusion.135
  (533 shorter events, 222.4 us)
Async XLA Ops:
  7.2 72.5 %all-gather.6.cloned.1.call-start = ((), (), s32[]{:S(2)}) async-start(), calls=%async_computation.2 | async-start | bytes 5242880 | tf_op jit(solution)/shard_map/all_gather | solution.py:524
  13.0 155.4 %all-gather.8.cloned.1.call-start = ((), (), s32[]{:S(2)}) async-start(), calls=%async_computation.3 | async-start | bytes 7864320 | tf_op jit(solution)/shard_map/all_gather | solution.py:530
  13.1 16.4 %collective-permute-start.1 = (bf16[256,1152]{1,0:T(8,128)(2,1)S(1)}, bf16[256,1152]{1,0:T(8,128)(2,1)S(1)}, u32[]{:S(2)}, u32[]{:S(2)}) collective-permute-start(bf16[256,1152]{1,0:T(8,128)(2,1)S(1)} %concatenate.106), channel_id=1, source_target_pairs={{1,0},{0,1},{3,2},{2,3},{5,4},{4,5},{7,6},{6,7},{9,8},{8,9},{11,10... | collective-permute-start | bytes 1769480 | tf_op jit(solution)/shard_map/ppermute | solution.py:368
  16.1 15.9 %collective-permute-start = (bf16[256,1152]{1,0:T(8,128)(2,1)S(1)}, bf16[256,1152]{1,0:T(8,128)(2,1)}, u32[]{:S(2)}, u32[]{:S(2)}) collective-permute-start(bf16[256,1152]{1,0:T(8,128)(2,1)S(1)} %concatenate.106), channel_id=1, source_target_pairs={{2,0},{3,1},{4,2},{5,3},{6,4},{7,5},{0,6},{1,7},{10,8},{11,9},{12,... | collective-permute-start | bytes 1769480 | tf_op jit(solution)/shard_map/ppermute | solution.py:368
  33.6 141.6 %all-gather.10.cloned.1.call-start = ((), (), s32[]{:S(2)}) async-start(), calls=%async_computation.4 | async-start | bytes 3932160 | tf_op jit(solution)/shard_map/all_gather | solution.py:533
  33.9 14.2 %collective-permute-start.3 = (bf16[256,1152]{1,0:T(8,128)(2,1)}, bf16[256,1152]{1,0:T(8,128)(2,1)S(1)}, u32[]{:S(2)}, u32[]{:S(2)}) collective-permute-start(bf16[256,1152]{1,0:T(8,128)(2,1)} %collective-permute-done), channel_id=1, source_target_pairs={{1,0},{0,1},{3,2},{2,3},{5,4},{4,5},{7,6},{6,7},{9,8},{8,9},{11,10... | collective-permute-start | bytes 1769480 | tf_op jit(solution)/shard_map/ppermute | solution.py:368
  34.4 15.8 %collective-permute-start.2 = (bf16[256,1152]{1,0:T(8,128)(2,1)}, bf16[256,1152]{1,0:T(8,128)(2,1)S(1)}, u32[]{:S(2)}, u32[]{:S(2)}) collective-permute-start(bf16[256,1152]{1,0:T(8,128)(2,1)} %collective-permute-done), channel_id=1, source_target_pairs={{2,0},{3,1},{4,2},{5,3},{6,4},{7,5},{0,6},{1,7},{10,8},{11,9},{12,... | collective-permute-start | bytes 1769480 | tf_op jit(solution)/shard_map/ppermute | solution.py:368
  50.2 12.7 %collective-permute-start.5 = (bf16[256,1152]{1,0:T(8,128)(2,1)S(1)}, bf16[256,1152]{1,0:T(8,128)(2,1)S(1)}, u32[]{:S(2)}, u32[]{:S(2)}) collective-permute-start(bf16[256,1152]{1,0:T(8,128)(2,1)S(1)} %collective-permute-done.2), channel_id=1, source_target_pairs={{1,0},{0,1},{3,2},{2,3},{5,4},{4,5},{7,6},{6,7},{9,8},{8,9},{11,10... | collective-permute-start | bytes 1769480 | tf_op jit(solution)/shard_map/ppermute | solution.py:368
  51.8 16.3 %collective-permute-start.4 = (bf16[256,1152]{1,0:T(8,128)(2,1)S(1)}, bf16[256,1152]{1,0:T(8,128)(2,1)S(1)}, u32[]{:S(2)}, u32[]{:S(2)}) collective-permute-start(bf16[256,1152]{1,0:T(8,128)(2,1)S(1)} %collective-permute-done.2), channel_id=1, source_target_pairs={{2,0},{3,1},{4,2},{5,3},{6,4},{7,5},{0,6},{1,7},{10,8},{11,9},{12,... | collective-permute-start | bytes 1769480 | tf_op jit(solution)/shard_map/ppermute | solution.py:368
  68.1 9.9 %collective-permute-start.6 = (bf16[256,1152]{1,0:T(8,128)(2,1)S(1)}, bf16[256,1152]{1,0:T(8,128)(2,1)S(1)}, u32[]{:S(2)}, u32[]{:S(2)}) collective-permute-start(bf16[256,1152]{1,0:T(8,128)(2,1)S(1)} %collective-permute-done.4), channel_id=1, source_target_pairs={{1,0},{0,1},{3,2},{2,3},{5,4},{4,5},{7,6},{6,7},{9,8},{8,9},{11,10... | collective-permute-start | bytes 1769480 | tf_op jit(solution)/shard_map/ppermute | solution.py:368
  68.9 21.0 %collective-permute-start.9 = (bf16[512,256]{1,0:T(8,128)(2,1)S(1)}, bf16[512,256]{1,0:T(8,128)(2,1)S(1)}, u32[]{:S(2)}, u32[]{:S(2)}) collective-permute-start(bf16[512,256]{1,0:T(8,128)(2,1)S(1)} %convert_element_type.305), channel_id=1, source_target_pairs={{6,0},{7,1},{0,2},{1,3},{2,4},{3,5},{4,6},{5,7},{14,8},{15,9},{8,1... | collective-permute-start | bytes 786440 | tf_op jit(solution)/shard_map/ppermute | solution.py:368
  68.9 21.0 %collective-permute-start.8 = (bf16[512,256]{1,0:T(8,128)(2,1)S(1)}, bf16[512,256]{1,0:T(8,128)(2,1)S(1)}, u32[]{:S(2)}, u32[]{:S(2)}) collective-permute-start(bf16[512,256]{1,0:T(8,128)(2,1)S(1)} %convert_element_type.305), channel_id=1, source_target_pairs={{4,0},{5,1},{6,2},{7,3},{0,4},{1,5},{2,6},{3,7},{12,8},{13,9},{14,... | collective-permute-start | bytes 786440 | tf_op jit(solution)/shard_map/ppermute | solution.py:368
  73.8 16.2 %collective-permute-start.7 = (bf16[512,256]{1,0:T(8,128)(2,1)S(1)}, bf16[512,256]{1,0:T(8,128)(2,1)}, u32[]{:S(2)}, u32[]{:S(2)}) collective-permute-start(bf16[512,256]{1,0:T(8,128)(2,1)S(1)} %convert_element_type.305), channel_id=1, source_target_pairs={{2,0},{3,1},{4,2},{5,3},{6,4},{7,5},{0,6},{1,7},{10,8},{11,9},{12,... | collective-permute-start | bytes 786440 | tf_op jit(solution)/shard_map/ppermute | solution.py:368
  90.0 26.3 %collective-permute-start.14 = (bf16[256,2048]{1,0:T(8,128)(2,1)}, bf16[256,2048]{1,0:T(8,128)(2,1)}, u32[]{:S(2)}, u32[]{:S(2)}) collective-permute-start(bf16[256,2048]{1,0:T(8,128)(2,1)} %fusion.56), channel_id=1, source_target_pairs={{2,0},{3,1},{4,2},{5,3},{6,4},{7,5},{0,6},{1,7},{10,8},{11,9},{12,... | collective-permute-start | bytes 3145736 | tf_op jit(solution)/shard_map/ppermute | solution.py:368
  95.6 20.3 %collective-permute-start.10 = (bf16[512,256]{1,0:T(8,128)(2,1)S(1)}, bf16[512,256]{1,0:T(8,128)(2,1)}, u32[]{:S(2)}, u32[]{:S(2)}) collective-permute-start(bf16[512,256]{1,0:T(8,128)(2,1)S(1)} %convert_element_type.305), channel_id=1, source_target_pairs={{1,0},{0,1},{3,2},{2,3},{5,4},{4,5},{7,6},{6,7},{9,8},{8,9},{11,10... | collective-permute-start | bytes 786440 | tf_op jit(solution)/shard_map/ppermute | solution.py:368
  95.6 20.3 %collective-permute-start.11 = (bf16[512,256]{1,0:T(8,128)(2,1)}, bf16[512,256]{1,0:T(8,128)(2,1)}, u32[]{:S(2)}, u32[]{:S(2)}) collective-permute-start(bf16[512,256]{1,0:T(8,128)(2,1)} %collective-permute-done.7), channel_id=1, source_target_pairs={{1,0},{0,1},{3,2},{2,3},{5,4},{4,5},{7,6},{6,7},{9,8},{8,9},{11,10... | collective-permute-start | bytes 786440 | tf_op jit(solution)/shard_map/ppermute | solution.py:368
  97.6 18.3 %collective-permute-start.12 = (bf16[512,256]{1,0:T(8,128)(2,1)S(1)}, bf16[512,256]{1,0:T(8,128)(2,1)}, u32[]{:S(2)}, u32[]{:S(2)}) collective-permute-start(bf16[512,256]{1,0:T(8,128)(2,1)S(1)} %collective-permute-done.8), channel_id=1, source_target_pairs={{1,0},{0,1},{3,2},{2,3},{5,4},{4,5},{7,6},{6,7},{9,8},{8,9},{11,10... | collective-permute-start | bytes 786440 | tf_op jit(solution)/shard_map/ppermute | solution.py:368
  97.6 18.6 %collective-permute-start.13 = (bf16[512,256]{1,0:T(8,128)(2,1)S(1)}, bf16[512,256]{1,0:T(8,128)(2,1)}, u32[]{:S(2)}, u32[]{:S(2)}) collective-permute-start(bf16[512,256]{1,0:T(8,128)(2,1)S(1)} %collective-permute-done.9), channel_id=1, source_target_pairs={{1,0},{0,1},{3,2},{2,3},{5,4},{4,5},{7,6},{6,7},{9,8},{8,9},{11,10... | collective-permute-start | bytes 786440 | tf_op jit(solution)/shard_map/ppermute | solution.py:368
  101.2 150.7 %all-gather.12.cloned.1.call-start = ((), (), s32[]{:S(2)}) async-start(), calls=%async_computation.5 | async-start | bytes 7864320 | tf_op jit(solution)/shard_map/all_gather | solution.py:530
  122.9 4.2 collective-permute-start.15
  123.8 36.0 %collective-permute-start.18 = (bf16[512,1536]{1,0:T(8,128)(2,1)S(1)}, bf16[512,1536]{1,0:T(8,128)(2,1)S(1)}, u32[]{:S(2)}, u32[]{:S(2)}) collective-permute-start(bf16[512,1536]{1,0:T(8,128)(2,1)S(1)} %copy-done.26), channel_id=1, source_target_pairs={{1,0},{0,1},{3,2},{2,3},{5,4},{4,5},{7,6},{6,7},{9,8},{8,9},{11,10... | collective-permute-start | bytes 4718600 | tf_op jit(solution)/shard_map/ppermute | solution.py:368
  128.5 14.8 %collective-permute-start.16 = (bf16[128,2048]{1,0:T(8,128)(2,1)S(1)}, bf16[128,2048]{1,0:T(8,128)(2,1)S(1)}, u32[]{:S(2)}, u32[]{:S(2)}) collective-permute-start(bf16[128,2048]{1,0:T(8,128)(2,1)S(1)} %get-tuple-element.647), channel_id=1, source_target_pairs={{0,16},{16,0},{1,17},{17,1},{2,18},{18,2},{3,19},{19,3},{4,20},{20... | collective-permute-start | bytes 1572872 | tf_op jit(solution)/shard_map/ppermute | solution.py:338
  130.1 23.7 %collective-permute-start.19 = (bf16[128,2048]{1,0:T(8,128)(2,1)S(1)}, bf16[128,2048]{1,0:T(8,128)(2,1)S(1)}, u32[]{:S(2)}, u32[]{:S(2)}) collective-permute-start(bf16[128,2048]{1,0:T(8,128)(2,1)S(1)} %get-tuple-element.648), channel_id=1, source_target_pairs={{0,16},{16,0},{1,17},{17,1},{2,18},{18,2},{3,19},{19,3},{4,20},{20... | collective-permute-start | bytes 1572872 | tf_op jit(solution)/shard_map/ppermute | solution.py:338
  130.6 25.0 %collective-permute-start.17 = (bf16[256,2048]{1,0:T(8,128)(2,1)}, bf16[256,2048]{1,0:T(8,128)(2,1)}, u32[]{:S(2)}, u32[]{:S(2)}) collective-permute-start(bf16[256,2048]{1,0:T(8,128)(2,1)} %collective-permute-done.14), channel_id=1, source_target_pairs={{2,0},{3,1},{4,2},{5,3},{6,4},{7,5},{0,6},{1,7},{10,8},{11,9},{12,... | collective-permute-start | bytes 3145736 | tf_op jit(solution)/shard_map/ppermute | solution.py:368
  161.0 97.0 %all-gather.14.cloned.1.call-start = ((), (), s32[]{:S(2)}) async-start(), calls=%async_computation.6 | async-start | bytes 3932160 | tf_op jit(solution)/shard_map/all_gather | solution.py:533
  161.1 23.1 %collective-permute-start.21 = (bf16[768,512]{1,0:T(8,128)(2,1)}, bf16[768,512]{1,0:T(8,128)(2,1)}, u32[]{:S(2)}, u32[]{:S(2)}) collective-permute-start(bf16[768,512]{1,0:T(8,128)(2,1)} %convert_element_type.310), channel_id=1, source_target_pairs={{1,0},{0,1},{3,2},{2,3},{5,4},{4,5},{7,6},{6,7},{9,8},{8,9},{11,10... | collective-permute-start | bytes 2359304 | tf_op jit(solution)/shard_map/ppermute | solution.py:368
  164.3 26.3 %collective-permute-start.20 = (bf16[256,2048]{1,0:T(8,128)(2,1)S(1)}, bf16[256,2048]{1,0:T(8,128)(2,1)}, u32[]{:S(2)}, u32[]{:S(2)}) collective-permute-start(bf16[256,2048]{1,0:T(8,128)(2,1)S(1)} %multiply_convert_fusion), channel_id=1, source_target_pairs={{2,0},{3,1},{4,2},{5,3},{6,4},{7,5},{0,6},{1,7},{10,8},{11,9},{12,... | collective-permute-start | bytes 3145736 | tf_op jit(solution)/shard_map/ppermute | solution.py:368
  165.7 44.8 %collective-permute-start.22 = (bf16[256,2048]{1,0:T(8,128)(2,1)}, bf16[256,2048]{1,0:T(8,128)(2,1)}, u32[]{:S(2)}, u32[]{:S(2)}) collective-permute-start(bf16[256,2048]{1,0:T(8,128)(2,1)} %collective-permute-done.17), channel_id=1, source_target_pairs={{2,0},{3,1},{4,2},{5,3},{6,4},{7,5},{0,6},{1,7},{10,8},{11,9},{12,... | collective-permute-start | bytes 3145736 | tf_op jit(solution)/shard_map/ppermute | solution.py:368
  210.5 23.6 %collective-permute-start.23 = (bf16[256,2048]{1,0:T(8,128)(2,1)}, bf16[256,2048]{1,0:T(8,128)(2,1)}, u32[]{:S(2)}, u32[]{:S(2)}) collective-permute-start(bf16[256,2048]{1,0:T(8,128)(2,1)} %collective-permute-done.20), channel_id=1, source_target_pairs={{2,0},{3,1},{4,2},{5,3},{6,4},{7,5},{0,6},{1,7},{10,8},{11,9},{12,... | collective-permute-start | bytes 3145736 | tf_op jit(solution)/shard_map/ppermute | solution.py:368
  213.7 313.1 %reduce-scatter.3.cloned.1.call-start = ((), (), s32[]{:S(2)}) async-start(), calls=%async_computation.7 | async-start | bytes 7864320 | tf_op jit(solution)/shard_map/reduce_scatter | solution.py:739
  234.1 31.8 %collective-permute-start.24 = (bf16[256,2048]{1,0:T(8,128)(2,1)}, bf16[256,2048]{1,0:T(8,128)(2,1)}, u32[]{:S(2)}, u32[]{:S(2)}) collective-permute-start(bf16[256,2048]{1,0:T(8,128)(2,1)} %collective-permute-done.23), channel_id=1, source_target_pairs={{2,0},{3,1},{4,2},{5,3},{6,4},{7,5},{0,6},{1,7},{10,8},{11,9},{12,... | collective-permute-start | bytes 3145736 | tf_op jit(solution)/shard_map/ppermute | solution.py:368
  265.9 21.9 %collective-permute-start.25 = (bf16[256,2048]{1,0:T(8,128)(2,1)S(1)}, bf16[256,2048]{1,0:T(8,128)(2,1)S(1)}, u32[]{:S(2)}, u32[]{:S(2)}) collective-permute-start(bf16[256,2048]{1,0:T(8,128)(2,1)S(1)} %add.574), channel_id=1, source_target_pairs={{2,0},{3,1},{4,2},{5,3},{6,4},{7,5},{0,6},{1,7},{10,8},{11,9},{12,... | collective-permute-start | bytes 3145736 | tf_op jit(solution)/shard_map/ppermute | solution.py:368
  288.1 22.2 %collective-permute-start.26 = (bf16[256,2048]{1,0:T(8,128)(2,1)S(1)}, bf16[256,2048]{1,0:T(8,128)(2,1)S(1)}, u32[]{:S(2)}, u32[]{:S(2)}) collective-permute-start(bf16[256,2048]{1,0:T(8,128)(2,1)S(1)} %add_convert_fusion.1), channel_id=1, source_target_pairs={{2,0},{3,1},{4,2},{5,3},{6,4},{7,5},{0,6},{1,7},{10,8},{11,9},{12,... | collective-permute-start | bytes 3145736 | tf_op jit(solution)/shard_map/ppermute | solution.py:368
  311.6 24.9 %collective-permute-start.27 = (bf16[256,2048]{1,0:T(8,128)(2,1)}, bf16[256,2048]{1,0:T(8,128)(2,1)S(1)}, u32[]{:S(2)}, u32[]{:S(2)}) collective-permute-start(bf16[256,2048]{1,0:T(8,128)(2,1)} %add_convert_fusion), channel_id=1, source_target_pairs={{2,0},{3,1},{4,2},{5,3},{6,4},{7,5},{0,6},{1,7},{10,8},{11,9},{12,... | collective-permute-start | bytes 3145736 | tf_op jit(solution)/shard_map/ppermute | solution.py:368
  336.5 13.7 %collective-permute-start.30 = (bf16[1024,1536]{1,0:T(8,128)(2,1)S(1)}, bf16[1024,1536]{1,0:T(8,128)(2,1)S(1)}, u32[]{:S(2)}, u32[]{:S(2)}) collective-permute-start(bf16[1024,1536]{1,0:T(8,128)(2,1)S(1)} %convolution_convert_fusion.1), channel_id=1, source_target_pairs={{0,8},{8,0},{1,9},{9,1},{2,10},{10,2},{3,11},{11,3},{4,12},{12,4},... | collective-permute-start | bytes 9437192 | tf_op jit(solution)/shard_map/ppermute | solution.py:333
  339.8 25.3 %collective-permute-start.28 = (bf16[256,2048]{1,0:T(8,128)(2,1)S(1)}, bf16[256,2048]{1,0:T(8,128)(2,1)S(1)}, u32[]{:S(2)}, u32[]{:S(2)}) collective-permute-start(bf16[256,2048]{1,0:T(8,128)(2,1)S(1)} %get-tuple-element.451), channel_id=1, source_target_pairs={{0,16},{16,0},{1,17},{17,1},{2,18},{18,2},{3,19},{19,3},{4,20},{20... | collective-permute-start | bytes 3145736 | tf_op jit(solution)/shard_map/ppermute | solution.py:338
  341.3 25.2 %collective-permute-start.29 = (bf16[256,2048]{1,0:T(8,128)(2,1)S(1)}, bf16[256,2048]{1,0:T(8,128)(2,1)S(1)}, u32[]{:S(2)}, u32[]{:S(2)}) collective-permute-start(bf16[256,2048]{1,0:T(8,128)(2,1)S(1)} %fusion.38), channel_id=1, source_target_pairs={{2,0},{3,1},{4,2},{5,3},{6,4},{7,5},{0,6},{1,7},{10,8},{11,9},{12,... | collective-permute-start | bytes 3145736 | tf_op jit(solution)/shard_map/ppermute | solution.py:368
  366.5 7.2 %collective-permute-start.33 = (bf16[768,1024]{1,0:T(8,128)(2,1)}, bf16[768,1024]{1,0:T(8,128)(2,1)S(1)}, u32[]{:S(2)}, u32[]{:S(2)}) collective-permute-start(bf16[768,1024]{1,0:T(8,128)(2,1)} %fusion.57), channel_id=1, source_target_pairs={{0,8},{8,0},{1,9},{9,1},{2,10},{10,2},{3,11},{11,3},{4,12},{12,4},... | collective-permute-start | bytes 4718600 | tf_op jit(solution)/shard_map/ppermute | solution.py:333
  366.5 4.5 collective-permute-start.31
  367.0 5.9 collective-permute-start.32
  367.0 36.9 %collective-permute-start.35 = (bf16[512,1536]{1,0:T(8,128)(2,1)S(1)}, bf16[512,1536]{1,0:T(8,128)(2,1)}, u32[]{:S(2)}, u32[]{:S(2)}) collective-permute-start(bf16[512,1536]{1,0:T(8,128)(2,1)S(1)} %fusion.30), channel_id=1, source_target_pairs={{0,16},{16,0},{1,17},{17,1},{2,18},{18,2},{3,19},{19,3},{4,20},{20... | collective-permute-start | bytes 4718600 | tf_op jit(solution)/shard_map/ppermute | solution.py:338
  367.9 33.2 %collective-permute-start.34 = (bf16[256,2048]{1,0:T(8,128)(2,1)S(1)}, bf16[256,2048]{1,0:T(8,128)(2,1)}, u32[]{:S(2)}, u32[]{:S(2)}) collective-permute-start(bf16[256,2048]{1,0:T(8,128)(2,1)S(1)} %add.603), channel_id=1, source_target_pairs={{2,0},{3,1},{4,2},{5,3},{6,4},{7,5},{0,6},{1,7},{10,8},{11,9},{12,... | collective-permute-start | bytes 3145736 | tf_op jit(solution)/shard_map/ppermute | solution.py:368
  403.9 161.6 %reduce-scatter.5.cloned.1.call-start = ((), (), s32[]{:S(2)}) async-start(), calls=%async_computation.8 | async-start | bytes 3932160 | tf_op jit(solution)/shard_map/reduce_scatter | solution.py:787
  405.8 33.8 %collective-permute-start.37 = (bf16[256,2048]{1,0:T(8,128)(2,1)S(1)}, bf16[256,2048]{1,0:T(8,128)(2,1)S(1)}, u32[]{:S(2)}, u32[]{:S(2)}) collective-permute-start(bf16[256,2048]{1,0:T(8,128)(2,1)S(1)} %add.608), channel_id=1, source_target_pairs={{2,0},{3,1},{4,2},{5,3},{6,4},{7,5},{0,6},{1,7},{10,8},{11,9},{12,... | collective-permute-start | bytes 3145736 | tf_op jit(solution)/shard_map/ppermute | solution.py:368
  416.1 22.6 %collective-permute-start.36 = (bf16[256,1152]{1,0:T(8,128)(2,1)S(1)}, bf16[256,1152]{1,0:T(8,128)(2,1)S(1)}, u32[]{:S(2)}, u32[]{:S(2)}) collective-permute-start(bf16[256,1152]{1,0:T(8,128)(2,1)S(1)} %dynamic-slice_convert_fusion.3), channel_id=1, source_target_pairs={{1,0},{0,1},{3,2},{2,3},{5,4},{4,5},{7,6},{6,7},{9,8},{8,9},{11,10... | collective-permute-start | bytes 1769480 | tf_op jit(solution)/shard_map/ppermute | solution.py:368
  439.6 21.1 %collective-permute-start.43 = (bf16[512,2048]{1,0:T(8,128)(2,1)}, bf16[512,2048]{1,0:T(8,128)(2,1)}, u32[]{:S(2)}, u32[]{:S(2)}) collective-permute-start(bf16[512,2048]{1,0:T(8,128)(2,1)} %convolution_convert_fusion.3), channel_id=1, source_target_pairs={{0,8},{8,0},{1,9},{9,1},{2,10},{10,2},{3,11},{11,3},{4,12},{12,4},... | collective-permute-start | bytes 6291464 | tf_op jit(solution)/shard_map/ppermute | solution.py:333
  439.6 29.4 %collective-permute-start.40 = (bf16[512,512]{1,0:T(8,128)(2,1)}, bf16[512,512]{1,0:T(8,128)(2,1)}, u32[]{:S(2)}, u32[]{:S(2)}) collective-permute-start(bf16[512,512]{1,0:T(8,128)(2,1)} %pad_maximum_fusion.7), channel_id=1, source_target_pairs={{2,0},{3,1},{4,2},{5,3},{6,4},{7,5},{0,6},{1,7},{10,8},{11,9},{12,... | collective-permute-start | bytes 1572872 | tf_op jit(solution)/shard_map/ppermute | solution.py:368
  441.4 16.6 %collective-permute-start.39 = (bf16[256,1152]{1,0:T(8,128)(2,1)}, bf16[256,1152]{1,0:T(8,128)(2,1)}, u32[]{:S(2)}, u32[]{:S(2)}) collective-permute-start(bf16[256,1152]{1,0:T(8,128)(2,1)} %dynamic-slice_convert_fusion.2), channel_id=1, source_target_pairs={{1,0},{0,1},{3,2},{2,3},{5,4},{4,5},{7,6},{6,7},{9,8},{8,9},{11,10... | collective-permute-start | bytes 1769480 | tf_op jit(solution)/shard_map/ppermute | solution.py:368
  442.7 26.4 %collective-permute-start.38 = (bf16[256,1152]{1,0:T(8,128)(2,1)}, bf16[256,1152]{1,0:T(8,128)(2,1)}, u32[]{:S(2)}, u32[]{:S(2)}) collective-permute-start(bf16[256,1152]{1,0:T(8,128)(2,1)} %convert_add_fusion.11), channel_id=1, source_target_pairs={{2,0},{3,1},{4,2},{5,3},{6,4},{7,5},{0,6},{1,7},{10,8},{11,9},{12,... | collective-permute-start | bytes 1769480 | tf_op jit(solution)/shard_map/ppermute | solution.py:368
  443.1 30.8 %collective-permute-start.41 = (bf16[256,1536]{1,0:T(8,128)(2,1)}, bf16[256,1536]{1,0:T(8,128)(2,1)S(1)}, u32[]{:S(2)}, u32[]{:S(2)}) collective-permute-start(bf16[256,1536]{1,0:T(8,128)(2,1)} %get-tuple-element.535), channel_id=1, source_target_pairs={{1,0},{0,1},{3,2},{2,3},{5,4},{4,5},{7,6},{6,7},{9,8},{8,9},{11,10... | collective-permute-start | bytes 2359304 | tf_op jit(solution)/shard_map/ppermute | solution.py:368
  457.9 18.4 %collective-permute-start.42 = (bf16[768,512]{1,0:T(8,128)(2,1)}, bf16[768,512]{1,0:T(8,128)(2,1)}, u32[]{:S(2)}, u32[]{:S(2)}) collective-permute-start(bf16[768,512]{1,0:T(8,128)(2,1)} %add_convert_fusion.3), channel_id=1, source_target_pairs={{0,16},{16,0},{1,17},{17,1},{2,18},{18,2},{3,19},{19,3},{4,20},{20... | collective-permute-start | bytes 2359304 | tf_op jit(solution)/shard_map/ppermute | solution.py:338
  478.5 16.6 %collective-permute-start.45 = (bf16[256,1152]{1,0:T(8,128)(2,1)}, bf16[256,1152]{1,0:T(8,128)(2,1)}, u32[]{:S(2)}, u32[]{:S(2)}) collective-permute-start(bf16[256,1152]{1,0:T(8,128)(2,1)} %dynamic-slice_convert_fusion.1), channel_id=1, source_target_pairs={{1,0},{0,1},{3,2},{2,3},{5,4},{4,5},{7,6},{6,7},{9,8},{8,9},{11,10... | collective-permute-start | bytes 1769480 | tf_op jit(solution)/shard_map/ppermute | solution.py:368
  481.7 45.0 %collective-permute-start.44 = (bf16[256,1152]{1,0:T(8,128)(2,1)S(1)}, bf16[256,1152]{1,0:T(8,128)(2,1)}, u32[]{:S(2)}, u32[]{:S(2)}) collective-permute-start(bf16[256,1152]{1,0:T(8,128)(2,1)S(1)} %add_convert_fusion.5), channel_id=1, source_target_pairs={{2,0},{3,1},{4,2},{5,3},{6,4},{7,5},{0,6},{1,7},{10,8},{11,9},{12,... | collective-permute-start | bytes 1769480 | tf_op jit(solution)/shard_map/ppermute | solution.py:368
  485.1 41.6 %collective-permute-start.47 = (bf16[256,1536]{1,0:T(8,128)(2,1)}, bf16[256,1536]{1,0:T(8,128)(2,1)}, u32[]{:S(2)}, u32[]{:S(2)}) collective-permute-start(bf16[256,1536]{1,0:T(8,128)(2,1)} %get-tuple-element.556), channel_id=1, source_target_pairs={{1,0},{0,1},{3,2},{2,3},{5,4},{4,5},{7,6},{6,7},{9,8},{8,9},{11,10... | collective-permute-start | bytes 2359304 | tf_op jit(solution)/shard_map/ppermute | solution.py:368
  487.2 38.0 %collective-permute-start.52 = (bf16[256,2048]{1,0:T(8,128)(2,1)S(1)}, bf16[256,2048]{1,0:T(8,128)(2,1)S(1)}, u32[]{:S(2)}, u32[]{:S(2)}) collective-permute-start(bf16[256,2048]{1,0:T(8,128)(2,1)S(1)} %slice.401), channel_id=1, source_target_pairs={{0,16},{16,0},{1,17},{17,1},{2,18},{18,2},{3,19},{19,3},{4,20},{20... | collective-permute-start | bytes 3145736 | tf_op jit(solution)/shard_map/ppermute | solution.py:338
  489.0 37.7 %collective-permute-start.46 = (bf16[512,512]{1,0:T(8,128)(2,1)S(1)}, bf16[512,512]{1,0:T(8,128)(2,1)S(1)}, u32[]{:S(2)}, u32[]{:S(2)}) collective-permute-start(bf16[512,512]{1,0:T(8,128)(2,1)S(1)} %fusion.96), channel_id=1, source_target_pairs={{2,0},{3,1},{4,2},{5,3},{6,4},{7,5},{0,6},{1,7},{10,8},{11,9},{12,... | collective-permute-start | bytes 1572872 | tf_op jit(solution)/shard_map/ppermute | solution.py:368
  528.3 16.3 %collective-permute-start.49 = (bf16[256,1152]{1,0:T(8,128)(2,1)S(1)}, bf16[256,1152]{1,0:T(8,128)(2,1)S(1)}, u32[]{:S(2)}, u32[]{:S(2)}) collective-permute-start(bf16[256,1152]{1,0:T(8,128)(2,1)S(1)} %dynamic-slice_convert_fusion), channel_id=1, source_target_pairs={{1,0},{0,1},{3,2},{2,3},{5,4},{4,5},{7,6},{6,7},{9,8},{8,9},{11,10... | collective-permute-start | bytes 1769480 | tf_op jit(solution)/shard_map/ppermute | solution.py:368
  531.2 19.4 %collective-permute-start.48 = (bf16[256,1152]{1,0:T(8,128)(2,1)S(1)}, bf16[256,1152]{1,0:T(8,128)(2,1)S(1)}, u32[]{:S(2)}, u32[]{:S(2)}) collective-permute-start(bf16[256,1152]{1,0:T(8,128)(2,1)S(1)} %add_convert_fusion.4), channel_id=1, source_target_pairs={{2,0},{3,1},{4,2},{5,3},{6,4},{7,5},{0,6},{1,7},{10,8},{11,9},{12,... | collective-permute-start | bytes 1769480 | tf_op jit(solution)/shard_map/ppermute | solution.py:368
  531.3 22.4 %collective-permute-start.51 = (bf16[768,512]{1,0:T(8,128)(2,1)}, bf16[768,512]{1,0:T(8,128)(2,1)S(1)}, u32[]{:S(2)}, u32[]{:S(2)}) collective-permute-start(bf16[768,512]{1,0:T(8,128)(2,1)} %add_convert_fusion.2), channel_id=1, source_target_pairs={{1,0},{0,1},{3,2},{2,3},{5,4},{4,5},{7,6},{6,7},{9,8},{8,9},{11,10... | collective-permute-start | bytes 2359304 | tf_op jit(solution)/shard_map/ppermute | solution.py:368
  534.5 16.1 %collective-permute-start.50 = (bf16[512,512]{1,0:T(8,128)(2,1)S(1)}, bf16[512,512]{1,0:T(8,128)(2,1)S(1)}, u32[]{:S(2)}, u32[]{:S(2)}) collective-permute-start(bf16[512,512]{1,0:T(8,128)(2,1)S(1)} %fusion.97), channel_id=1, source_target_pairs={{2,0},{3,1},{4,2},{5,3},{6,4},{7,5},{0,6},{1,7},{10,8},{11,9},{12,... | collective-permute-start | bytes 1572872 | tf_op jit(solution)/shard_map/ppermute | solution.py:368
  559.5 10.7 %collective-permute-start.53 = (bf16[512,256]{1,0:T(8,128)(2,1)}, bf16[512,256]{1,0:T(8,128)(2,1)}, u32[]{:S(2)}, u32[]{:S(2)}) collective-permute-start(bf16[512,256]{1,0:T(8,128)(2,1)} %slice.402), channel_id=1, source_target_pairs={{1,0},{0,1},{3,2},{2,3},{5,4},{4,5},{7,6},{6,7},{9,8},{8,9},{11,10... | collective-permute-start | bytes 786440 | tf_op jit(solution)/shard_map/ppermute | solution.py:368
  580.1 4.7 collective-permute-start.58
  580.2 4.7 collective-permute-start.57
  586.3 4.7 collective-permute-start.59
  (138 other events, 837.7 us)
Sparse Core Ops, SparseCore 0:
  13.1 37.1 all-gather.5
  52.5 46.3 all-gather.7
  101.3 28.2 all-gather.9
  161.1 45.2 all-gather.11
  213.8 26.6 all-gather.13
  404.0 57.1 reduce-scatter.2
  480.1 48.9 reduce-scatter.4

commit v4 on v3

--- a/solution.py
+++ b/solution.py
@@ -80,6 +80,11 @@
     return values * cosine + pltpu.roll(values, HD // 2, 1) * sine
 
 
+def lane_mean(values):
+    ones = jnp.full((HD, HD), 1.0 / HD, jnp.bfloat16)
+    return jnp.dot(values.astype(jnp.bfloat16), ones, preferred_element_type=jnp.float32)
+
+
 def dot_cols(left, right):
     return lax.dot_general(
         left, right, (((1,), (1,)), ((), ())), preferred_element_type=jnp.float32
@@ -90,6 +95,13 @@
     return lax.dot_general(
         left, right, (((0,), (0,)), ((), ())), preferred_element_type=jnp.float32
     )
+
+
+def allowed_queries(start, first, block, length, repeat):
+    keys = lax.broadcasted_iota(jnp.int32, (length, block), 0)
+    queries = first + lax.broadcasted_iota(jnp.int32, (length, block), 1)
+    allowed = (keys >= start) & (keys <= queries)
+    return jnp.concatenate([allowed] * repeat, 1)
 
 
 def allowed_keys(start, first, block, length, repeat):
@@ -124,7 +136,7 @@
 
     def prepared(column, gain_row):
         part = raw[:, column : column + HD]
-        scale = lax.rsqrt(jnp.mean(part * part, -1, keepdims=True) + NORM_EPS)
+        scale = lax.rsqrt(lane_mean(part * part) + NORM_EPS)
         return turn(part * scale * gain_row, cos, sin).astype(jnp.bfloat16)
 
     for g in range(groups):
@@ -195,10 +207,10 @@
     block,
     slots,
     gated_grad,
-    raw,
+    raw_all,
     start,
-    cosine,
-    sine,
+    cosine_all,
+    sine_all,
     gain,
     query,
     key,
@@ -213,30 +225,42 @@
     query_sum,
     key_sum,
     value_sum,
+    raw,
+    gates,
+    cosine,
+    sine,
+    copied,
 ):
     length = raw.shape[0]
     repeat = heads // groups
     key_from, value_from, gate_from = heads * HD, (heads + groups) * HD, (heads + 2 * groups) * HD
-    cos, sin = cosine[...], sine[...]
     scale = HD**-0.5
+    copies = [
+        pltpu.make_async_copy(raw_all.at[:, gate_from : gate_from + HD], gates, copied.at[0]),
+        pltpu.make_async_copy(raw_all.at[:, :value_from], raw, copied.at[1]),
+        pltpu.make_async_copy(cosine_all, cosine, copied.at[2]),
+        pltpu.make_async_copy(sine_all, sine, copied.at[3]),
+    ]
+    for copy in copies:
+        copy.start()
     nears = [
         pl.ds(pl.multiple_of(slots[i] * block, block), block) for i in range(length // block)
     ]
 
     def unprepared(grad, column, gain_row):
         part = raw[:, column : column + HD]
-        inverse = lax.rsqrt(jnp.mean(part * part, -1, keepdims=True) + NORM_EPS)
+        inverse = lax.rsqrt(lane_mean(part * part) + NORM_EPS)
         unit = part * inverse
         back = grad * cos - pltpu.roll(grad, HD // 2, 1) * sin
         inner = back * gain_row
-        mean = jnp.mean(inner * unit, -1, keepdims=True)
-        result = inverse * (inner - unit * mean)
+        result = inverse * (inner - unit * lane_mean(inner * unit))
         return result.astype(jnp.bfloat16), jnp.sum(back * unit, 0, keepdims=True)
 
     grads[:, gate_from:] = jnp.zeros((length, grads.shape[1] - gate_from), jnp.bfloat16)
+    copies[0].wait()
     for h in range(heads):
         columns = slice(h * HD, (h + 1) * HD)
-        gate = jax.nn.sigmoid(raw[:, gate_from + h : gate_from + h + 1])
+        gate = jax.nn.sigmoid(gates[:, h : h + 1])
         outer = jnp.concatenate([gated_grad[near, columns] for near in nears], 0)
         result = attended[:, columns]
         low = (outer * gate).astype(jnp.bfloat16)
@@ -246,28 +270,37 @@
         delta[:, h : h + 1] = jnp.sum(low.astype(jnp.float32) * result, -1, keepdims=True)
     key_sum[...] = jnp.zeros(key_sum.shape, jnp.float32)
     value_sum[...] = jnp.zeros(value_sum.shape, jnp.float32)
+    log_rows = jnp.transpose(total_log[...])
+    delta_rows = jnp.transpose(delta[...])
     for i in range(length // block):
         rows = slice(i * block, (i + 1) * block)
         seen = (i + 1) * block
-        mask = allowed_keys(start[rows, :], i * block, block, seen, repeat)
+        mask = allowed_queries(start[0:1, rows], i * block, block, seen, repeat)
         for g in range(groups):
             columns = slice(g * HD, (g + 1) * HD)
             hs = range(g * repeat, (g + 1) * repeat)
             queries = jnp.concatenate([query[rows, h * HD : (h + 1) * HD] for h in hs], 0)
             outers = jnp.concatenate([low_grad[rows, h * HD : (h + 1) * HD] for h in hs], 0)
-            logs = jnp.concatenate([total_log[rows, h : h + 1] for h in hs], 0)
-            deltas = jnp.concatenate([delta[rows, h : h + 1] for h in hs], 0)
+            logs = jnp.concatenate([log_rows[h : h + 1, rows] for h in hs], 1)
+            deltas = jnp.concatenate([delta_rows[h : h + 1, rows] for h in hs], 1)
             keys, values = key[:seen, columns], value[:seen, columns]
-            scores = dot_cols(queries, keys) * (scale * LOG2E)
+            scores = dot_cols(keys, queries) * (scale * LOG2E)
             probs = jnp.exp2(jnp.where(mask, scores - logs, MASK_FILL))
-            prob_grad = dot_cols(outers, values)
+            prob_grad = dot_cols(values, outers)
             score_grad = (probs * (prob_grad - deltas)).astype(jnp.bfloat16)
-            moved = jnp.dot(score_grad, keys, preferred_element_type=jnp.float32) * scale
+            moved = dot_rows(score_grad, keys) * scale
             for r, h in enumerate(hs):
                 query_sum[rows, h * HD : (h + 1) * HD] = moved[r * block : (r + 1) * block, :]
-            key_sum[:seen, columns] += dot_rows(score_grad, queries)
-            value_sum[:seen, columns] += dot_rows(probs.astype(jnp.bfloat16), outers)
+            key_sum[:seen, columns] += jnp.dot(
+                score_grad, queries, preferred_element_type=jnp.float32
+            )
+            value_sum[:seen, columns] += jnp.dot(
+                probs.astype(jnp.bfloat16), outers, preferred_element_type=jnp.float32
+            )
     gain_grads[...] = jnp.zeros(gain_grads.shape, jnp.float32)
+    for copy in copies[1:]:
+        copy.wait()
+    cos, sin = cosine[...], sine[...]
     for h in range(heads):
         part, gain_part = unprepared(query_sum[:, h * HD : (h + 1) * HD], h * HD, gain[0:1, :])
         grads[:, h * HD : (h + 1) * HD] = part
@@ -291,7 +324,10 @@
     query, key, value, attended, total_log = saved
     return pl.pallas_call(
         functools.partial(attend_back_kernel, heads, groups, length // slots.shape[0]),
-        in_specs=in_vmem(11),
+        in_specs=[
+            pl.BlockSpec(memory_space=pl.ANY) if i in (2, 4, 5) else spec
+            for i, spec in enumerate(in_vmem(11))
+        ],
         out_shape=(
             jax.ShapeDtypeStruct(raw.shape, jnp.bfloat16),
             jax.ShapeDtypeStruct(raw.shape, jnp.bfloat16),
@@ -303,6 +339,11 @@
             pltpu.VMEM((length, heads * HD), jnp.float32),
             pltpu.VMEM((length, groups * HD), jnp.float32),
             pltpu.VMEM((length, groups * HD), jnp.float32),
+            pltpu.VMEM((length, (heads + groups) * HD), jnp.float32),
+            pltpu.VMEM((length, HD), jnp.float32),
+            pltpu.VMEM((length, HD), jnp.float32),
+            pltpu.VMEM((length, HD), jnp.float32),
+            pltpu.SemaphoreType.DMA((4,)),
         ],
         compiler_params=pltpu.CompilerParams(vmem_limit_bytes=56 * 2**20),
         cost_estimate=pl.CostEstimate(
@@ -534,7 +575,8 @@
 
     group_size = group_in.shape[0]
     places = positions(segment_ids)
-    starts = (jnp.arange(group_size, dtype=jnp.int32) - places)[:, None]
+    starts = jnp.arange(group_size, dtype=jnp.int32) - places
+    starts = (starts[:, None], starts[None, :])
     cosine, sine = rope_tables(places)
 
     near = near_slots()
@@ -550,8 +592,8 @@
             reduce_low = masters_in[1].astype(low)
             expand_all = [expand_whole(expand_low)]
             reduce_all = [reduce_whole(reduce_low)]
-        moved, across, starts, cosine, sine = tie(
-            wide_from(row, 1, 0), inner_gather(row), starts, cosine, sine
+        moved, across, starts, cosine, sine, head_gains = tie(
+            wide_from(row, 1, 0), inner_gather(row), starts, cosine, sine, head_gains
         )
         project_pieces.append(across)
         row = moved
@@ -561,10 +603,13 @@
     project_pieces.append(across)
     project_all = assemble(project_pieces, 0)
     raw = jnp.dot(group_in, project_all, preferred_element_type=wide)
-    raw, output_rows, expand_low, upstream_low = tie(raw, output_rows, expand_low, upstream_low)
+    output_pair = inner_gather(output_low)
+    raw, output_rows, expand_low, upstream_low, output_pair = tie(
+        raw, output_rows, expand_low, upstream_low, output_pair
+    )
     upstream_parts = [upstream_low, outer_shift(upstream_low, 1)]
-    output_pieces = [inner_gather(piece) for piece in output_rows]
-    kept = attend(near, raw, starts, cosine, sine, head_gains, heads, groups)
+    output_pieces = [output_pair] + [inner_gather(piece) for piece in output_rows[1:]]
+    kept = attend(near, raw, starts[0], cosine, sine, head_gains, heads, groups)
     kept, output_pieces, upstream_parts, expand_low = tie(
         kept, output_pieces, upstream_parts, expand_low
     )
@@ -663,8 +708,7 @@
     moved = outer_shift(moved, 1)
     begin(2)
     rest(1)
-    upstream_near = near_columns(upstream_all)
-    moved, done, grad_sums, upstream_near = tie(moved, done, grad_sums, upstream_near)
+    moved, done, grad_sums = tie(moved, done, grad_sums)
     mixed_parts.append(moved)
     moved = outer_shift(grad_sums[1].astype(low), 1)
     rest(2)
@@ -685,8 +729,8 @@
     expand_fars = [None] + [expand_far(j) for j in late]
     output_sums = {1: summed(1)}
     expand_own = contract_rows(mixed_all, joined(1, 0)).astype(low)
-    moved, done, mixed_near, expand_fars, output_sums, upstream_near, expand_own, upstream_all = tie(
-        moved, done, mixed_near, expand_fars, output_sums, upstream_near, expand_own, upstream_all
+    moved, done, mixed_near, expand_fars, output_sums, expand_own, upstream_all = tie(
+        moved, done, mixed_near, expand_fars, output_sums, expand_own, upstream_all
     )
     mixed_grad = grad_sums[0] + moved.astype(wide)
     _, second_back = jax.vjp(norm_rows, residual, norm_two)
@@ -698,6 +742,7 @@
     expand_lead = [None] + [
         expand_term(j, 1 % x_size, expand_fars[j]).astype(low) for j in late
     ]
+    upstream_near = near_columns(upstream_all)
     reduce_fars = [None] + [reduce_far(j) for j in late]
     output_sums[2] = summed(2)
     output_sums[3] = summed(3)
@@ -725,7 +770,7 @@
         near,
         gated_grad,
         raw,
-        starts,
+        starts[1],
         cosine,
         sine,
         head_gains,
@@ -742,11 +787,11 @@
     def normed_back(rows):
         return contract_cols(rows, project_all)
 
+    project_grad = pinned(contract_rows(group_in, low_grads))
+    project_grad, low_near, done, upstream_all, residual_all, expand_moved, reduce_fars, output_total = tie(
+        project_grad, low_near, done, upstream_all, residual_all, expand_moved, reduce_fars, output_total
+    )
     output_total = outer_shift(output_sums[3] + output_total, 1)
-    project_grad = pinned(contract_rows(group_in, low_grads))
-    project_grad, low_near, done, upstream_all, residual_all, expand_moved, reduce_fars = tie(
-        project_grad, low_near, done, upstream_all, residual_all, expand_moved, reduce_fars
-    )
 
     def spread(parts):
         total = parts[0]
@@ -780,12 +825,17 @@
             normed_far = swapped(normed_far, "c", 1)
             reduce_moved = [None] + [hop(reduce_lead[j], "x") for j in late]
             expand_early = spread(expand_early)
-            normed_grad = normed_back(low_near[:half]) + normed_far.astype(wide)
+            normed_parts = []
+            width = half // x_size
+            for x in range(x_size):
+                block = slice(x * width, (x + 1) * width)
+                part = normed_back(low_near[block]) + normed_far[block].astype(wide)
+                normed_parts.append(part.astype(low) if x == 1 else part)
             reduce_own = contract_rows(joined(0, 0), upstream_all).astype(low)
             reduce_wide = ()
         if step == 1:
             reduce_own = lax.psum_scatter(reduce_own, ("x", "c"), scatter_dimension=1, tiled=True)
-            normed_grad = ring_scatter(by_x(normed_grad), "x")
+            normed_moved = hop(normed_parts[1 % x_size], "x")
             expand_late = spread(expand_late)
             reduce_wide = [
                 x_finish(reduce_term, j, reduce_fars[j], reduce_moved[j]).astype(low) for j in late
@@ -794,17 +844,21 @@
             reduce_wide = spread(reduce_wide)
         state = (moved, across, project_grad, output_new, output_grad, reduce_wide)
         if step == 0:
-            state, expand_early, reduce_own, reduce_moved, expand_late, normed_grad = tie(
-                state, expand_early, reduce_own, reduce_moved, expand_late, normed_grad
+            state, expand_early, reduce_own, reduce_moved, expand_late, normed_parts = tie(
+                state, expand_early, reduce_own, reduce_moved, expand_late, normed_parts
             )
         elif step == 1:
             state, expand_own, expand_late = tie(state, expand_own, expand_late)
         else:
-            state, normed_grad = tie(state, normed_grad)
+            state, normed_moved, normed_parts = tie(state, normed_moved, normed_parts)
         moved, across, project_grad, output_new, output_grad, reduce_wide = state
         project_total = across + moved.astype(wide)
         output_part = output_rows_of(i) + output_new.astype(wide)
     output_part = inner_scatter([output_part[:, j * depth : (j + 1) * depth] for j in range(inner)])
+    for step in range(1, x_size):
+        normed_grad = normed_parts[(step + 1) % x_size] + normed_moved.astype(wide)
+        if step + 1 < x_size:
+            normed_moved = hop(normed_grad.astype(low), "x")
     expand_both = jnp.concatenate([expand_early, expand_late], 0).astype(wide)
     expand_both = expand_both + expand_own.astype(wide)
     reduce_part = reduce_wide.astype(wide) + reduce_own.astype(wide)

time: 629 us -> 615 us (0.978)
  waiting for transfers between devices: 174 us -> 166 us
  Pallas kernels: 35.8 us -> 28.5 us
    ppermute x6, waiting for transfers between devices: 67.5 us -> 43.9 us  [hop(): return lax.ppermute(value, axis, [(i, (i - 1) % size) for i in range(size)])]
    ppermute x42, waiting for transfers between devices: 94.5 us -> 113 us  [wide_from(): return lax.ppermute(value, 'w', pairs)]
    dot_general x19 -> x20, matrix products: 66.4 us -> 68.8 us  [contract_cols(): lax.dot_general(left, right, (((1,), (1,)), ((), ())), preferred_element_...]
    unnamed x271 -> x275, local copies, waits for them, and re-layouts: 16 us -> 16.3 us
  transfers between devices with their start and end apart: 67 -> 67, of which waited for: 35 -> 35; matrix products, arithmetic and copies ran while one was open for 43% -> 43% of each run, Pallas kernels for 6% -> 5%
where the time goes in v4:
time: 615 us; the launch traced here: 607 us
  matrix products  170 us (28%)
  waiting for transfers between devices  166 us (27%)
  other arithmetic  89.2 us (15%)
  starting transfers between devices  82.6 us (13%)
  local copies, waits for them, and re-layouts  49 us (8%)
  Pallas kernels  28.5 us (5%)
  between operations  22.8 us (4%)
    ppermute x42, waiting for transfers between devices, wide_from(): return lax.ppermute(value, 'w', pairs)  113 us
    dot_general x20, matrix products, contract_cols(): lax.dot_general(left, right, (((1,), (1,)), ((), ())), preferred_element_...  68.8 us
    ppermute x42, starting transfers between devices, wide_from(): return lax.ppermute(value, 'w', pairs)  67.7 us
    ppermute x6, waiting for transfers between devices, hop(): return lax.ppermute(value, axis, [(i, (i - 1) % size) for i in range(size)])  43.9 us
    dot_general x10, matrix products, contract_rows(): lax.dot_general(left, right, (((0,), (0,)), ((), ())), preferred_element_...  41.2 us
    dot_general x8, matrix products, hidden_part(): both = jnp.dot(mixed_parts[k], expand_all[j], preferred_element_type=wide)  32.1 us
    pallas_call x1, Pallas kernels, attend_back(): pl.pallas_call(functools.partial(attend_back_kernel, heads, groups, lengt...  18.6 us
    convert_element_type x5, other arithmetic, body(): made = [updated, first_new, second_new, updated.astype(low)]  17.7 us
  transfers between devices with their start and end apart: 67, of which 35 were waited for; matrix products, arithmetic and copies ran while one was open for 43% of the time, Pallas kernels for 5%

profile of v4, /device:TPU:0, one launch (start us, length us, event | category | flops | bytes accessed | tf_op | source)
XLA Modules:
  0.0 607.2 jit_solution(17149186660717543310)
XLA Ops:
  13.1 3.0 collective-permute-start.1
  16.1 3.6 collective-permute-start
  34.4 4.4 collective-permute-start.2
  40.1 7.9 %collective-permute-done.3 = bf16[256,1152]{1,0:T(8,128)(2,1)S(1)} collective-permute-done((bf16[256,1152]{1,0:T(8,128)(2,1)}, bf16[256,1152]{1,0:T(8,128)(2,1)S(1)}, u32[]{:S(2)}, u32[]{:S(2)}) %collective-permute-start.3) | collective-permute-done | bytes 589856 | tf_op jit(solution)/shard_map/ppermute | solution.py:409
  51.8 4.2 collective-permute-start.4
  62.9 3.9 collective-permute-done.4
  69.7 4.8 collective-permute-start.8
  76.3 3.8 collective-permute-done.6
  81.9 10.3 %fusion.158.raw.raw_all = f32[1024,1152]{1,0:T(8,128)} fusion(bf16[1024,2048]{1,0:T(8,128)(2,1)} %all-gather.6.cloned.1.call-done, bf16[2048,1152]{1,0:T(8,128)(2,1)} %constant_dynamic-update-slice_fusion.8), kind=kOutput, calls=%fused_computation.340 | convolution fusion | flops 4831838208 | bytes 13631488 | tf_op jit(solution)/shard_map/dot_general | solution.py:605
  92.2 4.4 collective-permute-start.14
  101.0 9.9 %shard_map.481 = (bf16[1024,512]{1,0:T(8,128)(2,1)}, bf16[1024,256]{1,0:T(8,128)(2,1)}, bf16[1024,256]{1,0:T(8,128)(2,1)}, f32[1024,512]{1,0:T(8,128)}, f32[1024...) custom-call(s32[4]{0:T(128)} %pad_add_fusion.slots, f32[1024,1152]{1,0:T(8,128)} %fusion.158.raw.raw_all, ...), custom_call_target="tpu_custom_call" | custom-call | flops 2147483648 | bytes 9961472 | tf_op jit(solution)/shard_map/pallas_call | solution.py:183
  110.9 4.9 collective-permute-done.14
  123.9 2.8 collective-permute-done.15
  130.9 12.0 %collective-permute-done.16 = bf16[128,2048]{1,0:T(8,128)(2,1)S(1)} collective-permute-done((bf16[128,2048]{1,0:T(8,128)(2,1)S(1)}, bf16[128,2048]{1,0:T(8,128)(2,1)S(1)}, u32[]{:S(2)}, u32[]{:S(2)}) %collective-permute-start.16) | collective-permute-done | bytes 524320 | tf_op jit(solution)/shard_map/ppermute | solution.py:379
  142.9 10.4 %collective-permute-done.19 = bf16[128,2048]{1,0:T(8,128)(2,1)S(1)} collective-permute-done((bf16[128,2048]{1,0:T(8,128)(2,1)S(1)}, bf16[128,2048]{1,0:T(8,128)(2,1)S(1)}, u32[]{:S(2)}, u32[]{:S(2)}) %collective-permute-start.19) | collective-permute-done | bytes 524320 | tf_op jit(solution)/shard_map/ppermute | solution.py:379
  155.1 4.2 collective-permute-done.18
  166.5 6.8 %fusion.159 = f32[256,1536]{1,0:T(8,128)} fusion(bf16[256,2048]{1,0:T(8,128)(2,1)S(1)} %multiply_convert_fusion, bf16[2048,1536]{1,0:T(8,128)(2,1)} %all-gather.8.cloned.1.call-done), kind=kOutput, calls=%fused_computation.341 | convolution fusion | flops 1610612736 | bytes 8912896 | tf_op jit(solution)/shard_map/dot_general | solution.py:641
  173.3 4.9 multiply_convert_fusion.23
  179.1 3.1 fusion.140
  182.2 8.1 %collective-permute-done.20 = bf16[256,2048]{1,0:T(8,128)(2,1)} collective-permute-done((bf16[256,2048]{1,0:T(8,128)(2,1)S(1)}, bf16[256,2048]{1,0:T(8,128)(2,1)}, u32[]{:S(2)}, u32[]{:S(2)}) %collective-permute-start.20) | collective-permute-done | bytes 1048608 | tf_op jit(solution)/shard_map/ppermute | solution.py:409
  190.3 19.9 %collective-permute-done.22 = bf16[256,2048]{1,0:T(8,128)(2,1)} collective-permute-done((bf16[256,2048]{1,0:T(8,128)(2,1)}, bf16[256,2048]{1,0:T(8,128)(2,1)}, u32[]{:S(2)}, u32[]{:S(2)}) %collective-permute-start.22) | collective-permute-done | bytes 1048608 | tf_op jit(solution)/shard_map/ppermute | solution.py:409
  212.8 5.0 fusion.160
  221.6 3.8 pad_maximum_fusion
  225.4 3.1 fusion.139
  228.6 4.7 collective-permute-done.23
  233.2 4.7 collective-permute-start.24
  238.0 3.0 fusion.162
  241.0 3.3 multiply_convert_fusion.14
  245.2 3.1 fusion.137
  248.4 6.1 fusion.161
  254.4 4.8 multiply_convert_fusion.17
  262.5 3.2 fusion.163
  265.8 3.5 multiply_convert_fusion.11
  272.0 3.2 fusion.164
  275.3 3.4 multiply_convert_fusion.8
  288.4 3.3 multiply_convert_fusion.5
  295.2 3.0 fusion.166
  298.2 3.3 multiply_convert_fusion.2
  312.9 9.0 %convolution_convert_fusion = bf16[2048,1536]{1,0:T(8,128)(2,1)} fusion(bf16[1024,2048]{1,0:T(8,128)(2,1)S(1)} %pad_maximum_fusion.1, bf16[256,1536]{1,0:T(8,128)(2,1)S(1)} %pad_maximum_fusion.12, bf16[256,1536]{1,0:T(8,128)(2,1)S(1)} %copy-done.77, bf16[256,1536]{1,0:T(8,128)(2,1)S(1)} %copy-done.76, bf16[256,1536]{1,0:T(8,128)(2,1)S(1)} %copy-done.75), kind=kOutput, calls=%fused_computation | convolution fusion | flops 6458179584 | bytes 13631488 | tf_op jit(solution)/shard_map/dot_general | solution.py:50
  321.9 3.1 fusion.167
  329.1 3.5 convolution_convert_fusion.1
  345.3 3.1 fusion.30
  348.4 12.9 %collective-permute-done.28 = bf16[256,2048]{1,0:T(8,128)(2,1)S(1)} collective-permute-done((bf16[256,2048]{1,0:T(8,128)(2,1)S(1)}, bf16[256,2048]{1,0:T(8,128)(2,1)S(1)}, u32[]{:S(2)}, u32[]{:S(2)}) %collective-permute-start.28) | collective-permute-done | bytes 1048608 | tf_op jit(solution)/shard_map/ppermute | solution.py:379
  372.2 3.7 fusion.170.gated_grad
  375.9 18.6 %shard_map.482 = (bf16[1024,1152]{1,0:T(8,128)(2,1)}, bf16[1024,1152]{1,0:T(8,128)(2,1)}, f32[2,128]{1,0:T(2,128)}) custom-call(s32[4]{0:T(128)} %pad_add_fusion.slots, f32[1024,512]{1,0:T(8,128)} %fusion.170.gated_grad, f32[1024,1152]{1,0:T(8,128)} %fusion.158.raw.raw_all, s32[1,1024]{1,0:T(1,128)} %subtract_subtract_fusion.1.start, ...), custom_call_target="tpu_custom_call" | custom-call | flops 5368709120 | bytes 13369344 | tf_op jit(solution)/shard_map/pallas_call | solution.py:325
  394.5 6.2 %collective-permute-done.35 = bf16[512,1536]{1,0:T(8,128)(2,1)} collective-permute-done((bf16[512,1536]{1,0:T(8,128)(2,1)}, bf16[512,1536]{1,0:T(8,128)(2,1)}, u32[]{:S(2)}, u32[]{:S(2)}) %collective-permute-start.35) | collective-permute-done | bytes 1572896 | tf_op jit(solution)/shard_map/ppermute | solution.py:379
  400.8 8.5 %fusion.171 = f32[2048,1152]{1,0:T(8,128)S(1)} fusion(bf16[1024,2048]{1,0:T(8,128)(2,1)} %all-gather.6.cloned.1.call-done, bf16[1024,1152]{1,0:T(8,128)(2,1)} %get-tuple-element.505), kind=kOutput, calls=%fused_computation.353 | convolution fusion | flops 4831838208 | bytes 15990784 | tf_op jit(solution)/shard_map/dot_general | solution.py:50
  421.9 6.6 %convolution_convert_fusion.3 = bf16[512,2048]{1,0:T(8,128)(2,1)} fusion(bf16[2048,1152]{1,0:T(8,128)(2,1)} %constant_dynamic-update-slice_fusion.8, bf16[1024,1152]{1,0:T(8,128)(2,1)S(1)} %copy-done.131), kind=kOutput, calls=%fused_computation.55 | convolution fusion | flops 2416967680 | bytes 7995392 | tf_op jit(solution)/shard_map/dot_general | solution.py:56
  428.6 3.7 fusion.33
  436.0 3.9 collective-permute-start.40
  445.2 5.1 convolution_convert_fusion.2
  450.3 7.0 %collective-permute-done.39 = bf16[256,1152]{1,0:T(8,128)(2,1)} collective-permute-done((bf16[256,1152]{1,0:T(8,128)(2,1)}, bf16[256,1152]{1,0:T(8,128)(2,1)}, u32[]{:S(2)}, u32[]{:S(2)}) %collective-permute-start.39) | collective-permute-done | bytes 589856 | tf_op jit(solution)/shard_map/ppermute | solution.py:409
  460.4 5.2 fusion.38
  465.6 5.5 convolution_add_fusion.7
  488.5 5.8 collective-permute-done.45
  496.9 8.0 %collective-permute-done.46 = bf16[512,512]{1,0:T(8,128)(2,1)S(1)} collective-permute-done((bf16[512,512]{1,0:T(8,128)(2,1)S(1)}, bf16[512,512]{1,0:T(8,128)(2,1)S(1)}, u32[]{:S(2)}, u32[]{:S(2)}) %collective-permute-start.46) | collective-permute-done | bytes 524320 | tf_op jit(solution)/shard_map/ppermute | solution.py:409
  511.3 3.8 collective-permute-start.48
  521.0 4.5 collective-permute-done.49
  527.0 10.3 %collective-permute-done.50 = bf16[512,512]{1,0:T(8,128)(2,1)S(1)} collective-permute-done((bf16[512,512]{1,0:T(8,128)(2,1)S(1)}, bf16[512,512]{1,0:T(8,128)(2,1)S(1)}, u32[]{:S(2)}, u32[]{:S(2)}) %collective-permute-start.50) | collective-permute-done | bytes 524320 | tf_op jit(solution)/shard_map/ppermute | solution.py:409
  558.2 3.3 fusion.173
  563.8 3.2 collective-permute-start.58
  571.2 3.0 collective-permute-start.59
  585.5 7.4 %fusion.143 = (bf16[2,512,768]{2,1,0:T(8,128)(2,1)}, f32[2,512,768]{2,1,0:T(8,128)}, f32[2,512,768]{2,1,0:T(8,128)}, f32[2,512,768]{2,1,0:T(8,128)}) fusion(f32[2,512,768]{2,1,0:T(8,128)S(1)} %copy-done.17, f32[]{:T(128)S(6)} %div.205, f32[1,512,768]{2,1,0:T(8,128)S(1)} %copy-done.15, f32[1,512,768]{2,1,0:T(8,128)S(1)} %copy-done.13, ...), kind=kLoop, calls=%fused_computation.331 | loop fusion | flops 14155776 | bytes 23592964 | tf_op jit(solution)/shard_map/convert_element_type | solution.py:914
  595.7 3.4 fusion.141
  (536 shorter events, 223.8 us)
Async XLA Ops:
  7.2 74.7 %all-gather.6.cloned.1.call-start = ((), (), s32[]{:S(2)}) async-start(), calls=%async_computation.2 | async-start | bytes 5242880 | tf_op jit(solution)/shard_map/all_gather | solution.py:565
  13.0 153.5 %all-gather.8.cloned.1.call-start = ((), (), s32[]{:S(2)}) async-start(), calls=%async_computation.3 | async-start | bytes 7864320 | tf_op jit(solution)/shard_map/all_gather | solution.py:571
  13.1 16.4 %collective-permute-start.1 = (bf16[256,1152]{1,0:T(8,128)(2,1)S(1)}, bf16[256,1152]{1,0:T(8,128)(2,1)S(1)}, u32[]{:S(2)}, u32[]{:S(2)}) collective-permute-start(bf16[256,1152]{1,0:T(8,128)(2,1)S(1)} %concatenate.106), channel_id=1, source_target_pairs={{1,0},{0,1},{3,2},{2,3},{5,4},{4,5},{7,6},{6,7},{9,8},{8,9},{11,10... | collective-permute-start | bytes 1769480 | tf_op jit(solution)/shard_map/ppermute | solution.py:409
  16.1 15.9 %collective-permute-start = (bf16[256,1152]{1,0:T(8,128)(2,1)S(1)}, bf16[256,1152]{1,0:T(8,128)(2,1)}, u32[]{:S(2)}, u32[]{:S(2)}) collective-permute-start(bf16[256,1152]{1,0:T(8,128)(2,1)S(1)} %concatenate.106), channel_id=1, source_target_pairs={{2,0},{3,1},{4,2},{5,3},{6,4},{7,5},{0,6},{1,7},{10,8},{11,9},{12,... | collective-permute-start | bytes 1769480 | tf_op jit(solution)/shard_map/ppermute | solution.py:409
  33.6 139.6 %all-gather.10.cloned.1.call-start = ((), (), s32[]{:S(2)}) async-start(), calls=%async_computation.4 | async-start | bytes 3932160 | tf_op jit(solution)/shard_map/all_gather | solution.py:574
  33.9 14.2 %collective-permute-start.3 = (bf16[256,1152]{1,0:T(8,128)(2,1)}, bf16[256,1152]{1,0:T(8,128)(2,1)S(1)}, u32[]{:S(2)}, u32[]{:S(2)}) collective-permute-start(bf16[256,1152]{1,0:T(8,128)(2,1)} %collective-permute-done), channel_id=1, source_target_pairs={{1,0},{0,1},{3,2},{2,3},{5,4},{4,5},{7,6},{6,7},{9,8},{8,9},{11,10... | collective-permute-start | bytes 1769480 | tf_op jit(solution)/shard_map/ppermute | solution.py:409
  34.4 15.8 %collective-permute-start.2 = (bf16[256,1152]{1,0:T(8,128)(2,1)}, bf16[256,1152]{1,0:T(8,128)(2,1)S(1)}, u32[]{:S(2)}, u32[]{:S(2)}) collective-permute-start(bf16[256,1152]{1,0:T(8,128)(2,1)} %collective-permute-done), channel_id=1, source_target_pairs={{2,0},{3,1},{4,2},{5,3},{6,4},{7,5},{0,6},{1,7},{10,8},{11,9},{12,... | collective-permute-start | bytes 1769480 | tf_op jit(solution)/shard_map/ppermute | solution.py:409
  50.2 12.7 %collective-permute-start.5 = (bf16[256,1152]{1,0:T(8,128)(2,1)S(1)}, bf16[256,1152]{1,0:T(8,128)(2,1)S(1)}, u32[]{:S(2)}, u32[]{:S(2)}) collective-permute-start(bf16[256,1152]{1,0:T(8,128)(2,1)S(1)} %collective-permute-done.2), channel_id=1, source_target_pairs={{1,0},{0,1},{3,2},{2,3},{5,4},{4,5},{7,6},{6,7},{9,8},{8,9},{11,10... | collective-permute-start | bytes 1769480 | tf_op jit(solution)/shard_map/ppermute | solution.py:409
  51.8 15.0 %collective-permute-start.4 = (bf16[256,1152]{1,0:T(8,128)(2,1)S(1)}, bf16[256,1152]{1,0:T(8,128)(2,1)S(1)}, u32[]{:S(2)}, u32[]{:S(2)}) collective-permute-start(bf16[256,1152]{1,0:T(8,128)(2,1)S(1)} %collective-permute-done.2), channel_id=1, source_target_pairs={{2,0},{3,1},{4,2},{5,3},{6,4},{7,5},{0,6},{1,7},{10,8},{11,9},{12,... | collective-permute-start | bytes 1769480 | tf_op jit(solution)/shard_map/ppermute | solution.py:409
  66.8 13.3 %collective-permute-start.6 = (bf16[256,1152]{1,0:T(8,128)(2,1)S(1)}, bf16[256,1152]{1,0:T(8,128)(2,1)S(1)}, u32[]{:S(2)}, u32[]{:S(2)}) collective-permute-start(bf16[256,1152]{1,0:T(8,128)(2,1)S(1)} %collective-permute-done.4), channel_id=1, source_target_pairs={{1,0},{0,1},{3,2},{2,3},{5,4},{4,5},{7,6},{6,7},{9,8},{8,9},{11,10... | collective-permute-start | bytes 1769480 | tf_op jit(solution)/shard_map/ppermute | solution.py:409
  68.2 24.0 %collective-permute-start.10 = (bf16[512,256]{1,0:T(8,128)(2,1)S(1)}, bf16[512,256]{1,0:T(8,128)(2,1)}, u32[]{:S(2)}, u32[]{:S(2)}) collective-permute-start(bf16[512,256]{1,0:T(8,128)(2,1)S(1)} %convert_element_type.310), channel_id=1, source_target_pairs={{1,0},{0,1},{3,2},{2,3},{5,4},{4,5},{7,6},{6,7},{9,8},{8,9},{11,10... | collective-permute-start | bytes 786440 | tf_op jit(solution)/shard_map/ppermute | solution.py:409
  69.7 22.5 %collective-permute-start.9 = (bf16[512,256]{1,0:T(8,128)(2,1)S(1)}, bf16[512,256]{1,0:T(8,128)(2,1)S(1)}, u32[]{:S(2)}, u32[]{:S(2)}) collective-permute-start(bf16[512,256]{1,0:T(8,128)(2,1)S(1)} %convert_element_type.310), channel_id=1, source_target_pairs={{6,0},{7,1},{0,2},{1,3},{2,4},{3,5},{4,6},{5,7},{14,8},{15,9},{8,1... | collective-permute-start | bytes 786440 | tf_op jit(solution)/shard_map/ppermute | solution.py:409
  69.7 22.5 %collective-permute-start.8 = (bf16[512,256]{1,0:T(8,128)(2,1)S(1)}, bf16[512,256]{1,0:T(8,128)(2,1)S(1)}, u32[]{:S(2)}, u32[]{:S(2)}) collective-permute-start(bf16[512,256]{1,0:T(8,128)(2,1)S(1)} %convert_element_type.310), channel_id=1, source_target_pairs={{4,0},{5,1},{6,2},{7,3},{0,4},{1,5},{2,6},{3,7},{12,8},{13,9},{14,... | collective-permute-start | bytes 786440 | tf_op jit(solution)/shard_map/ppermute | solution.py:409
  74.6 17.7 %collective-permute-start.7 = (bf16[512,256]{1,0:T(8,128)(2,1)S(1)}, bf16[512,256]{1,0:T(8,128)(2,1)}, u32[]{:S(2)}, u32[]{:S(2)}) collective-permute-start(bf16[512,256]{1,0:T(8,128)(2,1)S(1)} %convert_element_type.310), channel_id=1, source_target_pairs={{2,0},{3,1},{4,2},{5,3},{6,4},{7,5},{0,6},{1,7},{10,8},{11,9},{12,... | collective-permute-start | bytes 786440 | tf_op jit(solution)/shard_map/ppermute | solution.py:409
  92.2 23.5 %collective-permute-start.14 = (bf16[256,2048]{1,0:T(8,128)(2,1)}, bf16[256,2048]{1,0:T(8,128)(2,1)}, u32[]{:S(2)}, u32[]{:S(2)}) collective-permute-start(bf16[256,2048]{1,0:T(8,128)(2,1)} %fusion.59), channel_id=1, source_target_pairs={{2,0},{3,1},{4,2},{5,3},{6,4},{7,5},{0,6},{1,7},{10,8},{11,9},{12,... | collective-permute-start | bytes 3145736 | tf_op jit(solution)/shard_map/ppermute | solution.py:409
  96.6 14.3 %collective-permute-start.11 = (bf16[512,256]{1,0:T(8,128)(2,1)}, bf16[512,256]{1,0:T(8,128)(2,1)}, u32[]{:S(2)}, u32[]{:S(2)}) collective-permute-start(bf16[512,256]{1,0:T(8,128)(2,1)} %collective-permute-done.7), channel_id=1, source_target_pairs={{1,0},{0,1},{3,2},{2,3},{5,4},{4,5},{7,6},{6,7},{9,8},{8,9},{11,10... | collective-permute-start | bytes 786440 | tf_op jit(solution)/shard_map/ppermute | solution.py:409
  97.1 13.8 %collective-permute-start.12 = (bf16[512,256]{1,0:T(8,128)(2,1)S(1)}, bf16[512,256]{1,0:T(8,128)(2,1)}, u32[]{:S(2)}, u32[]{:S(2)}) collective-permute-start(bf16[512,256]{1,0:T(8,128)(2,1)S(1)} %collective-permute-done.8), channel_id=1, source_target_pairs={{1,0},{0,1},{3,2},{2,3},{5,4},{4,5},{7,6},{6,7},{9,8},{8,9},{11,10... | collective-permute-start | bytes 786440 | tf_op jit(solution)/shard_map/ppermute | solution.py:409
  98.6 12.3 %collective-permute-start.13 = (bf16[512,256]{1,0:T(8,128)(2,1)S(1)}, bf16[512,256]{1,0:T(8,128)(2,1)}, u32[]{:S(2)}, u32[]{:S(2)}) collective-permute-start(bf16[512,256]{1,0:T(8,128)(2,1)S(1)} %collective-permute-done.9), channel_id=1, source_target_pairs={{1,0},{0,1},{3,2},{2,3},{5,4},{4,5},{7,6},{6,7},{9,8},{8,9},{11,10... | collective-permute-start | bytes 786440 | tf_op jit(solution)/shard_map/ppermute | solution.py:409
  100.7 147.6 %all-gather.12.cloned.1.call-start = ((), (), s32[]{:S(2)}) async-start(), calls=%async_computation.5 | async-start | bytes 7864320 | tf_op jit(solution)/shard_map/all_gather | solution.py:571
  122.5 4.2 collective-permute-start.15
  123.4 36.0 %collective-permute-start.18 = (bf16[512,1536]{1,0:T(8,128)(2,1)S(1)}, bf16[512,1536]{1,0:T(8,128)(2,1)S(1)}, u32[]{:S(2)}, u32[]{:S(2)}) collective-permute-start(bf16[512,1536]{1,0:T(8,128)(2,1)S(1)} %copy-done.26), channel_id=1, source_target_pairs={{1,0},{0,1},{3,2},{2,3},{5,4},{4,5},{7,6},{6,7},{9,8},{8,9},{11,10... | collective-permute-start | bytes 4718600 | tf_op jit(solution)/shard_map/ppermute | solution.py:409
  128.1 14.8 %collective-permute-start.16 = (bf16[128,2048]{1,0:T(8,128)(2,1)S(1)}, bf16[128,2048]{1,0:T(8,128)(2,1)S(1)}, u32[]{:S(2)}, u32[]{:S(2)}) collective-permute-start(bf16[128,2048]{1,0:T(8,128)(2,1)S(1)} %get-tuple-element.661), channel_id=1, source_target_pairs={{0,16},{16,0},{1,17},{17,1},{2,18},{18,2},{3,19},{19,3},{4,20},{20... | collective-permute-start | bytes 1572872 | tf_op jit(solution)/shard_map/ppermute | solution.py:379
  129.7 23.6 %collective-permute-start.19 = (bf16[128,2048]{1,0:T(8,128)(2,1)S(1)}, bf16[128,2048]{1,0:T(8,128)(2,1)S(1)}, u32[]{:S(2)}, u32[]{:S(2)}) collective-permute-start(bf16[128,2048]{1,0:T(8,128)(2,1)S(1)} %get-tuple-element.662), channel_id=1, source_target_pairs={{0,16},{16,0},{1,17},{17,1},{2,18},{18,2},{3,19},{19,3},{4,20},{20... | collective-permute-start | bytes 1572872 | tf_op jit(solution)/shard_map/ppermute | solution.py:379
  130.2 25.0 %collective-permute-start.17 = (bf16[256,2048]{1,0:T(8,128)(2,1)}, bf16[256,2048]{1,0:T(8,128)(2,1)}, u32[]{:S(2)}, u32[]{:S(2)}) collective-permute-start(bf16[256,2048]{1,0:T(8,128)(2,1)} %collective-permute-done.14), channel_id=1, source_target_pairs={{2,0},{3,1},{4,2},{5,3},{6,4},{7,5},{0,6},{1,7},{10,8},{11,9},{12,... | collective-permute-start | bytes 3145736 | tf_op jit(solution)/shard_map/ppermute | solution.py:409
  160.5 93.9 %all-gather.14.cloned.1.call-start = ((), (), s32[]{:S(2)}) async-start(), calls=%async_computation.6 | async-start | bytes 3932160 | tf_op jit(solution)/shard_map/all_gather | solution.py:574
  160.6 21.6 %collective-permute-start.21 = (bf16[768,512]{1,0:T(8,128)(2,1)}, bf16[768,512]{1,0:T(8,128)(2,1)}, u32[]{:S(2)}, u32[]{:S(2)}) collective-permute-start(bf16[768,512]{1,0:T(8,128)(2,1)} %convert_element_type.315), channel_id=1, source_target_pairs={{1,0},{0,1},{3,2},{2,3},{5,4},{4,5},{7,6},{6,7},{9,8},{8,9},{11,10... | collective-permute-start | bytes 2359304 | tf_op jit(solution)/shard_map/ppermute | solution.py:409
  164.0 26.3 %collective-permute-start.20 = (bf16[256,2048]{1,0:T(8,128)(2,1)S(1)}, bf16[256,2048]{1,0:T(8,128)(2,1)}, u32[]{:S(2)}, u32[]{:S(2)}) collective-permute-start(bf16[256,2048]{1,0:T(8,128)(2,1)S(1)} %multiply_convert_fusion), channel_id=1, source_target_pairs={{2,0},{3,1},{4,2},{5,3},{6,4},{7,5},{0,6},{1,7},{10,8},{11,9},{12,... | collective-permute-start | bytes 3145736 | tf_op jit(solution)/shard_map/ppermute | solution.py:409
  164.8 45.4 %collective-permute-start.22 = (bf16[256,2048]{1,0:T(8,128)(2,1)}, bf16[256,2048]{1,0:T(8,128)(2,1)}, u32[]{:S(2)}, u32[]{:S(2)}) collective-permute-start(bf16[256,2048]{1,0:T(8,128)(2,1)} %collective-permute-done.17), channel_id=1, source_target_pairs={{2,0},{3,1},{4,2},{5,3},{6,4},{7,5},{0,6},{1,7},{10,8},{11,9},{12,... | collective-permute-start | bytes 3145736 | tf_op jit(solution)/shard_map/ppermute | solution.py:409
  210.2 23.0 %collective-permute-start.23 = (bf16[256,2048]{1,0:T(8,128)(2,1)}, bf16[256,2048]{1,0:T(8,128)(2,1)}, u32[]{:S(2)}, u32[]{:S(2)}) collective-permute-start(bf16[256,2048]{1,0:T(8,128)(2,1)} %collective-permute-done.20), channel_id=1, source_target_pairs={{2,0},{3,1},{4,2},{5,3},{6,4},{7,5},{0,6},{1,7},{10,8},{11,9},{12,... | collective-permute-start | bytes 3145736 | tf_op jit(solution)/shard_map/ppermute | solution.py:409
  212.8 295.0 %reduce-scatter.3.cloned.1.call-start = ((), (), s32[]{:S(2)}) async-start(), calls=%async_computation.7 | async-start | bytes 7864320 | tf_op jit(solution)/shard_map/reduce_scatter | solution.py:784
  233.2 29.1 %collective-permute-start.24 = (bf16[256,2048]{1,0:T(8,128)(2,1)}, bf16[256,2048]{1,0:T(8,128)(2,1)}, u32[]{:S(2)}, u32[]{:S(2)}) collective-permute-start(bf16[256,2048]{1,0:T(8,128)(2,1)} %collective-permute-done.23), channel_id=1, source_target_pairs={{2,0},{3,1},{4,2},{5,3},{6,4},{7,5},{0,6},{1,7},{10,8},{11,9},{12,... | collective-permute-start | bytes 3145736 | tf_op jit(solution)/shard_map/ppermute | solution.py:409
  262.4 22.9 %collective-permute-start.25 = (bf16[256,2048]{1,0:T(8,128)(2,1)S(1)}, bf16[256,2048]{1,0:T(8,128)(2,1)S(1)}, u32[]{:S(2)}, u32[]{:S(2)}) collective-permute-start(bf16[256,2048]{1,0:T(8,128)(2,1)S(1)} %add.577), channel_id=1, source_target_pairs={{2,0},{3,1},{4,2},{5,3},{6,4},{7,5},{0,6},{1,7},{10,8},{11,9},{12,... | collective-permute-start | bytes 3145736 | tf_op jit(solution)/shard_map/ppermute | solution.py:409
  285.6 21.9 %collective-permute-start.26 = (bf16[256,2048]{1,0:T(8,128)(2,1)S(1)}, bf16[256,2048]{1,0:T(8,128)(2,1)S(1)}, u32[]{:S(2)}, u32[]{:S(2)}) collective-permute-start(bf16[256,2048]{1,0:T(8,128)(2,1)S(1)} %add_convert_fusion.1), channel_id=1, source_target_pairs={{2,0},{3,1},{4,2},{5,3},{6,4},{7,5},{0,6},{1,7},{10,8},{11,9},{12,... | collective-permute-start | bytes 3145736 | tf_op jit(solution)/shard_map/ppermute | solution.py:409
  308.7 23.9 %collective-permute-start.27 = (bf16[256,2048]{1,0:T(8,128)(2,1)}, bf16[256,2048]{1,0:T(8,128)(2,1)S(1)}, u32[]{:S(2)}, u32[]{:S(2)}) collective-permute-start(bf16[256,2048]{1,0:T(8,128)(2,1)} %add_convert_fusion), channel_id=1, source_target_pairs={{2,0},{3,1},{4,2},{5,3},{6,4},{7,5},{0,6},{1,7},{10,8},{11,9},{12,... | collective-permute-start | bytes 3145736 | tf_op jit(solution)/shard_map/ppermute | solution.py:409
  332.7 12.6 %collective-permute-start.30 = (bf16[1024,1536]{1,0:T(8,128)(2,1)S(1)}, bf16[1024,1536]{1,0:T(8,128)(2,1)S(1)}, u32[]{:S(2)}, u32[]{:S(2)}) collective-permute-start(bf16[1024,1536]{1,0:T(8,128)(2,1)S(1)} %convolution_convert_fusion.1), channel_id=1, source_target_pairs={{0,8},{8,0},{1,9},{9,1},{2,10},{10,2},{3,11},{11,3},{4,12},{12,4},... | collective-permute-start | bytes 9437192 | tf_op jit(solution)/shard_map/ppermute | solution.py:374
  336.0 25.3 %collective-permute-start.28 = (bf16[256,2048]{1,0:T(8,128)(2,1)S(1)}, bf16[256,2048]{1,0:T(8,128)(2,1)S(1)}, u32[]{:S(2)}, u32[]{:S(2)}) collective-permute-start(bf16[256,2048]{1,0:T(8,128)(2,1)S(1)} %get-tuple-element.464), channel_id=1, source_target_pairs={{0,16},{16,0},{1,17},{17,1},{2,18},{18,2},{3,19},{19,3},{4,20},{20... | collective-permute-start | bytes 3145736 | tf_op jit(solution)/shard_map/ppermute | solution.py:379
  337.6 25.4 %collective-permute-start.29 = (bf16[256,2048]{1,0:T(8,128)(2,1)S(1)}, bf16[256,2048]{1,0:T(8,128)(2,1)S(1)}, u32[]{:S(2)}, u32[]{:S(2)}) collective-permute-start(bf16[256,2048]{1,0:T(8,128)(2,1)S(1)} %fusion.39), channel_id=1, source_target_pairs={{2,0},{3,1},{4,2},{5,3},{6,4},{7,5},{0,6},{1,7},{10,8},{11,9},{12,... | collective-permute-start | bytes 3145736 | tf_op jit(solution)/shard_map/ppermute | solution.py:409
  363.0 7.2 %collective-permute-start.33 = (bf16[768,1024]{1,0:T(8,128)(2,1)S(1)}, bf16[768,1024]{1,0:T(8,128)(2,1)S(1)}, u32[]{:S(2)}, u32[]{:S(2)}) collective-permute-start(bf16[768,1024]{1,0:T(8,128)(2,1)S(1)} %fusion.60), channel_id=1, source_target_pairs={{0,8},{8,0},{1,9},{9,1},{2,10},{10,2},{3,11},{11,3},{4,12},{12,4},... | collective-permute-start | bytes 4718600 | tf_op jit(solution)/shard_map/ppermute | solution.py:374
  363.0 4.9 collective-permute-start.31
  363.5 5.9 collective-permute-start.32
  363.5 37.1 %collective-permute-start.35 = (bf16[512,1536]{1,0:T(8,128)(2,1)}, bf16[512,1536]{1,0:T(8,128)(2,1)}, u32[]{:S(2)}, u32[]{:S(2)}) collective-permute-start(bf16[512,1536]{1,0:T(8,128)(2,1)} %fusion.30), channel_id=1, source_target_pairs={{0,16},{16,0},{1,17},{17,1},{2,18},{18,2},{3,19},{19,3},{4,20},{20... | collective-permute-start | bytes 4718600 | tf_op jit(solution)/shard_map/ppermute | solution.py:379
  364.4 30.1 %collective-permute-start.34 = (bf16[256,2048]{1,0:T(8,128)(2,1)S(1)}, bf16[256,2048]{1,0:T(8,128)(2,1)S(1)}, u32[]{:S(2)}, u32[]{:S(2)}) collective-permute-start(bf16[256,2048]{1,0:T(8,128)(2,1)S(1)} %add.606), channel_id=1, source_target_pairs={{2,0},{3,1},{4,2},{5,3},{6,4},{7,5},{0,6},{1,7},{10,8},{11,9},{12,... | collective-permute-start | bytes 3145736 | tf_op jit(solution)/shard_map/ppermute | solution.py:409
  400.7 150.8 %reduce-scatter.5.cloned.1.call-start = ((), (), s32[]{:S(2)}) async-start(), calls=%async_computation.8 | async-start | bytes 3932160 | tf_op jit(solution)/shard_map/reduce_scatter | solution.py:837
  409.3 25.1 %collective-permute-start.36 = (bf16[256,1152]{1,0:T(8,128)(2,1)S(1)}, bf16[256,1152]{1,0:T(8,128)(2,1)S(1)}, u32[]{:S(2)}, u32[]{:S(2)}) collective-permute-start(bf16[256,1152]{1,0:T(8,128)(2,1)S(1)} %dynamic-slice_convert_fusion.3), channel_id=1, source_target_pairs={{1,0},{0,1},{3,2},{2,3},{5,4},{4,5},{7,6},{6,7},{9,8},{8,9},{11,10... | collective-permute-start | bytes 1769480 | tf_op jit(solution)/shard_map/ppermute | solution.py:409
  411.4 24.6 %collective-permute-start.37 = (bf16[256,2048]{1,0:T(8,128)(2,1)S(1)}, bf16[256,2048]{1,0:T(8,128)(2,1)S(1)}, u32[]{:S(2)}, u32[]{:S(2)}) collective-permute-start(bf16[256,2048]{1,0:T(8,128)(2,1)S(1)} %add.611), channel_id=1, source_target_pairs={{2,0},{3,1},{4,2},{5,3},{6,4},{7,5},{0,6},{1,7},{10,8},{11,9},{12,... | collective-permute-start | bytes 3145736 | tf_op jit(solution)/shard_map/ppermute | solution.py:409
  435.9 24.4 %collective-permute-start.43 = (bf16[512,2048]{1,0:T(8,128)(2,1)}, bf16[512,2048]{1,0:T(8,128)(2,1)}, u32[]{:S(2)}, u32[]{:S(2)}) collective-permute-start(bf16[512,2048]{1,0:T(8,128)(2,1)} %convolution_convert_fusion.3), channel_id=1, source_target_pairs={{0,8},{8,0},{1,9},{9,1},{2,10},{10,2},{3,11},{11,3},{4,12},{12,4},... | collective-permute-start | bytes 6291464 | tf_op jit(solution)/shard_map/ppermute | solution.py:374
  436.0 35.2 %collective-permute-start.40 = (bf16[512,512]{1,0:T(8,128)(2,1)}, bf16[512,512]{1,0:T(8,128)(2,1)}, u32[]{:S(2)}, u32[]{:S(2)}) collective-permute-start(bf16[512,512]{1,0:T(8,128)(2,1)} %pad_maximum_fusion.6), channel_id=1, source_target_pairs={{2,0},{3,1},{4,2},{5,3},{6,4},{7,5},{0,6},{1,7},{10,8},{11,9},{12,... | collective-permute-start | bytes 1572872 | tf_op jit(solution)/shard_map/ppermute | solution.py:409
  440.8 16.5 %collective-permute-start.39 = (bf16[256,1152]{1,0:T(8,128)(2,1)}, bf16[256,1152]{1,0:T(8,128)(2,1)}, u32[]{:S(2)}, u32[]{:S(2)}) collective-permute-start(bf16[256,1152]{1,0:T(8,128)(2,1)} %dynamic-slice_convert_fusion.2), channel_id=1, source_target_pairs={{1,0},{0,1},{3,2},{2,3},{5,4},{4,5},{7,6},{6,7},{9,8},{8,9},{11,10... | collective-permute-start | bytes 1769480 | tf_op jit(solution)/shard_map/ppermute | solution.py:409
  441.3 29.8 %collective-permute-start.38 = (bf16[256,1152]{1,0:T(8,128)(2,1)}, bf16[256,1152]{1,0:T(8,128)(2,1)}, u32[]{:S(2)}, u32[]{:S(2)}) collective-permute-start(bf16[256,1152]{1,0:T(8,128)(2,1)} %convert_add_fusion.10), channel_id=1, source_target_pairs={{2,0},{3,1},{4,2},{5,3},{6,4},{7,5},{0,6},{1,7},{10,8},{11,9},{12,... | collective-permute-start | bytes 1769480 | tf_op jit(solution)/shard_map/ppermute | solution.py:409
  441.5 31.8 %collective-permute-start.41 = (bf16[256,1536]{1,0:T(8,128)(2,1)}, bf16[256,1536]{1,0:T(8,128)(2,1)S(1)}, u32[]{:S(2)}, u32[]{:S(2)}) collective-permute-start(bf16[256,1536]{1,0:T(8,128)(2,1)} %get-tuple-element.549), channel_id=1, source_target_pairs={{1,0},{0,1},{3,2},{2,3},{5,4},{4,5},{7,6},{6,7},{9,8},{8,9},{11,10... | collective-permute-start | bytes 2359304 | tf_op jit(solution)/shard_map/ppermute | solution.py:409
  457.3 18.3 %collective-permute-start.42 = (bf16[768,512]{1,0:T(8,128)(2,1)}, bf16[768,512]{1,0:T(8,128)(2,1)}, u32[]{:S(2)}, u32[]{:S(2)}) collective-permute-start(bf16[768,512]{1,0:T(8,128)(2,1)} %add_convert_fusion.3), channel_id=1, source_target_pairs={{0,16},{16,0},{1,17},{17,1},{2,18},{18,2},{3,19},{19,3},{4,20},{20... | collective-permute-start | bytes 2359304 | tf_op jit(solution)/shard_map/ppermute | solution.py:379
  477.8 16.6 %collective-permute-start.45 = (bf16[256,1152]{1,0:T(8,128)(2,1)}, bf16[256,1152]{1,0:T(8,128)(2,1)}, u32[]{:S(2)}, u32[]{:S(2)}) collective-permute-start(bf16[256,1152]{1,0:T(8,128)(2,1)} %dynamic-slice_convert_fusion.1), channel_id=1, source_target_pairs={{1,0},{0,1},{3,2},{2,3},{5,4},{4,5},{7,6},{6,7},{9,8},{8,9},{11,10... | collective-permute-start | bytes 1769480 | tf_op jit(solution)/shard_map/ppermute | solution.py:409
  479.8 25.1 %collective-permute-start.44 = (bf16[256,1152]{1,0:T(8,128)(2,1)S(1)}, bf16[256,1152]{1,0:T(8,128)(2,1)}, u32[]{:S(2)}, u32[]{:S(2)}) collective-permute-start(bf16[256,1152]{1,0:T(8,128)(2,1)S(1)} %add_convert_fusion.5), channel_id=1, source_target_pairs={{2,0},{3,1},{4,2},{5,3},{6,4},{7,5},{0,6},{1,7},{10,8},{11,9},{12,... | collective-permute-start | bytes 1769480 | tf_op jit(solution)/shard_map/ppermute | solution.py:409
  481.9 25.9 %collective-permute-start.47 = (bf16[256,1536]{1,0:T(8,128)(2,1)}, bf16[256,1536]{1,0:T(8,128)(2,1)}, u32[]{:S(2)}, u32[]{:S(2)}) collective-permute-start(bf16[256,1536]{1,0:T(8,128)(2,1)} %get-tuple-element.570), channel_id=1, source_target_pairs={{1,0},{0,1},{3,2},{2,3},{5,4},{4,5},{7,6},{6,7},{9,8},{8,9},{11,10... | collective-permute-start | bytes 2359304 | tf_op jit(solution)/shard_map/ppermute | solution.py:409
  484.9 20.0 %collective-permute-start.46 = (bf16[512,512]{1,0:T(8,128)(2,1)S(1)}, bf16[512,512]{1,0:T(8,128)(2,1)S(1)}, u32[]{:S(2)}, u32[]{:S(2)}) collective-permute-start(bf16[512,512]{1,0:T(8,128)(2,1)S(1)} %fusion.98), channel_id=1, source_target_pairs={{2,0},{3,1},{4,2},{5,3},{6,4},{7,5},{0,6},{1,7},{10,8},{11,9},{12,... | collective-permute-start | bytes 1572872 | tf_op jit(solution)/shard_map/ppermute | solution.py:409
  485.5 41.5 %collective-permute-start.52 = (bf16[256,2048]{1,0:T(8,128)(2,1)}, bf16[256,2048]{1,0:T(8,128)(2,1)S(1)}, u32[]{:S(2)}, u32[]{:S(2)}) collective-permute-start(bf16[256,2048]{1,0:T(8,128)(2,1)} %fusion.38), channel_id=1, source_target_pairs={{0,16},{16,0},{1,17},{17,1},{2,18},{18,2},{3,19},{19,3},{4,20},{20... | collective-permute-start | bytes 3145736 | tf_op jit(solution)/shard_map/ppermute | solution.py:379
  509.2 16.3 %collective-permute-start.49 = (bf16[256,1152]{1,0:T(8,128)(2,1)S(1)}, bf16[256,1152]{1,0:T(8,128)(2,1)S(1)}, u32[]{:S(2)}, u32[]{:S(2)}) collective-permute-start(bf16[256,1152]{1,0:T(8,128)(2,1)S(1)} %dynamic-slice_convert_fusion), channel_id=1, source_target_pairs={{1,0},{0,1},{3,2},{2,3},{5,4},{4,5},{7,6},{6,7},{9,8},{8,9},{11,10... | collective-permute-start | bytes 1769480 | tf_op jit(solution)/shard_map/ppermute | solution.py:409
  511.3 25.9 %collective-permute-start.48 = (bf16[256,1152]{1,0:T(8,128)(2,1)S(1)}, bf16[256,1152]{1,0:T(8,128)(2,1)S(1)}, u32[]{:S(2)}, u32[]{:S(2)}) collective-permute-start(bf16[256,1152]{1,0:T(8,128)(2,1)S(1)} %add_convert_fusion.4), channel_id=1, source_target_pairs={{2,0},{3,1},{4,2},{5,3},{6,4},{7,5},{0,6},{1,7},{10,8},{11,9},{12,... | collective-permute-start | bytes 1769480 | tf_op jit(solution)/shard_map/ppermute | solution.py:409
  515.1 23.0 %collective-permute-start.51 = (bf16[768,512]{1,0:T(8,128)(2,1)S(1)}, bf16[768,512]{1,0:T(8,128)(2,1)S(1)}, u32[]{:S(2)}, u32[]{:S(2)}) collective-permute-start(bf16[768,512]{1,0:T(8,128)(2,1)S(1)} %copy-done.78), channel_id=1, source_target_pairs={{1,0},{0,1},{3,2},{2,3},{5,4},{4,5},{7,6},{6,7},{9,8},{8,9},{11,10... | collective-permute-start | bytes 2359304 | tf_op jit(solution)/shard_map/ppermute | solution.py:409
  516.8 20.4 %collective-permute-start.50 = (bf16[512,512]{1,0:T(8,128)(2,1)S(1)}, bf16[512,512]{1,0:T(8,128)(2,1)S(1)}, u32[]{:S(2)}, u32[]{:S(2)}) collective-permute-start(bf16[512,512]{1,0:T(8,128)(2,1)S(1)} %fusion.99), channel_id=1, source_target_pairs={{2,0},{3,1},{4,2},{5,3},{6,4},{7,5},{0,6},{1,7},{10,8},{11,9},{12,... | collective-permute-start | bytes 1572872 | tf_op jit(solution)/shard_map/ppermute | solution.py:409
  543.4 10.4 %collective-permute-start.53 = (bf16[512,256]{1,0:T(8,128)(2,1)}, bf16[512,256]{1,0:T(8,128)(2,1)}, u32[]{:S(2)}, u32[]{:S(2)}) collective-permute-start(bf16[512,256]{1,0:T(8,128)(2,1)} %slice.387), channel_id=1, source_target_pairs={{1,0},{0,1},{3,2},{2,3},{5,4},{4,5},{7,6},{6,7},{9,8},{8,9},{11,10... | collective-permute-start | bytes 786440 | tf_op jit(solution)/shard_map/ppermute | solution.py:409
  557.7 3.8 collective-permute-start.54
  563.8 5.0 collective-permute-start.58
  571.2 5.1 collective-permute-start.59
  (140 other events, 789.6 us)
Sparse Core Ops, SparseCore 0:
  13.1 37.1 all-gather.5
  52.5 46.3 all-gather.7
  101.0 28.5 all-gather.9
  160.7 44.7 all-gather.11
  212.9 26.8 all-gather.13
  400.8 57.1 reduce-scatter.2
  478.4 48.8 reduce-scatter.4

commit v5 on v4

--- a/solution.py
+++ b/solution.py
@@ -751,7 +751,8 @@
     )
     residual_far = [swapped(piece, "c", 1) for piece in residual_row]
     reduce_fars = [None] + [swapped(reduce_fars[j], "c", 1) for j in late]
-    expand_moved = [None] + [hop(expand_lead[j], "x") for j in late]
+    gate_moved = [hop(expand_lead[j][:, :hidden], "x") for j in late]
+    up_moved = [hop(expand_lead[j][:, hidden:], "x") for j in late]
     residual_all = jnp.concatenate(residual_row + residual_far, 0)
     residual_all, reduce_fars, done = tie(residual_all, reduce_fars, done)
     slots = wide_slots()
@@ -778,8 +779,8 @@
         heads,
         groups,
     )
-    back, output_total, done, residual_all, expand_moved, expand_own, upstream_all = tie(
-        back, output_total, done, residual_all, expand_moved, expand_own, upstream_all
+    back, output_total, done, residual_all, gate_moved, expand_own, upstream_all = tie(
+        back, output_total, done, residual_all, gate_moved, expand_own, upstream_all
     )
     expand_own = lax.psum_scatter(expand_own, ("x", "c"), scatter_dimension=0, tiled=True)
     low_grads, low_near, head_gain_grads = back
@@ -788,9 +789,10 @@
         return contract_cols(rows, project_all)
 
     project_grad = pinned(contract_rows(group_in, low_grads))
-    project_grad, low_near, done, upstream_all, residual_all, expand_moved, reduce_fars, output_total = tie(
-        project_grad, low_near, done, upstream_all, residual_all, expand_moved, reduce_fars, output_total
-    )
+    project_grad, low_near, done, upstream_all, residual_all, gate_moved, reduce_fars, output_total = tie(
+        project_grad, low_near, done, upstream_all, residual_all, gate_moved, reduce_fars, output_total
+    )
+    expand_moved = [None] + [jnp.concatenate(pair, 1) for pair in zip(gate_moved, up_moved)]
     output_total = outer_shift(output_sums[3] + output_total, 1)
 
     def spread(parts):
@@ -820,9 +822,11 @@
     for step, i in enumerate(order[1:]):
         moved = outer_shift(project_total.astype(low), 1)
         across = inner_scatter(wide_parts(project_grad, 0, i))
+        if step == 0:
+            normed_far = swapped(normed_far, "c", 1)
+            normed_far, output_part = tie(normed_far, output_part)
         output_new = outer_shift(output_part.astype(low), 1)
         if step == 0:
-            normed_far = swapped(normed_far, "c", 1)
             reduce_moved = [None] + [hop(reduce_lead[j], "x") for j in late]
             expand_early = spread(expand_early)
             normed_parts = []

time: 615 us -> 613 us (level)
  waiting for transfers between devices: 166 us -> 149 us
  starting transfers between devices: 82.6 us -> 91.8 us
    ppermute x42, waiting for transfers between devices: 113 us -> 104 us  [wide_from(): return lax.ppermute(value, 'w', pairs)]
    ppermute x42, starting transfers between devices: 67.7 us -> 75.4 us  [wide_from(): return lax.ppermute(value, 'w', pairs)]
    ppermute x6 -> x7, waiting for transfers between devices: 43.9 us -> 37.2 us  [hop(): return lax.ppermute(value, axis, [(i, (i - 1) % size) for i in range(size)])]
    unnamed x275 -> x267, local copies, waits for them, and re-layouts: 16.3 us -> 15.3 us
  transfers between devices with their start and end apart: 67 -> 68, of which waited for: 35 -> 33; matrix products, arithmetic and copies ran while one was open for 43% -> 44% of each run, Pallas kernels for 5% -> 5%
where the time goes in v5:
time: 613 us; the launch traced here: 605 us
  matrix products  169 us (28%)
  waiting for transfers between devices  149 us (24%)
  other arithmetic  93.8 us (15%)
  starting transfers between devices  91.8 us (15%)
  local copies, waits for them, and re-layouts  49.6 us (8%)
  Pallas kernels  28.5 us (5%)
  between operations  22.9 us (4%)
    ppermute x42, waiting for transfers between devices, wide_from(): return lax.ppermute(value, 'w', pairs)  104 us
    ppermute x42, starting transfers between devices, wide_from(): return lax.ppermute(value, 'w', pairs)  75.4 us
    dot_general x20, matrix products, contract_cols(): lax.dot_general(left, right, (((1,), (1,)), ((), ())), preferred_element_...  68.9 us
    dot_general x10, matrix products, contract_rows(): lax.dot_general(left, right, (((0,), (0,)), ((), ())), preferred_element_...  41.6 us
    ppermute x7, waiting for transfers between devices, hop(): return lax.ppermute(value, axis, [(i, (i - 1) % size) for i in range(size)])  37.2 us
    dot_general x8, matrix products, hidden_part(): both = jnp.dot(mixed_parts[k], expand_all[j], preferred_element_type=wide)  32.1 us
    pallas_call x1, Pallas kernels, attend_back(): pl.pallas_call(functools.partial(attend_back_kernel, heads, groups, lengt...  18.6 us
    convert_element_type x5, other arithmetic, body(): made = [updated, first_new, second_new, updated.astype(low)]  17.7 us
  transfers between devices with their start and end apart: 68, of which 33 were waited for; matrix products, arithmetic and copies ran while one was open for 44% of the time, Pallas kernels for 5%

profile of v5, /device:TPU:0, one launch (start us, length us, event | category | flops | bytes accessed | tf_op | source)
XLA Modules:
  0.0 604.7 jit_solution(12337745033904422791)
XLA Ops:
  13.1 3.0 collective-permute-start.1
  16.1 3.6 collective-permute-start
  26.6 2.8 collective-permute-done.1
  34.4 4.4 collective-permute-start.2
  40.2 7.8 %collective-permute-done.3 = bf16[256,1152]{1,0:T(8,128)(2,1)S(1)} collective-permute-done((bf16[256,1152]{1,0:T(8,128)(2,1)}, bf16[256,1152]{1,0:T(8,128)(2,1)S(1)}, u32[]{:S(2)}, u32[]{:S(2)}) %collective-permute-start.3) | collective-permute-done | bytes 589856 | tf_op jit(solution)/shard_map/ppermute | solution.py:409
  51.8 4.2 collective-permute-start.4
  62.9 3.9 collective-permute-done.4
  69.7 4.8 collective-permute-start.8
  76.2 3.9 collective-permute-done.6
  81.9 10.3 %fusion.159.raw.raw_all = f32[1024,1152]{1,0:T(8,128)} fusion(bf16[1024,2048]{1,0:T(8,128)(2,1)} %all-gather.6.cloned.1.call-done, bf16[2048,1152]{1,0:T(8,128)(2,1)} %constant_dynamic-update-slice_fusion.8), kind=kOutput, calls=%fused_computation.341 | convolution fusion | flops 4831838208 | bytes 13631488 | tf_op jit(solution)/shard_map/dot_general | solution.py:605
  92.2 4.3 collective-permute-start.14
  100.9 9.9 %shard_map.481 = (bf16[1024,512]{1,0:T(8,128)(2,1)}, bf16[1024,256]{1,0:T(8,128)(2,1)}, bf16[1024,256]{1,0:T(8,128)(2,1)}, f32[1024,512]{1,0:T(8,128)}, f32[1024...) custom-call(s32[4]{0:T(128)} %pad_add_fusion.slots, f32[1024,1152]{1,0:T(8,128)} %fusion.159.raw.raw_all, ...), custom_call_target="tpu_custom_call" | custom-call | flops 2147483648 | bytes 9961472 | tf_op jit(solution)/shard_map/pallas_call | solution.py:183
  110.8 5.0 collective-permute-done.14
  123.9 2.9 collective-permute-done.15
  130.9 12.1 %collective-permute-done.16 = bf16[128,2048]{1,0:T(8,128)(2,1)S(1)} collective-permute-done((bf16[128,2048]{1,0:T(8,128)(2,1)S(1)}, bf16[128,2048]{1,0:T(8,128)(2,1)S(1)}, u32[]{:S(2)}, u32[]{:S(2)}) %collective-permute-start.16) | collective-permute-done | bytes 524320 | tf_op jit(solution)/shard_map/ppermute | solution.py:379
  143.0 10.4 %collective-permute-done.19 = bf16[128,2048]{1,0:T(8,128)(2,1)S(1)} collective-permute-done((bf16[128,2048]{1,0:T(8,128)(2,1)S(1)}, bf16[128,2048]{1,0:T(8,128)(2,1)S(1)}, u32[]{:S(2)}, u32[]{:S(2)}) %collective-permute-start.19) | collective-permute-done | bytes 524320 | tf_op jit(solution)/shard_map/ppermute | solution.py:379
  155.2 4.2 collective-permute-done.18
  166.5 6.8 %fusion.160 = f32[256,1536]{1,0:T(8,128)} fusion(bf16[256,2048]{1,0:T(8,128)(2,1)S(1)} %multiply_convert_fusion, bf16[2048,1536]{1,0:T(8,128)(2,1)} %all-gather.8.cloned.1.call-done), kind=kOutput, calls=%fused_computation.342 | convolution fusion | flops 1610612736 | bytes 8912896 | tf_op jit(solution)/shard_map/dot_general | solution.py:641
  173.3 4.9 multiply_convert_fusion.23
  179.1 3.1 fusion.140
  182.2 8.1 %collective-permute-done.20 = bf16[256,2048]{1,0:T(8,128)(2,1)} collective-permute-done((bf16[256,2048]{1,0:T(8,128)(2,1)S(1)}, bf16[256,2048]{1,0:T(8,128)(2,1)}, u32[]{:S(2)}, u32[]{:S(2)}) %collective-permute-start.20) | collective-permute-done | bytes 1048608 | tf_op jit(solution)/shard_map/ppermute | solution.py:409
  190.3 19.9 %collective-permute-done.22 = bf16[256,2048]{1,0:T(8,128)(2,1)} collective-permute-done((bf16[256,2048]{1,0:T(8,128)(2,1)}, bf16[256,2048]{1,0:T(8,128)(2,1)}, u32[]{:S(2)}, u32[]{:S(2)}) %collective-permute-start.22) | collective-permute-done | bytes 1048608 | tf_op jit(solution)/shard_map/ppermute | solution.py:409
  212.8 5.0 fusion.161
  217.9 2.8 multiply_convert_fusion.20
  221.7 3.7 pad_maximum_fusion
  225.4 3.1 fusion.139
  228.6 4.7 collective-permute-done.23
  233.2 4.7 collective-permute-start.24
  238.0 3.0 fusion.163
  241.0 3.3 multiply_convert_fusion.14
  245.2 3.1 fusion.137
  248.4 6.1 %fusion.162 = f32[256,1536]{1,0:T(8,128)} fusion(bf16[256,2048]{1,0:T(8,128)(2,1)} %collective-permute-done.20, bf16[2048,1536]{1,0:T(8,128)(2,1)} %all-gather.12.cloned.1.call-done), kind=kOutput, calls=%fused_computation.344 | convolution fusion | flops 1610612736 | bytes 8912896 | tf_op jit(solution)/shard_map/dot_general | solution.py:641
  254.4 4.8 multiply_convert_fusion.17
  262.6 3.2 fusion.164
  265.8 3.5 multiply_convert_fusion.11
  272.1 3.2 fusion.165
  275.3 3.4 multiply_convert_fusion.8
  288.5 3.3 multiply_convert_fusion.5
  295.2 3.0 fusion.167
  298.2 3.3 multiply_convert_fusion.2
  312.9 9.1 %convolution_convert_fusion = bf16[2048,1536]{1,0:T(8,128)(2,1)} fusion(bf16[1024,2048]{1,0:T(8,128)(2,1)S(1)} %pad_maximum_fusion.1, bf16[256,1536]{1,0:T(8,128)(2,1)S(1)} %pad_maximum_fusion.12, bf16[256,1536]{1,0:T(8,128)(2,1)S(1)} %copy-done.74, bf16[256,1536]{1,0:T(8,128)(2,1)S(1)} %copy-done.73, bf16[256,1536]{1,0:T(8,128)(2,1)S(1)} %copy-done.72), kind=kOutput, calls=%fused_computation | convolution fusion | flops 6458179584 | bytes 13631488 | tf_op jit(solution)/shard_map/dot_general | solution.py:50
  322.0 3.1 fusion.168
  329.2 3.5 convolution_convert_fusion.1
  346.7 14.7 %collective-permute-done.28 = bf16[256,2048]{1,0:T(8,128)(2,1)S(1)} collective-permute-done((bf16[256,2048]{1,0:T(8,128)(2,1)S(1)}, bf16[256,2048]{1,0:T(8,128)(2,1)S(1)}, u32[]{:S(2)}, u32[]{:S(2)}) %collective-permute-start.28) | collective-permute-done | bytes 1048608 | tf_op jit(solution)/shard_map/ppermute | solution.py:379
  372.2 3.7 fusion.171.gated_grad
  375.9 18.6 %shard_map.482 = (bf16[1024,1152]{1,0:T(8,128)(2,1)}, bf16[1024,1152]{1,0:T(8,128)(2,1)}, f32[2,128]{1,0:T(2,128)}) custom-call(s32[4]{0:T(128)} %pad_add_fusion.slots, f32[1024,512]{1,0:T(8,128)} %fusion.171.gated_grad, f32[1024,1152]{1,0:T(8,128)} %fusion.159.raw.raw_all, s32[1,1024]{1,0:T(1,128)} %subtract_subtract_fusion.1.start, ...), custom_call_target="tpu_custom_call" | custom-call | flops 5368709120 | bytes 13369344 | tf_op jit(solution)/shard_map/pallas_call | solution.py:325
  396.1 8.4 %fusion.172 = f32[2048,1152]{1,0:T(8,128)S(1)} fusion(bf16[1024,2048]{1,0:T(8,128)(2,1)} %all-gather.6.cloned.1.call-done, bf16[1024,1152]{1,0:T(8,128)(2,1)} %get-tuple-element.507), kind=kOutput, calls=%fused_computation.354 | convolution fusion | flops 4831838208 | bytes 15990784 | tf_op jit(solution)/shard_map/dot_general | solution.py:50
  406.2 4.7 add.611
  413.3 3.0 add_convert_fusion.3
  420.9 6.6 %convolution_convert_fusion.3 = bf16[512,2048]{1,0:T(8,128)(2,1)} fusion(bf16[2048,1152]{1,0:T(8,128)(2,1)} %constant_dynamic-update-slice_fusion.8, bf16[1024,1152]{1,0:T(8,128)(2,1)S(1)} %copy-done.127), kind=kOutput, calls=%fused_computation.55 | convolution fusion | flops 2416967680 | bytes 7995392 | tf_op jit(solution)/shard_map/dot_general | solution.py:56
  427.6 3.9 fusion.33
  436.9 4.2 collective-permute-start.39
  446.8 5.1 convolution_convert_fusion.2
  456.0 4.1 collective-permute-start.42
  460.1 5.2 fusion.38
  465.3 5.5 convolution_add_fusion.7
  475.0 4.3 collective-permute-start.45
  492.4 9.2 %collective-permute-done.47 = bf16[512,512]{1,0:T(8,128)(2,1)S(1)} collective-permute-done((bf16[512,512]{1,0:T(8,128)(2,1)S(1)}, bf16[512,512]{1,0:T(8,128)(2,1)S(1)}, u32[]{:S(2)}, u32[]{:S(2)}) %collective-permute-start.47) | collective-permute-done | bytes 524320 | tf_op jit(solution)/shard_map/ppermute | solution.py:409
  508.0 3.7 collective-permute-start.49
  518.3 3.9 collective-permute-done.50
  523.6 9.6 %collective-permute-done.51 = bf16[512,512]{1,0:T(8,128)(2,1)S(1)} collective-permute-done((bf16[512,512]{1,0:T(8,128)(2,1)S(1)}, bf16[512,512]{1,0:T(8,128)(2,1)S(1)}, u32[]{:S(2)}, u32[]{:S(2)}) %collective-permute-start.51) | collective-permute-done | bytes 524320 | tf_op jit(solution)/shard_map/ppermute | solution.py:409
  557.3 3.0 fusion.174
  583.0 7.4 %fusion.143 = (bf16[2,512,768]{2,1,0:T(8,128)(2,1)}, f32[2,512,768]{2,1,0:T(8,128)}, f32[2,512,768]{2,1,0:T(8,128)}, f32[2,512,768]{2,1,0:T(8,128)}) fusion(f32[2,512,768]{2,1,0:T(8,128)S(1)} %copy-done.17, f32[]{:T(128)S(6)} %div.205, f32[1,512,768]{2,1,0:T(8,128)S(1)} %copy-done.15, f32[1,512,768]{2,1,0:T(8,128)S(1)} %copy-done.13, ...), kind=kLoop, calls=%fused_computation.331 | loop fusion | flops 14155776 | bytes 23592964 | tf_op jit(solution)/shard_map/convert_element_type | solution.py:918
  593.2 3.4 fusion.141
  (531 shorter events, 226.1 us)
Async XLA Ops:
  7.2 74.7 %all-gather.6.cloned.1.call-start = ((), (), s32[]{:S(2)}) async-start(), calls=%async_computation.2 | async-start | bytes 5242880 | tf_op jit(solution)/shard_map/all_gather | solution.py:565
  13.0 153.5 %all-gather.8.cloned.1.call-start = ((), (), s32[]{:S(2)}) async-start(), calls=%async_computation.3 | async-start | bytes 7864320 | tf_op jit(solution)/shard_map/all_gather | solution.py:571
  13.1 16.4 %collective-permute-start.1 = (bf16[256,1152]{1,0:T(8,128)(2,1)S(1)}, bf16[256,1152]{1,0:T(8,128)(2,1)S(1)}, u32[]{:S(2)}, u32[]{:S(2)}) collective-permute-start(bf16[256,1152]{1,0:T(8,128)(2,1)S(1)} %concatenate.109), channel_id=1, source_target_pairs={{1,0},{0,1},{3,2},{2,3},{5,4},{4,5},{7,6},{6,7},{9,8},{8,9},{11,10... | collective-permute-start | bytes 1769480 | tf_op jit(solution)/shard_map/ppermute | solution.py:409
  16.1 15.9 %collective-permute-start = (bf16[256,1152]{1,0:T(8,128)(2,1)S(1)}, bf16[256,1152]{1,0:T(8,128)(2,1)}, u32[]{:S(2)}, u32[]{:S(2)}) collective-permute-start(bf16[256,1152]{1,0:T(8,128)(2,1)S(1)} %concatenate.109), channel_id=1, source_target_pairs={{2,0},{3,1},{4,2},{5,3},{6,4},{7,5},{0,6},{1,7},{10,8},{11,9},{12,... | collective-permute-start | bytes 1769480 | tf_op jit(solution)/shard_map/ppermute | solution.py:409
  33.6 139.7 %all-gather.10.cloned.1.call-start = ((), (), s32[]{:S(2)}) async-start(), calls=%async_computation.4 | async-start | bytes 3932160 | tf_op jit(solution)/shard_map/all_gather | solution.py:574
  33.9 14.2 %collective-permute-start.3 = (bf16[256,1152]{1,0:T(8,128)(2,1)}, bf16[256,1152]{1,0:T(8,128)(2,1)S(1)}, u32[]{:S(2)}, u32[]{:S(2)}) collective-permute-start(bf16[256,1152]{1,0:T(8,128)(2,1)} %collective-permute-done), channel_id=1, source_target_pairs={{1,0},{0,1},{3,2},{2,3},{5,4},{4,5},{7,6},{6,7},{9,8},{8,9},{11,10... | collective-permute-start | bytes 1769480 | tf_op jit(solution)/shard_map/ppermute | solution.py:409
  34.4 15.8 %collective-permute-start.2 = (bf16[256,1152]{1,0:T(8,128)(2,1)}, bf16[256,1152]{1,0:T(8,128)(2,1)S(1)}, u32[]{:S(2)}, u32[]{:S(2)}) collective-permute-start(bf16[256,1152]{1,0:T(8,128)(2,1)} %collective-permute-done), channel_id=1, source_target_pairs={{2,0},{3,1},{4,2},{5,3},{6,4},{7,5},{0,6},{1,7},{10,8},{11,9},{12,... | collective-permute-start | bytes 1769480 | tf_op jit(solution)/shard_map/ppermute | solution.py:409
  50.2 12.7 %collective-permute-start.5 = (bf16[256,1152]{1,0:T(8,128)(2,1)S(1)}, bf16[256,1152]{1,0:T(8,128)(2,1)S(1)}, u32[]{:S(2)}, u32[]{:S(2)}) collective-permute-start(bf16[256,1152]{1,0:T(8,128)(2,1)S(1)} %collective-permute-done.2), channel_id=1, source_target_pairs={{1,0},{0,1},{3,2},{2,3},{5,4},{4,5},{7,6},{6,7},{9,8},{8,9},{11,10... | collective-permute-start | bytes 1769480 | tf_op jit(solution)/shard_map/ppermute | solution.py:409
  51.8 15.0 %collective-permute-start.4 = (bf16[256,1152]{1,0:T(8,128)(2,1)S(1)}, bf16[256,1152]{1,0:T(8,128)(2,1)S(1)}, u32[]{:S(2)}, u32[]{:S(2)}) collective-permute-start(bf16[256,1152]{1,0:T(8,128)(2,1)S(1)} %collective-permute-done.2), channel_id=1, source_target_pairs={{2,0},{3,1},{4,2},{5,3},{6,4},{7,5},{0,6},{1,7},{10,8},{11,9},{12,... | collective-permute-start | bytes 1769480 | tf_op jit(solution)/shard_map/ppermute | solution.py:409
  66.8 13.4 %collective-permute-start.6 = (bf16[256,1152]{1,0:T(8,128)(2,1)S(1)}, bf16[256,1152]{1,0:T(8,128)(2,1)S(1)}, u32[]{:S(2)}, u32[]{:S(2)}) collective-permute-start(bf16[256,1152]{1,0:T(8,128)(2,1)S(1)} %collective-permute-done.4), channel_id=1, source_target_pairs={{1,0},{0,1},{3,2},{2,3},{5,4},{4,5},{7,6},{6,7},{9,8},{8,9},{11,10... | collective-permute-start | bytes 1769480 | tf_op jit(solution)/shard_map/ppermute | solution.py:409
  68.2 24.0 %collective-permute-start.10 = (bf16[512,256]{1,0:T(8,128)(2,1)S(1)}, bf16[512,256]{1,0:T(8,128)(2,1)}, u32[]{:S(2)}, u32[]{:S(2)}) collective-permute-start(bf16[512,256]{1,0:T(8,128)(2,1)S(1)} %convert_element_type.310), channel_id=1, source_target_pairs={{1,0},{0,1},{3,2},{2,3},{5,4},{4,5},{7,6},{6,7},{9,8},{8,9},{11,10... | collective-permute-start | bytes 786440 | tf_op jit(solution)/shard_map/ppermute | solution.py:409
  69.7 22.5 %collective-permute-start.9 = (bf16[512,256]{1,0:T(8,128)(2,1)S(1)}, bf16[512,256]{1,0:T(8,128)(2,1)S(1)}, u32[]{:S(2)}, u32[]{:S(2)}) collective-permute-start(bf16[512,256]{1,0:T(8,128)(2,1)S(1)} %convert_element_type.310), channel_id=1, source_target_pairs={{6,0},{7,1},{0,2},{1,3},{2,4},{3,5},{4,6},{5,7},{14,8},{15,9},{8,1... | collective-permute-start | bytes 786440 | tf_op jit(solution)/shard_map/ppermute | solution.py:409
  69.7 22.5 %collective-permute-start.8 = (bf16[512,256]{1,0:T(8,128)(2,1)S(1)}, bf16[512,256]{1,0:T(8,128)(2,1)S(1)}, u32[]{:S(2)}, u32[]{:S(2)}) collective-permute-start(bf16[512,256]{1,0:T(8,128)(2,1)S(1)} %convert_element_type.310), channel_id=1, source_target_pairs={{4,0},{5,1},{6,2},{7,3},{0,4},{1,5},{2,6},{3,7},{12,8},{13,9},{14,... | collective-permute-start | bytes 786440 | tf_op jit(solution)/shard_map/ppermute | solution.py:409
  74.5 17.7 %collective-permute-start.7 = (bf16[512,256]{1,0:T(8,128)(2,1)S(1)}, bf16[512,256]{1,0:T(8,128)(2,1)}, u32[]{:S(2)}, u32[]{:S(2)}) collective-permute-start(bf16[512,256]{1,0:T(8,128)(2,1)S(1)} %convert_element_type.310), channel_id=1, source_target_pairs={{2,0},{3,1},{4,2},{5,3},{6,4},{7,5},{0,6},{1,7},{10,8},{11,9},{12,... | collective-permute-start | bytes 786440 | tf_op jit(solution)/shard_map/ppermute | solution.py:409
  92.2 23.6 %collective-permute-start.14 = (bf16[256,2048]{1,0:T(8,128)(2,1)}, bf16[256,2048]{1,0:T(8,128)(2,1)}, u32[]{:S(2)}, u32[]{:S(2)}) collective-permute-start(bf16[256,2048]{1,0:T(8,128)(2,1)} %fusion.59), channel_id=1, source_target_pairs={{2,0},{3,1},{4,2},{5,3},{6,4},{7,5},{0,6},{1,7},{10,8},{11,9},{12,... | collective-permute-start | bytes 3145736 | tf_op jit(solution)/shard_map/ppermute | solution.py:409
  96.5 14.3 %collective-permute-start.11 = (bf16[512,256]{1,0:T(8,128)(2,1)}, bf16[512,256]{1,0:T(8,128)(2,1)}, u32[]{:S(2)}, u32[]{:S(2)}) collective-permute-start(bf16[512,256]{1,0:T(8,128)(2,1)} %collective-permute-done.7), channel_id=1, source_target_pairs={{1,0},{0,1},{3,2},{2,3},{5,4},{4,5},{7,6},{6,7},{9,8},{8,9},{11,10... | collective-permute-start | bytes 786440 | tf_op jit(solution)/shard_map/ppermute | solution.py:409
  97.0 13.8 %collective-permute-start.12 = (bf16[512,256]{1,0:T(8,128)(2,1)S(1)}, bf16[512,256]{1,0:T(8,128)(2,1)}, u32[]{:S(2)}, u32[]{:S(2)}) collective-permute-start(bf16[512,256]{1,0:T(8,128)(2,1)S(1)} %collective-permute-done.8), channel_id=1, source_target_pairs={{1,0},{0,1},{3,2},{2,3},{5,4},{4,5},{7,6},{6,7},{9,8},{8,9},{11,10... | collective-permute-start | bytes 786440 | tf_op jit(solution)/shard_map/ppermute | solution.py:409
  98.6 12.3 %collective-permute-start.13 = (bf16[512,256]{1,0:T(8,128)(2,1)S(1)}, bf16[512,256]{1,0:T(8,128)(2,1)}, u32[]{:S(2)}, u32[]{:S(2)}) collective-permute-start(bf16[512,256]{1,0:T(8,128)(2,1)S(1)} %collective-permute-done.9), channel_id=1, source_target_pairs={{1,0},{0,1},{3,2},{2,3},{5,4},{4,5},{7,6},{6,7},{9,8},{8,9},{11,10... | collective-permute-start | bytes 786440 | tf_op jit(solution)/shard_map/ppermute | solution.py:409
  100.7 147.7 %all-gather.12.cloned.1.call-start = ((), (), s32[]{:S(2)}) async-start(), calls=%async_computation.5 | async-start | bytes 7864320 | tf_op jit(solution)/shard_map/all_gather | solution.py:571
  123.5 36.0 %collective-permute-start.18 = (bf16[512,1536]{1,0:T(8,128)(2,1)S(1)}, bf16[512,1536]{1,0:T(8,128)(2,1)S(1)}, u32[]{:S(2)}, u32[]{:S(2)}) collective-permute-start(bf16[512,1536]{1,0:T(8,128)(2,1)S(1)} %copy-done.26), channel_id=1, source_target_pairs={{1,0},{0,1},{3,2},{2,3},{5,4},{4,5},{7,6},{6,7},{9,8},{8,9},{11,10... | collective-permute-start | bytes 4718600 | tf_op jit(solution)/shard_map/ppermute | solution.py:409
  128.1 14.8 %collective-permute-start.16 = (bf16[128,2048]{1,0:T(8,128)(2,1)S(1)}, bf16[128,2048]{1,0:T(8,128)(2,1)S(1)}, u32[]{:S(2)}, u32[]{:S(2)}) collective-permute-start(bf16[128,2048]{1,0:T(8,128)(2,1)S(1)} %get-tuple-element.665), channel_id=1, source_target_pairs={{0,16},{16,0},{1,17},{17,1},{2,18},{18,2},{3,19},{19,3},{4,20},{20... | collective-permute-start | bytes 1572872 | tf_op jit(solution)/shard_map/ppermute | solution.py:379
  129.8 23.6 %collective-permute-start.19 = (bf16[128,2048]{1,0:T(8,128)(2,1)S(1)}, bf16[128,2048]{1,0:T(8,128)(2,1)S(1)}, u32[]{:S(2)}, u32[]{:S(2)}) collective-permute-start(bf16[128,2048]{1,0:T(8,128)(2,1)S(1)} %get-tuple-element.666), channel_id=1, source_target_pairs={{0,16},{16,0},{1,17},{17,1},{2,18},{18,2},{3,19},{19,3},{4,20},{20... | collective-permute-start | bytes 1572872 | tf_op jit(solution)/shard_map/ppermute | solution.py:379
  130.2 25.0 %collective-permute-start.17 = (bf16[256,2048]{1,0:T(8,128)(2,1)}, bf16[256,2048]{1,0:T(8,128)(2,1)}, u32[]{:S(2)}, u32[]{:S(2)}) collective-permute-start(bf16[256,2048]{1,0:T(8,128)(2,1)} %collective-permute-done.14), channel_id=1, source_target_pairs={{2,0},{3,1},{4,2},{5,3},{6,4},{7,5},{0,6},{1,7},{10,8},{11,9},{12,... | collective-permute-start | bytes 3145736 | tf_op jit(solution)/shard_map/ppermute | solution.py:409
  160.6 93.9 %all-gather.14.cloned.1.call-start = ((), (), s32[]{:S(2)}) async-start(), calls=%async_computation.6 | async-start | bytes 3932160 | tf_op jit(solution)/shard_map/all_gather | solution.py:574
  160.7 21.6 %collective-permute-start.21 = (bf16[768,512]{1,0:T(8,128)(2,1)}, bf16[768,512]{1,0:T(8,128)(2,1)}, u32[]{:S(2)}, u32[]{:S(2)}) collective-permute-start(bf16[768,512]{1,0:T(8,128)(2,1)} %convert_element_type.315), channel_id=1, source_target_pairs={{1,0},{0,1},{3,2},{2,3},{5,4},{4,5},{7,6},{6,7},{9,8},{8,9},{11,10... | collective-permute-start | bytes 2359304 | tf_op jit(solution)/shard_map/ppermute | solution.py:409
  164.1 26.3 %collective-permute-start.20 = (bf16[256,2048]{1,0:T(8,128)(2,1)S(1)}, bf16[256,2048]{1,0:T(8,128)(2,1)}, u32[]{:S(2)}, u32[]{:S(2)}) collective-permute-start(bf16[256,2048]{1,0:T(8,128)(2,1)S(1)} %multiply_convert_fusion), channel_id=1, source_target_pairs={{2,0},{3,1},{4,2},{5,3},{6,4},{7,5},{0,6},{1,7},{10,8},{11,9},{12,... | collective-permute-start | bytes 3145736 | tf_op jit(solution)/shard_map/ppermute | solution.py:409
  164.8 45.5 %collective-permute-start.22 = (bf16[256,2048]{1,0:T(8,128)(2,1)}, bf16[256,2048]{1,0:T(8,128)(2,1)}, u32[]{:S(2)}, u32[]{:S(2)}) collective-permute-start(bf16[256,2048]{1,0:T(8,128)(2,1)} %collective-permute-done.17), channel_id=1, source_target_pairs={{2,0},{3,1},{4,2},{5,3},{6,4},{7,5},{0,6},{1,7},{10,8},{11,9},{12,... | collective-permute-start | bytes 3145736 | tf_op jit(solution)/shard_map/ppermute | solution.py:409
  210.3 23.0 %collective-permute-start.23 = (bf16[256,2048]{1,0:T(8,128)(2,1)}, bf16[256,2048]{1,0:T(8,128)(2,1)}, u32[]{:S(2)}, u32[]{:S(2)}) collective-permute-start(bf16[256,2048]{1,0:T(8,128)(2,1)} %collective-permute-done.20), channel_id=1, source_target_pairs={{2,0},{3,1},{4,2},{5,3},{6,4},{7,5},{0,6},{1,7},{10,8},{11,9},{12,... | collective-permute-start | bytes 3145736 | tf_op jit(solution)/shard_map/ppermute | solution.py:409
  212.8 291.6 %reduce-scatter.3.cloned.1.call-start = ((), (), s32[]{:S(2)}) async-start(), calls=%async_computation.7 | async-start | bytes 7864320 | tf_op jit(solution)/shard_map/reduce_scatter | solution.py:785
  233.2 29.2 %collective-permute-start.24 = (bf16[256,2048]{1,0:T(8,128)(2,1)}, bf16[256,2048]{1,0:T(8,128)(2,1)}, u32[]{:S(2)}, u32[]{:S(2)}) collective-permute-start(bf16[256,2048]{1,0:T(8,128)(2,1)} %collective-permute-done.23), channel_id=1, source_target_pairs={{2,0},{3,1},{4,2},{5,3},{6,4},{7,5},{0,6},{1,7},{10,8},{11,9},{12,... | collective-permute-start | bytes 3145736 | tf_op jit(solution)/shard_map/ppermute | solution.py:409
  262.4 22.9 %collective-permute-start.25 = (bf16[256,2048]{1,0:T(8,128)(2,1)S(1)}, bf16[256,2048]{1,0:T(8,128)(2,1)S(1)}, u32[]{:S(2)}, u32[]{:S(2)}) collective-permute-start(bf16[256,2048]{1,0:T(8,128)(2,1)S(1)} %add.577), channel_id=1, source_target_pairs={{2,0},{3,1},{4,2},{5,3},{6,4},{7,5},{0,6},{1,7},{10,8},{11,9},{12,... | collective-permute-start | bytes 3145736 | tf_op jit(solution)/shard_map/ppermute | solution.py:409
  285.6 21.9 %collective-permute-start.26 = (bf16[256,2048]{1,0:T(8,128)(2,1)S(1)}, bf16[256,2048]{1,0:T(8,128)(2,1)S(1)}, u32[]{:S(2)}, u32[]{:S(2)}) collective-permute-start(bf16[256,2048]{1,0:T(8,128)(2,1)S(1)} %add_convert_fusion.1), channel_id=1, source_target_pairs={{2,0},{3,1},{4,2},{5,3},{6,4},{7,5},{0,6},{1,7},{10,8},{11,9},{12,... | collective-permute-start | bytes 3145736 | tf_op jit(solution)/shard_map/ppermute | solution.py:409
  308.8 24.0 %collective-permute-start.27 = (bf16[256,2048]{1,0:T(8,128)(2,1)}, bf16[256,2048]{1,0:T(8,128)(2,1)S(1)}, u32[]{:S(2)}, u32[]{:S(2)}) collective-permute-start(bf16[256,2048]{1,0:T(8,128)(2,1)} %add_convert_fusion), channel_id=1, source_target_pairs={{2,0},{3,1},{4,2},{5,3},{6,4},{7,5},{0,6},{1,7},{10,8},{11,9},{12,... | collective-permute-start | bytes 3145736 | tf_op jit(solution)/shard_map/ppermute | solution.py:409
  332.8 11.7 %collective-permute-start.30 = (bf16[1024,1536]{1,0:T(8,128)(2,1)S(1)}, bf16[1024,1536]{1,0:T(8,128)(2,1)S(1)}, u32[]{:S(2)}, u32[]{:S(2)}) collective-permute-start(bf16[1024,1536]{1,0:T(8,128)(2,1)S(1)} %convolution_convert_fusion.1), channel_id=1, source_target_pairs={{0,8},{8,0},{1,9},{9,1},{2,10},{10,2},{3,11},{11,3},{4,12},{12,4},... | collective-permute-start | bytes 9437192 | tf_op jit(solution)/shard_map/ppermute | solution.py:374
  336.1 25.3 %collective-permute-start.28 = (bf16[256,2048]{1,0:T(8,128)(2,1)S(1)}, bf16[256,2048]{1,0:T(8,128)(2,1)S(1)}, u32[]{:S(2)}, u32[]{:S(2)}) collective-permute-start(bf16[256,2048]{1,0:T(8,128)(2,1)S(1)} %get-tuple-element.466), channel_id=1, source_target_pairs={{0,16},{16,0},{1,17},{17,1},{2,18},{18,2},{3,19},{19,3},{4,20},{20... | collective-permute-start | bytes 3145736 | tf_op jit(solution)/shard_map/ppermute | solution.py:379
  337.6 25.4 %collective-permute-start.29 = (bf16[256,2048]{1,0:T(8,128)(2,1)S(1)}, bf16[256,2048]{1,0:T(8,128)(2,1)S(1)}, u32[]{:S(2)}, u32[]{:S(2)}) collective-permute-start(bf16[256,2048]{1,0:T(8,128)(2,1)S(1)} %fusion.39), channel_id=1, source_target_pairs={{2,0},{3,1},{4,2},{5,3},{6,4},{7,5},{0,6},{1,7},{10,8},{11,9},{12,... | collective-permute-start | bytes 3145736 | tf_op jit(solution)/shard_map/ppermute | solution.py:409
  363.1 7.2 %collective-permute-start.33 = (bf16[768,1024]{1,0:T(8,128)(2,1)S(1)}, bf16[768,1024]{1,0:T(8,128)(2,1)}, u32[]{:S(2)}, u32[]{:S(2)}) collective-permute-start(bf16[768,1024]{1,0:T(8,128)(2,1)S(1)} %fusion.60), channel_id=1, source_target_pairs={{0,8},{8,0},{1,9},{9,1},{2,10},{10,2},{3,11},{11,3},{4,12},{12,4},... | collective-permute-start | bytes 4718600 | tf_op jit(solution)/shard_map/ppermute | solution.py:374
  363.1 4.5 collective-permute-start.31
  363.6 5.9 collective-permute-start.32
  364.0 30.6 %collective-permute-start.34 = (bf16[256,2048]{1,0:T(8,128)(2,1)S(1)}, bf16[256,2048]{1,0:T(8,128)(2,1)}, u32[]{:S(2)}, u32[]{:S(2)}) collective-permute-start(bf16[256,2048]{1,0:T(8,128)(2,1)S(1)} %add.606), channel_id=1, source_target_pairs={{2,0},{3,1},{4,2},{5,3},{6,4},{7,5},{0,6},{1,7},{10,8},{11,9},{12,... | collective-permute-start | bytes 3145736 | tf_op jit(solution)/shard_map/ppermute | solution.py:409
  367.1 27.4 %collective-permute-start.35 = (bf16[512,768]{1,0:T(8,128)(2,1)S(1)}, bf16[512,768]{1,0:T(8,128)(2,1)S(1)}, u32[]{:S(2)}, u32[]{:S(2)}) collective-permute-start(bf16[512,768]{1,0:T(8,128)(2,1)S(1)} %get-tuple-element.670), channel_id=1, source_target_pairs={{0,16},{16,0},{1,17},{17,1},{2,18},{18,2},{3,19},{19,3},{4,20},{20... | collective-permute-start | bytes 2359304 | tf_op jit(solution)/shard_map/ppermute | solution.py:379
  395.5 154.3 %reduce-scatter.5.cloned.1.call-start = ((), (), s32[]{:S(2)}) async-start(), calls=%async_computation.8 | async-start | bytes 3932160 | tf_op jit(solution)/shard_map/reduce_scatter | solution.py:841
  395.5 32.0 %collective-permute-start.37 = (bf16[512,768]{1,0:T(8,128)(2,1)}, bf16[512,768]{1,0:T(8,128)(2,1)S(1)}, u32[]{:S(2)}, u32[]{:S(2)}) collective-permute-start(bf16[512,768]{1,0:T(8,128)(2,1)} %get-tuple-element.669), channel_id=1, source_target_pairs={{0,16},{16,0},{1,17},{17,1},{2,18},{18,2},{3,19},{19,3},{4,20},{20... | collective-permute-start | bytes 2359304 | tf_op jit(solution)/shard_map/ppermute | solution.py:379
  404.6 28.9 %collective-permute-start.36 = (bf16[256,1152]{1,0:T(8,128)(2,1)S(1)}, bf16[256,1152]{1,0:T(8,128)(2,1)S(1)}, u32[]{:S(2)}, u32[]{:S(2)}) collective-permute-start(bf16[256,1152]{1,0:T(8,128)(2,1)S(1)} %dynamic-slice_convert_fusion.3), channel_id=1, source_target_pairs={{1,0},{0,1},{3,2},{2,3},{5,4},{4,5},{7,6},{6,7},{9,8},{8,9},{11,10... | collective-permute-start | bytes 1769480 | tf_op jit(solution)/shard_map/ppermute | solution.py:409
  410.9 24.9 %collective-permute-start.38 = (bf16[256,2048]{1,0:T(8,128)(2,1)S(1)}, bf16[256,2048]{1,0:T(8,128)(2,1)S(1)}, u32[]{:S(2)}, u32[]{:S(2)}) collective-permute-start(bf16[256,2048]{1,0:T(8,128)(2,1)S(1)} %add.611), channel_id=1, source_target_pairs={{2,0},{3,1},{4,2},{5,3},{6,4},{7,5},{0,6},{1,7},{10,8},{11,9},{12,... | collective-permute-start | bytes 3145736 | tf_op jit(solution)/shard_map/ppermute | solution.py:409
  435.9 20.1 %collective-permute-start.41 = (bf16[512,2048]{1,0:T(8,128)(2,1)}, bf16[512,2048]{1,0:T(8,128)(2,1)}, u32[]{:S(2)}, u32[]{:S(2)}) collective-permute-start(bf16[512,2048]{1,0:T(8,128)(2,1)} %convolution_convert_fusion.3), channel_id=1, source_target_pairs={{0,8},{8,0},{1,9},{9,1},{2,10},{10,2},{3,11},{11,3},{4,12},{12,4},... | collective-permute-start | bytes 6291464 | tf_op jit(solution)/shard_map/ppermute | solution.py:374
  436.9 16.5 %collective-permute-start.40 = (bf16[256,1152]{1,0:T(8,128)(2,1)}, bf16[256,1152]{1,0:T(8,128)(2,1)}, u32[]{:S(2)}, u32[]{:S(2)}) collective-permute-start(bf16[256,1152]{1,0:T(8,128)(2,1)} %dynamic-slice_convert_fusion.2), channel_id=1, source_target_pairs={{1,0},{0,1},{3,2},{2,3},{5,4},{4,5},{7,6},{6,7},{9,8},{8,9},{11,10... | collective-permute-start | bytes 1769480 | tf_op jit(solution)/shard_map/ppermute | solution.py:409
  436.9 33.9 %collective-permute-start.39 = (bf16[256,1152]{1,0:T(8,128)(2,1)}, bf16[256,1152]{1,0:T(8,128)(2,1)}, u32[]{:S(2)}, u32[]{:S(2)}) collective-permute-start(bf16[256,1152]{1,0:T(8,128)(2,1)} %convert_add_fusion.10), channel_id=1, source_target_pairs={{2,0},{3,1},{4,2},{5,3},{6,4},{7,5},{0,6},{1,7},{10,8},{11,9},{12,... | collective-permute-start | bytes 1769480 | tf_op jit(solution)/shard_map/ppermute | solution.py:409
  441.1 29.7 %collective-permute-start.43 = (bf16[256,1536]{1,0:T(8,128)(2,1)}, bf16[256,1536]{1,0:T(8,128)(2,1)S(1)}, u32[]{:S(2)}, u32[]{:S(2)}) collective-permute-start(bf16[256,1536]{1,0:T(8,128)(2,1)} %get-tuple-element.553), channel_id=1, source_target_pairs={{1,0},{0,1},{3,2},{2,3},{5,4},{4,5},{7,6},{6,7},{9,8},{8,9},{11,10... | collective-permute-start | bytes 2359304 | tf_op jit(solution)/shard_map/ppermute | solution.py:409
  443.1 27.8 %collective-permute-start.44 = (bf16[768,512]{1,0:T(8,128)(2,1)}, bf16[768,512]{1,0:T(8,128)(2,1)}, u32[]{:S(2)}, u32[]{:S(2)}) collective-permute-start(bf16[768,512]{1,0:T(8,128)(2,1)} %add_convert_fusion.3), channel_id=1, source_target_pairs={{0,16},{16,0},{1,17},{17,1},{2,18},{18,2},{3,19},{19,3},{4,20},{20... | collective-permute-start | bytes 2359304 | tf_op jit(solution)/shard_map/ppermute | solution.py:379
  456.0 14.9 %collective-permute-start.42 = (bf16[512,512]{1,0:T(8,128)(2,1)}, bf16[512,512]{1,0:T(8,128)(2,1)}, u32[]{:S(2)}, u32[]{:S(2)}) collective-permute-start(bf16[512,512]{1,0:T(8,128)(2,1)} %pad_maximum_fusion.6), channel_id=1, source_target_pairs={{2,0},{3,1},{4,2},{5,3},{6,4},{7,5},{0,6},{1,7},{10,8},{11,9},{12,... | collective-permute-start | bytes 1572872 | tf_op jit(solution)/shard_map/ppermute | solution.py:409
  473.3 16.6 %collective-permute-start.46 = (bf16[256,1152]{1,0:T(8,128)(2,1)}, bf16[256,1152]{1,0:T(8,128)(2,1)}, u32[]{:S(2)}, u32[]{:S(2)}) collective-permute-start(bf16[256,1152]{1,0:T(8,128)(2,1)} %dynamic-slice_convert_fusion.1), channel_id=1, source_target_pairs={{1,0},{0,1},{3,2},{2,3},{5,4},{4,5},{7,6},{6,7},{9,8},{8,9},{11,10... | collective-permute-start | bytes 1769480 | tf_op jit(solution)/shard_map/ppermute | solution.py:409
  475.0 26.7 %collective-permute-start.45 = (bf16[256,1152]{1,0:T(8,128)(2,1)S(1)}, bf16[256,1152]{1,0:T(8,128)(2,1)}, u32[]{:S(2)}, u32[]{:S(2)}) collective-permute-start(bf16[256,1152]{1,0:T(8,128)(2,1)S(1)} %add_convert_fusion.5), channel_id=1, source_target_pairs={{2,0},{3,1},{4,2},{5,3},{6,4},{7,5},{0,6},{1,7},{10,8},{11,9},{12,... | collective-permute-start | bytes 1769480 | tf_op jit(solution)/shard_map/ppermute | solution.py:409
  479.3 25.1 %collective-permute-start.48 = (bf16[256,1536]{1,0:T(8,128)(2,1)}, bf16[256,1536]{1,0:T(8,128)(2,1)}, u32[]{:S(2)}, u32[]{:S(2)}) collective-permute-start(bf16[256,1536]{1,0:T(8,128)(2,1)} %get-tuple-element.574), channel_id=1, source_target_pairs={{1,0},{0,1},{3,2},{2,3},{5,4},{4,5},{7,6},{6,7},{9,8},{8,9},{11,10... | collective-permute-start | bytes 2359304 | tf_op jit(solution)/shard_map/ppermute | solution.py:409
  483.3 18.3 %collective-permute-start.47 = (bf16[512,512]{1,0:T(8,128)(2,1)S(1)}, bf16[512,512]{1,0:T(8,128)(2,1)S(1)}, u32[]{:S(2)}, u32[]{:S(2)}) collective-permute-start(bf16[512,512]{1,0:T(8,128)(2,1)S(1)} %fusion.98), channel_id=1, source_target_pairs={{2,0},{3,1},{4,2},{5,3},{6,4},{7,5},{0,6},{1,7},{10,8},{11,9},{12,... | collective-permute-start | bytes 1572872 | tf_op jit(solution)/shard_map/ppermute | solution.py:409
  483.4 40.2 %collective-permute-start.53 = (bf16[256,2048]{1,0:T(8,128)(2,1)}, bf16[256,2048]{1,0:T(8,128)(2,1)S(1)}, u32[]{:S(2)}, u32[]{:S(2)}) collective-permute-start(bf16[256,2048]{1,0:T(8,128)(2,1)} %fusion.38), channel_id=1, source_target_pairs={{0,16},{16,0},{1,17},{17,1},{2,18},{18,2},{3,19},{19,3},{4,20},{20... | collective-permute-start | bytes 3145736 | tf_op jit(solution)/shard_map/ppermute | solution.py:379
  505.8 16.3 %collective-permute-start.50 = (bf16[256,1152]{1,0:T(8,128)(2,1)S(1)}, bf16[256,1152]{1,0:T(8,128)(2,1)S(1)}, u32[]{:S(2)}, u32[]{:S(2)}) collective-permute-start(bf16[256,1152]{1,0:T(8,128)(2,1)S(1)} %dynamic-slice_convert_fusion), channel_id=1, source_target_pairs={{1,0},{0,1},{3,2},{2,3},{5,4},{4,5},{7,6},{6,7},{9,8},{8,9},{11,10... | collective-permute-start | bytes 1769480 | tf_op jit(solution)/shard_map/ppermute | solution.py:409
  508.0 25.2 %collective-permute-start.49 = (bf16[256,1152]{1,0:T(8,128)(2,1)S(1)}, bf16[256,1152]{1,0:T(8,128)(2,1)S(1)}, u32[]{:S(2)}, u32[]{:S(2)}) collective-permute-start(bf16[256,1152]{1,0:T(8,128)(2,1)S(1)} %add_convert_fusion.4), channel_id=1, source_target_pairs={{2,0},{3,1},{4,2},{5,3},{6,4},{7,5},{0,6},{1,7},{10,8},{11,9},{12,... | collective-permute-start | bytes 1769480 | tf_op jit(solution)/shard_map/ppermute | solution.py:409
  511.8 23.9 %collective-permute-start.52 = (bf16[768,512]{1,0:T(8,128)(2,1)S(1)}, bf16[768,512]{1,0:T(8,128)(2,1)S(1)}, u32[]{:S(2)}, u32[]{:S(2)}) collective-permute-start(bf16[768,512]{1,0:T(8,128)(2,1)S(1)} %copy-done.75), channel_id=1, source_target_pairs={{1,0},{0,1},{3,2},{2,3},{5,4},{4,5},{7,6},{6,7},{9,8},{8,9},{11,10... | collective-permute-start | bytes 2359304 | tf_op jit(solution)/shard_map/ppermute | solution.py:409
  514.8 18.5 %collective-permute-start.51 = (bf16[512,512]{1,0:T(8,128)(2,1)S(1)}, bf16[512,512]{1,0:T(8,128)(2,1)S(1)}, u32[]{:S(2)}, u32[]{:S(2)}) collective-permute-start(bf16[512,512]{1,0:T(8,128)(2,1)S(1)} %fusion.99), channel_id=1, source_target_pairs={{2,0},{3,1},{4,2},{5,3},{6,4},{7,5},{0,6},{1,7},{10,8},{11,9},{12,... | collective-permute-start | bytes 1572872 | tf_op jit(solution)/shard_map/ppermute | solution.py:409
  541.1 11.0 %collective-permute-start.54 = (bf16[512,256]{1,0:T(8,128)(2,1)}, bf16[512,256]{1,0:T(8,128)(2,1)}, u32[]{:S(2)}, u32[]{:S(2)}) collective-permute-start(bf16[512,256]{1,0:T(8,128)(2,1)} %slice.393), channel_id=1, source_target_pairs={{1,0},{0,1},{3,2},{2,3},{5,4},{4,5},{7,6},{6,7},{9,8},{8,9},{11,10... | collective-permute-start | bytes 786440 | tf_op jit(solution)/shard_map/ppermute | solution.py:409
  556.0 4.4 collective-permute-start.55
  562.7 4.8 collective-permute-start.59
  569.1 4.7 collective-permute-start.60
  (137 other events, 807.3 us)
Sparse Core Ops, SparseCore 0:
  13.1 37.1 all-gather.5
  52.5 46.3 all-gather.7
  101.0 28.5 all-gather.9
  160.7 44.7 all-gather.11
  212.9 26.8 all-gather.13
  395.6 62.6 reduce-scatter.2
  473.5 50.9 reduce-scatter.4
